TPU v7x, 256 devices: a whole 4x4x8 slice. The times are simulated.
256 devices in a mesh: dp: 8 (over y, core), mp: 32 (over x, z).
Axes of the slice: x: 4, y: 4, z: 8, core: 2. Of those that a mesh axis runs over, the one named last changes fastest.
Arguments:
- acts_in: bfloat16 [65536, 4096], P(('dp', 'mp')), may hold values from -6 to 6
- grad_in: bfloat16 [65536, 8192], P('dp', 'mp'), may hold values from -0.0234375 to 0.0234375
- acts_out: bfloat16 [65536, 8192], P('dp', 'mp'), may hold values from -6 to 6
- grad_out: bfloat16 [65536, 4096], P(('dp', 'mp')), may hold values from -0.0234375 to 0.0234375
- basis_in: bfloat16 [4096, 256], P('mp'), may hold values from -0.09375 to 0.09375
- basis_out: bfloat16 [4096, 256], P('mp'), may hold values from -0.09375 to 0.09375
- first_in: float32 [256, 8192], P('dp', 'mp'), may hold values from -1.8 to 1.8
- second_in: float32 [256, 8192], P('dp', 'mp'), may hold values from 0.0001 to 0.01
- first_out: float32 [256, 8192], P('dp', 'mp'), may hold values from -1.8 to 1.8
- second_out: float32 [256, 8192], P('dp', 'mp'), may hold values from 0.0001 to 0.01
Outputs:
- delta_in: bfloat16 [4096, 8192], P(None, 'mp')
- delta_out: bfloat16 [8192, 4096], P('mp')
- new_first_in: float32 [256, 8192], P('dp', 'mp')
- new_second_in: float32 [256, 8192], P('dp', 'mp')
- new_first_out: float32 [256, 8192], P('dp', 'mp')
- new_second_out: float32 [256, 8192], P('dp', 'mp')
All inputs are finite; a program needn't handle non-finite values.
Results may differ from a plain program's by a relative error of at most 0.0058.
Values may be sent and summed in bfloat16 or wider, within the bound.
No kernel may reach another device: no remote copies, remote signals or barrier semaphores. Data moves between devices by JAX's collectives and lax.ppermute only.
A program may use at most 128 MiB of HBM per device.

v0:
```python
import jax
import jax.numpy as jnp
from jax import lax
from jax.sharding import PartitionSpec as P

beta_one = 0.9
beta_two = 0.999
correct_one = 1.0 - 0.9**10
correct_two = 1.0 - 0.999**10
adam_eps = 1e-08


def adam_moments(low, first, second):
    new_first = beta_one * first + (1.0 - beta_one) * low
    new_second = beta_two * second + (1.0 - beta_two) * low * low
    direction = new_first / correct_one / (jnp.sqrt(new_second / correct_two) + adam_eps)
    return (new_first, new_second, direction.astype(jnp.bfloat16))


def contract_rows(left, right):
    return lax.dot_general(
        left, right, (((0,), (0,)), ((), ())), preferred_element_type=jnp.float32
    )


def body(
    acts_in,
    grad_in,
    acts_out,
    grad_out,
    basis_in,
    basis_out,
    first_in,
    second_in,
    first_out,
    second_out,
):
    whole_in, whole_out = (
        lax.all_gather(basis_in, "mp", axis=0, tiled=True),
        lax.all_gather(basis_out, "mp", axis=0, tiled=True),
    )
    proj_in = jnp.dot(acts_in, whole_in, preferred_element_type=jnp.float32)
    proj_out = jnp.dot(grad_out, whole_out, preferred_element_type=jnp.float32)
    proj_in = proj_in.astype(jnp.bfloat16)
    proj_out = proj_out.astype(jnp.bfloat16)
    low_in = contract_rows(lax.all_gather(proj_in, "mp", axis=0, tiled=True), grad_in)
    low_out = contract_rows(lax.all_gather(proj_out, "mp", axis=0, tiled=True), acts_out)
    share_in, share_out = (
        lax.psum_scatter(low_in, "dp", scatter_dimension=0, tiled=True),
        lax.psum_scatter(low_out, "dp", scatter_dimension=0, tiled=True),
    )
    new_first_in, new_second_in, step_in = adam_moments(share_in, first_in, second_in)
    new_first_out, new_second_out, step_out = adam_moments(share_out, first_out, second_out)
    direction_in, direction_out = (
        lax.all_gather(step_in, "dp", axis=0, tiled=True),
        lax.all_gather(step_out, "dp", axis=0, tiled=True),
    )
    delta_in = jnp.dot(whole_in, direction_in, preferred_element_type=jnp.float32)
    delta_out = lax.dot_general(
        direction_out, whole_out, (((0,), (1,)), ((), ())), preferred_element_type=jnp.float32
    )
    return (
        delta_in.astype(jnp.bfloat16),
        delta_out.astype(jnp.bfloat16),
        new_first_in,
        new_second_in,
        new_first_out,
        new_second_out,
    )


def solution(mesh):
    in_specs = (
        P(("dp", "mp"), None),
        P("dp", "mp"),
        P("dp", "mp"),
        P(("dp", "mp"), None),
        P("mp", None),
        P("mp", None),
        P("dp", "mp"),
        P("dp", "mp"),
        P("dp", "mp"),
        P("dp", "mp"),
    )
    out_specs = (
        P(None, "mp"),
        P("mp", None),
        P("dp", "mp"),
        P("dp", "mp"),
        P("dp", "mp"),
        P("dp", "mp"),
    )
    return jax.shard_map(body, mesh=mesh, in_specs=in_specs, out_specs=out_specs, check_vma=False)
```

profile of v0, /device:TPU:1, one launch (start us, length us, event | category | flops | bytes accessed | tf_op | source)
XLA Modules:
  0.0 435.5 jit_solution(14537629724516841553)
XLA Ops:
  7.2 0.0 copy-start
  7.2 0.0 all-gather.9.cloned.1.call-start
  7.2 0.7 all-gather.9.cloned.1.call-update
  7.9 0.0 all-gather.5.cloned.1.call-start
  8.0 0.7 all-gather.5.cloned.1.call-update
  8.7 0.0 all-gather.11.cloned.1.call-start
  8.7 79.7 %all-gather.9.cloned.1.call-done = bf16[4096,256]{1,0:T(8,128)(2,1)} async-done(((bf16[128,256]{1,0:T(8,128)(2,1)}), bf16[4096,256]{1,0:T(8,128)(2,1)}) %all-gather.9.cloned.1.call-update) | async-done | bytes 2097168 | tf_op jit(solution)/shard_map/all_gather | solution.py:40
  88.4 3.0 convolution_convert_fusion.2
  91.4 0.0 all-gather.11.cloned.1.call-update
  91.4 0.0 all-gather.7.cloned.1.call-start
  91.5 74.7 %all-gather.5.cloned.1.call-done = bf16[4096,256]{1,0:T(8,128)(2,1)} async-done(((bf16[128,256]{1,0:T(8,128)(2,1)}), bf16[4096,256]{1,0:T(8,128)(2,1)}) %all-gather.5.cloned.1.call-update) | async-done | bytes 2097168 | tf_op jit(solution)/shard_map/all_gather | solution.py:39
  166.2 3.6 convolution_convert_fusion.3
  169.8 0.0 all-gather.7.cloned.1.call-update
  169.8 0.0 reduce-scatter.5.cloned.1.call-start
  169.8 79.8 %all-gather.11.cloned.1.call-done = bf16[8192,256]{1,0:T(8,128)(2,1)} async-done(((bf16[256,256]{1,0:T(8,128)(2,1)}), bf16[8192,256]{1,0:T(8,128)(2,1)}) %all-gather.11.cloned.1.call-update) | async-done | bytes 4194320 | tf_op jit(solution)/shard_map/all_gather | solution.py:47
  249.6 5.4 %fusion.6 = f32[256,256]{1,0:T(8,128)} fusion(bf16[8192,256]{1,0:T(8,128)(2,1)} %all-gather.11.cloned.1.call-done, bf16[8192,256]{1,0:T(8,128)(2,1)} %param.12), kind=kOutput, calls=%fused_computation.14 | convolution fusion | flops 1073741824 | bytes 8650752 | tf_op jit(solution)/shard_map/dot_general | solution.py:21
  255.0 0.0 reduce-scatter.5.cloned.1.call-update
  255.1 0.0 copy-start.1
  255.1 0.0 copy-start.2
  255.1 0.0 reduce-scatter.3.cloned.1.call-start
  255.2 76.5 %all-gather.7.cloned.1.call-done = bf16[8192,256]{1,0:T(8,128)(2,1)} async-done(((bf16[256,256]{1,0:T(8,128)(2,1)}), bf16[8192,256]{1,0:T(8,128)(2,1)}) %all-gather.7.cloned.1.call-update) | async-done | bytes 4194320 | tf_op jit(solution)/shard_map/all_gather | solution.py:46
  331.6 5.4 %fusion.5 = f32[256,256]{1,0:T(8,128)} fusion(bf16[8192,256]{1,0:T(8,128)(2,1)} %all-gather.7.cloned.1.call-done, bf16[8192,256]{1,0:T(8,128)(2,1)} %param.11), kind=kOutput, calls=%fused_computation.13 | convolution fusion | flops 1073741824 | bytes 8650752 | tf_op jit(solution)/shard_map/dot_general | solution.py:21
  337.1 0.0 reduce-scatter.3.cloned.1.call-update
  337.1 28.1 %reduce-scatter.5.cloned.1.call-done = f32[32,256]{1,0:T(8,128)} async-done(((f32[256,256]{1,0:T(8,128)}), f32[32,256]{1,0:T(8,128)}) %reduce-scatter.5.cloned.1.call-update) | async-done | bytes 32784 | tf_op jit(solution)/shard_map/reduce_scatter | solution.py:50
  365.3 1.4 divide_convert_fusion
  366.7 15.6 %all_gather.23 = bf16[256,256]{1,0:T(8,128)(2,1)S(1)} all-gather(bf16[32,256]{1,0:T(8,128)(2,1)S(1)} %get-tuple-element.12), channel_id=1, replica_groups=mesh['dp'=8,'mp'=32] {'dp'}, dimensions={0}, use_global_device_ids=true | all-gather | bytes 147456 | tf_op jit(solution)/shard_map/all_gather | solution.py:56
  382.2 18.1 %reduce-scatter.3.cloned.1.call-done = f32[32,256]{1,0:T(8,128)} async-done(((f32[256,256]{1,0:T(8,128)}), f32[32,256]{1,0:T(8,128)}) %reduce-scatter.3.cloned.1.call-update) | async-done | bytes 32784 | tf_op jit(solution)/shard_map/reduce_scatter | solution.py:49
  400.3 1.4 divide_convert_fusion.1
  401.7 15.6 %all_gather.20 = bf16[256,256]{1,0:T(8,128)(2,1)S(1)} all-gather(bf16[32,256]{1,0:T(8,128)(2,1)S(1)} %get-tuple-element.15), channel_id=1, replica_groups=mesh['dp'=8,'mp'=32] {'dp'}, dimensions={0}, use_global_device_ids=true | all-gather | bytes 147456 | tf_op jit(solution)/shard_map/all_gather | solution.py:55
  417.3 3.7 fusion
  421.0 4.1 copy.16
  425.0 3.7 convolution_convert_fusion
  (7 shorter events, 0.0 us)
Async XLA Ops:
  7.2 81.3 %copy-start = (bf16[256,4096]{1,0:T(8,128)(2,1)S(1)}, bf16[256,4096]{1,0:T(8,128)(2,1)}, u32[]{:S(2)}) copy-start(bf16[256,4096]{1,0:T(8,128)(2,1)} %param.13) | copy-start | bytes 6291460
  7.2 81.2 %all-gather.9.cloned.1.call-start = ((), (), s32[]{:S(2)}) async-start(), calls=%async_computation.5 | async-start | bytes 2162688 | tf_op jit(solution)/shard_map/all_gather | solution.py:40
  7.9 158.3 %all-gather.5.cloned.1.call-start = ((), (), s32[]{:S(2)}) async-start(), calls=%async_computation.2 | async-start | bytes 2162688 | tf_op jit(solution)/shard_map/all_gather | solution.py:39
  8.7 240.9 %all-gather.11.cloned.1.call-start = ((), (), s32[]{:S(2)}) async-start(), calls=%async_computation.6 | async-start | bytes 4325376 | tf_op jit(solution)/shard_map/all_gather | solution.py:47
  91.4 240.2 %all-gather.7.cloned.1.call-start = ((), (), s32[]{:S(2)}) async-start(), calls=%async_computation.3 | async-start | bytes 4325376 | tf_op jit(solution)/shard_map/all_gather | solution.py:46
  169.8 195.5 %reduce-scatter.5.cloned.1.call-start = ((), (), s32[]{:S(2)}) async-start(), calls=%async_computation.7 | async-start | bytes 294912 | tf_op jit(solution)/shard_map/reduce_scatter | solution.py:50
  255.1 110.2 %copy-start.1 = (f32[32,256]{1,0:T(8,128)S(1)}, f32[32,256]{1,0:T(8,128)}, u32[]{:S(2)}) copy-start(f32[32,256]{1,0:T(8,128)} %param.18) | copy-start | bytes 98308
  255.1 110.2 %copy-start.2 = (f32[32,256]{1,0:T(8,128)S(1)}, f32[32,256]{1,0:T(8,128)}, u32[]{:S(2)}) copy-start(f32[32,256]{1,0:T(8,128)} %param.19) | copy-start | bytes 98308
  255.1 145.2 %copy-start.3 = (f32[32,256]{1,0:T(8,128)S(1)}, f32[32,256]{1,0:T(8,128)}, u32[]{:S(2)}) copy-start(f32[32,256]{1,0:T(8,128)} %param.16) | copy-start | bytes 98308
  255.1 145.2 %copy-start.4 = (f32[32,256]{1,0:T(8,128)S(1)}, f32[32,256]{1,0:T(8,128)}, u32[]{:S(2)}) copy-start(f32[32,256]{1,0:T(8,128)} %param.17) | copy-start | bytes 98308
  255.1 145.2 %reduce-scatter.3.cloned.1.call-start = ((), (), s32[]{:S(2)}) async-start(), calls=%async_computation.4 | async-start | bytes 294912 | tf_op jit(solution)/shard_map/reduce_scatter | solution.py:49
Sparse Core Ops, SparseCore 0:
  10.6 77.7 all-gather.8
  91.0 75.1 all-gather.4
  169.3 80.2 all-gather.10
  252.6 78.9 all-gather.6
  334.6 30.6 reduce-scatter.4
  368.3 31.9 reduce-scatter.2
where the time goes:
time: 436 us
  waiting for transfers between devices  358 us (82%)
  blocking collectives  31.1 us (7%)
  matrix products  24.8 us (6%)
  between operations  14.2 us (3%)
    all_gather x1, waiting for transfers between devices, body(): lax.all_gather(proj_out, 'mp', axis=0, tiled=True)  79.8 us
    all_gather x1, waiting for transfers between devices, body(): lax.all_gather(basis_out, 'mp', axis=0, tiled=True)  79.7 us
    all_gather x1, waiting for transfers between devices, body(): lax.all_gather(proj_in, 'mp', axis=0, tiled=True)  76.5 us
    all_gather x1, waiting for transfers between devices, body(): lax.all_gather(basis_in, 'mp', axis=0, tiled=True)  74.7 us
    reduce_scatter x1, waiting for transfers between devices, body(): lax.psum_scatter(low_out, 'dp', scatter_dimension=0, tiled=True)  28.1 us
    reduce_scatter x1, waiting for transfers between devices, body(): lax.psum_scatter(low_in, 'dp', scatter_dimension=0, tiled=True)  18.1 us
    all_gather x1, blocking collectives, body(): lax.all_gather(step_in, 'dp', axis=0, tiled=True)  15.6 us
    all_gather x1, blocking collectives, body(): lax.all_gather(step_out, 'dp', axis=0, tiled=True)  15.6 us
  transfers between devices with their start and end apart: 6, of which 6 were waited for; matrix products, arithmetic and copies ran while one was open for 4% of the time, Pallas kernels for 0%

commit v1 on v0

v1 whole, which is shorter than its diff:
```python
import functools

import jax
import jax.numpy as jnp
from jax import lax
from jax.experimental import pallas as pl
from jax.experimental.pallas import tpu as pltpu
from jax.sharding import PartitionSpec as P

beta_one = 0.9
beta_two = 0.999
correct_one = 1.0 - 0.9**10
correct_two = 1.0 - 0.999**10
adam_eps = 1e-08

NX, NZ, NY = 4, 8, 4
TOK = 256
R = 256

GROUPS_Z = [[x * NZ + z for z in range(NZ)] for x in range(NX)]
GROUPS_X = [[x * NZ + z for x in range(NX)] for z in range(NZ)]
GROUPS_Y = [[y * 2 + c for y in range(NY)] for c in range(2)]

bar = lax.optimization_barrier


def adam_moments(low, first, second):
    new_first = beta_one * first + (1.0 - beta_one) * low
    new_second = beta_two * second + (1.0 - beta_two) * low * low
    direction = new_first / correct_one / (jnp.sqrt(new_second / correct_two) + adam_eps)
    return (new_first, new_second, direction.astype(jnp.bfloat16))


def shift(a, dx, dz):
    perm = [
        (x * NZ + z, (x + dx) % NX * NZ + (z + dz) % NZ) for x in range(NX) for z in range(NZ)
    ]
    return lax.ppermute(a, "mp", perm)


def other_core(a):
    return lax.ppermute(a, "dp", [(d, d ^ 1) for d in range(2 * NY)])


def gather_direct(a, axis, groups):
    n = len(groups[0])
    many = jnp.broadcast_to(a[None], (n, *a.shape))
    got = lax.all_to_all(many, axis, 0, 0, axis_index_groups=groups, tiled=True)
    return got.reshape(n * a.shape[0], *a.shape[1:])


class Piece:
    def __init__(self, array, segments):
        self.array, self.segments = array, segments

    def moved(self, dx, dz):
        return Piece(
            shift(self.array, dx, dz),
            [(p, x + dx, z + dz, r, n) for p, x, z, r, n in self.segments],
        )

    def rows(self, start, count):
        at, kept = 0, []
        for p, x, z, r, n in self.segments:
            low, high = max(at, start), min(at + n, start + count)
            if low < high:
                kept.append((p, x, z, r + low - at, high - low))
            at += n
        return Piece(self.array[start : start + count], kept)

    def halves(self):
        half = self.array.shape[0] // 2
        return self.rows(0, half), self.rows(half, half)


def stack(pieces):
    return Piece(
        jnp.concatenate([p.array for p in pieces], 0), [s for p in pieces for s in p.segments]
    )


def together(*pieces):
    arrays = bar(tuple(p.array for p in pieces))
    return [Piece(a, p.segments) for a, p in zip(arrays, pieces)]


def gather_pieces(own, partner):
    a, b = Piece(own, [(0, 0, 0, 0, TOK)]), Piece(partner, [(1, 0, 0, 0, TOK)])
    zp, zm, xp, xm = together(b.moved(0, 1), b.moved(0, -1), a.moved(1, 0), a.moved(-1, 0))
    zp2, zm2, x2a, x2b = together(
        zp.moved(0, 1), zm.moved(0, -1), xp.halves()[0].moved(1, 0), xm.halves()[1].moved(-1, 0)
    )
    four = stack([a, xp, xm, x2a, x2b])
    five = stack([b, zp, zm, zp2, zm2])
    up, down, five = together(stack([zp2, four]), stack([zm2, four]), five)
    up, down, xp, xm = together(
        up.moved(0, 1), down.moved(0, -1), five.moved(1, 0), five.moved(-1, 0)
    )
    zp3, fp = up.rows(0, TOK), up.rows(TOK, 4 * TOK)
    zm3, fm = down.rows(0, TOK), down.rows(TOK, 4 * TOK)
    early = [four, five, up, down, xp, xm]
    s = together(
        stack([zp3.halves()[0], fp]),
        stack([zm3.halves()[1], fm]),
        stack([xp.halves()[0], zp3, zm3]),
        stack([xm.halves()[1], zp3, zm3]),
    )
    u4, d4, p4, m4 = together(
        s[0].moved(0, 1), s[1].moved(0, -1), s[2].moved(1, 0), s[3].moved(-1, 0)
    )
    early += [u4, d4, p4, m4]
    h = TOK // 2
    z4 = [u4.rows(0, h), d4.rows(0, h)]
    k = 5 * h
    y3p, y3m = p4.rows(k, 2 * TOK), m4.rows(k, 2 * TOK)
    s = together(
        u4.rows(h, 4 * TOK),
        d4.rows(h, 4 * TOK),
        stack(z4 + [y3p.halves()[0]]),
        stack(z4 + [y3m.halves()[1]]),
    )
    u5, d5, p5, m5 = together(
        s[0].moved(0, 1), s[1].moved(0, -1), s[2].moved(1, 0), s[3].moved(-1, 0)
    )
    s = together(u5.halves()[0], d5.halves()[1], p5.rows(0, h), m5.rows(h, h))
    last = together(s[0].moved(0, 1), s[1].moved(0, -1), s[2].moved(1, 0), s[3].moved(-1, 0))
    return early, [u5, d5, p5, m5, *last]


def low_kernel(count, segments, blocks_ref, grads_own, grads_partner, *refs):
    pieces, start_ref, out_ref, held, arrived = refs[:count], refs[count], *refs[count + 1 :]
    copies, at = [], 0
    for index, (_, part, row, rows, _) in enumerate(segments):
        source = grads_partner if part else grads_own
        first = pl.multiple_of(blocks_ref[index] * TOK + row, 128)
        copies.append(
            pltpu.make_async_copy(
                source.at[pl.ds(first, rows)], held.at[pl.ds(at, rows)], arrived.at[index]
            )
        )
        copies[-1].start()
        at += rows
    total, at = start_ref[...], 0
    for index, (piece, _, _, rows, offset) in enumerate(segments):
        copies[index].wait()
        total += lax.dot_general(
            pieces[piece][pl.ds(offset, rows)],
            held[pl.ds(at, rows)],
            (((0,), (0,)), ((), ())),
            preferred_element_type=jnp.float32,
        )
        at += rows
    out_ref[...] = total


def low_of(pieces, grads_own, grads_partner, start):
    x, z = lax.axis_index("mp") // NZ, lax.axis_index("mp") % NZ
    segments, dxs, dzs, total = [], [], [], 0
    for index, piece in enumerate(pieces):
        offset = 0
        for part, dx, dz, row, rows in piece.segments:
            segments.append((index, part, row, rows, offset))
            dxs.append(dx)
            dzs.append(dz)
            offset += rows
            total += rows
    blocks = (x - jnp.array(dxs, jnp.int32) + NX) % NX * NZ + (
        z - jnp.array(dzs, jnp.int32) + NZ
    ) % NZ
    vmem = pl.BlockSpec(memory_space=pltpu.VMEM)
    hbm = pl.BlockSpec(memory_space=pl.ANY)
    return pl.pallas_call(
        functools.partial(low_kernel, len(pieces), segments),
        out_shape=jax.ShapeDtypeStruct((R, 256), jnp.float32),
        in_specs=[pl.BlockSpec(memory_space=pltpu.SMEM), hbm, hbm]
        + [vmem] * (len(pieces) + 1),
        out_specs=vmem,
        scratch_shapes=[
            pltpu.VMEM((total, 256), jnp.bfloat16),
            pltpu.SemaphoreType.DMA((len(segments),)),
        ],
        compiler_params=pltpu.CompilerParams(vmem_limit_bytes=40 << 20),
        cost_estimate=pl.CostEstimate(
            flops=2 * total * 256 * 256, bytes_accessed=total * 1024, transcendentals=0
        ),
    )(blocks, grads_own, grads_partner, *[p.array for p in pieces], start)


def body(
    acts_in,
    grad_in,
    acts_out,
    grad_out,
    basis_in,
    basis_out,
    first_in,
    second_in,
    first_out,
    second_out,
):
    even = lax.axis_index("dp") % 2 == 0

    def mine(a, b):
        return jnp.where(even, a, b)

    left_partner = other_core(mine(grad_out, acts_in))
    grads_partner = other_core(mine(acts_out, grad_in))
    moments_partner = other_core(
        jnp.stack([mine(first_out, first_in), mine(second_out, second_in)])
    )
    grads_own = mine(grad_in, acts_out)

    along_z = gather_direct(mine(basis_in, basis_out), "mp", GROUPS_Z)
    basis = gather_direct(along_z, "mp", GROUPS_X)
    basis_other = other_core(basis)

    def project(left):
        return jnp.dot(left, basis, preferred_element_type=jnp.float32).astype(jnp.bfloat16)

    early, late = gather_pieces(project(mine(acts_in, grad_out)), project(left_partner))
    low = low_of(early, grads_own, grads_partner, jnp.zeros((R, 256), jnp.float32))
    low = low_of(late, grads_own, grads_partner, low)

    shares = lax.all_to_all(
        low.reshape(NY, R // NY, 256), "dp", 0, 0, axis_index_groups=GROUPS_Y, tiled=True
    )
    share = shares[0] + shares[1] + shares[2] + shares[3]

    def both(own, partner):
        return mine(jnp.concatenate([own, partner]), jnp.concatenate([partner, own]))

    new_first, new_second, step = adam_moments(
        share,
        both(mine(first_in, first_out), moments_partner[0]),
        both(mine(second_in, second_out), moments_partner[1]),
    )
    h = R // NY // 2
    given = other_core(
        jnp.stack([mine(m[h:], m[:h]) for m in (new_first, new_second)])
    )
    kept = [mine(m[:h], m[h:]) for m in (new_first, new_second)]

    direction = gather_direct(step, "dp", GROUPS_Y)
    direction_other = other_core(direction)
    delta_in = jnp.dot(
        mine(basis, basis_other),
        mine(direction, direction_other),
        preferred_element_type=jnp.float32,
    )
    delta_out = lax.dot_general(
        mine(direction_other, direction),
        mine(basis_other, basis),
        (((0,), (1,)), ((), ())),
        preferred_element_type=jnp.float32,
    )
    return (
        delta_in.astype(jnp.bfloat16),
        delta_out.astype(jnp.bfloat16),
        mine(kept[0], given[0]),
        mine(kept[1], given[1]),
        mine(given[0], kept[0]),
        mine(given[1], kept[1]),
    )


def solution(mesh):
    in_specs = (
        P(("dp", "mp"), None),
        P("dp", "mp"),
        P("dp", "mp"),
        P(("dp", "mp"), None),
        P("mp", None),
        P("mp", None),
        P("dp", "mp"),
        P("dp", "mp"),
        P("dp", "mp"),
        P("dp", "mp"),
    )
    out_specs = (
        P(None, "mp"),
        P("mp", None),
        P("dp", "mp"),
        P("dp", "mp"),
        P("dp", "mp"),
        P("dp", "mp"),
    )
    return jax.shard_map(body, mesh=mesh, in_specs=in_specs, out_specs=out_specs, check_vma=False)
```

time: 436 us -> 197 us (0.45)
  waiting for transfers between devices: 358 us -> 63.7 us
  starting transfers between devices: 0.24 us -> 79.8 us
  blocking collectives: 31.1 us -> 0 us
  Pallas kernels: 0 us -> 18.4 us
  matrix products: 24.8 us -> 9.6 us
  between operations: 14.2 us -> 1.23 us
  other arithmetic: 2.79 us -> 12.9 us
  local copies, waits for them, and re-layouts: 4.1 us -> 11 us
    all_gather x4 -> x0, waiting for transfers between devices: 311 us -> none  [the longest x1 79.8 us: body(): lax.all_gather(proj_out, 'mp', axis=0, tiled=True)]
    ppermute x0 -> x30, starting transfers between devices: none -> 59.1 us  [the longest x24 34.9 us: shift(): return lax.ppermute(a, 'mp', perm)]
    reduce_scatter x2 -> x0, waiting for transfers between devices: 46.2 us -> none  [the longest x1 28.1 us: body(): lax.psum_scatter(low_out, 'dp', scatter_dimension=0, tiled=True)]
    all_to_all x0 -> x4, waiting for transfers between devices: none -> 38.5 us  [the longest x3 33 us: gather_direct(): got = lax.all_to_all(many, axis, 0, 0, axis_index_groups=groups, tiled=True)]
    all_gather x2 -> x0, blocking collectives: 31.1 us -> none  [the longest x1 15.6 us: body(): lax.all_gather(step_in, 'dp', axis=0, tiled=True)]
    ppermute x0 -> x30, waiting for transfers between devices: none -> 25.2 us  [the longest x24 24.9 us: shift(): return lax.ppermute(a, 'mp', perm)]
    all_to_all x0 -> x4, starting transfers between devices: none -> 20.7 us  [the longest x3 16.4 us: gather_direct(): got = lax.all_to_all(many, axis, 0, 0, axis_index_groups=groups, tiled=True)]
    pallas_call x0 -> x2, Pallas kernels: none -> 18.4 us  [low_of(): pl.pallas_call(functools.partial(low_kernel, len(pieces), segments), out_...]
  transfers between devices with their start and end apart: 6 -> 34, of which waited for: 6 -> 11; matrix products, arithmetic and copies ran while one was open for 4% -> 10% of each run, Pallas kernels for 0% -> 9%
where the time goes in v1:
time: 197 us
  starting transfers between devices  79.8 us (41%)
  waiting for transfers between devices  63.7 us (32%)
  Pallas kernels  18.4 us (9%)
  other arithmetic  12.9 us (7%)
  local copies, waits for them, and re-layouts  11 us (6%)
  matrix products  9.6 us (5%)
    ppermute x24, starting transfers between devices, shift(): return lax.ppermute(a, 'mp', perm)  34.9 us
    all_to_all x3, waiting for transfers between devices, gather_direct(): got = lax.all_to_all(many, axis, 0, 0, axis_index_groups=groups, tiled=True)  33 us
    ppermute x24, waiting for transfers between devices, shift(): return lax.ppermute(a, 'mp', perm)  24.9 us
    ppermute x6, starting transfers between devices, other_core(): return lax.ppermute(a, 'dp', [(d, d ^ 1) for d in range(2 * NY)])  24.2 us
    pallas_call x2, Pallas kernels, low_of(): pl.pallas_call(functools.partial(low_kernel, len(pieces), segments), out_...  18.4 us
    all_to_all x3, starting transfers between devices, gather_direct(): got = lax.all_to_all(many, axis, 0, 0, axis_index_groups=groups, tiled=True)  16.4 us
    select_n x6, other arithmetic, mine(): return jnp.where(even, a, b)  11.2 us
    unnamed x53, local copies, waits for them, and re-layouts  6.04 us
  transfers between devices with their start and end apart: 34, of which 11 were waited for; matrix products, arithmetic and copies ran while one was open for 10% of the time, Pallas kernels for 9%

profile of v1, /device:TPU:1, one launch (start us, length us, event | category | flops | bytes accessed | tf_op | source)
XLA Modules:
  0.0 196.7 jit_solution(5030319963738211423)
XLA Ops:
  2.3 9.0 %all-to-all-start = ((bf16[8,128,256]{2,1,0:T(8,128)(2,1)}), bf16[8,128,256]{2,1,0:T(8,128)(2,1)S(1)}, u32[]{:S(2)}, u32[]{:S(2)}) async-start(bf16[8,128,256]{2,1,0:T(8,128)(2,1)} %broadcast_in_dim.24), calls=%async_computation | async-start | bytes 1048576 | tf_op jit(solution)/shard_map/all_to_all | solution.py:48
  11.4 3.1 %broadcast_select_fusion.2 = bf16[256,4096]{1,0:T(8,128)(2,1)} fusion(bf16[256,4096]{1,0:T(8,128)(2,1)} %param.17, bf16[256,4096]{1,0:T(8,128)(2,1)} %param.14, pred[]{:T(512)S(6)} %eq.13), kind=kLoop, calls=%fused_computation.9 | loop fusion | flops 1048576 | bytes 6291457 | tf_op jit(solution)/shard_map/jit(_where)/select_n | solution.py:204
  15.4 13.9 %all-to-all-done = bf16[8,128,256]{2,1,0:T(8,128)(2,1)S(1)} async-done(((bf16[8,128,256]{2,1,0:T(8,128)(2,1)}), bf16[8,128,256]{2,1,0:T(8,128)(2,1)S(1)}, u32[]{:S(2)}, u32[]{:S(2)}) %all-to-all-start) | async-done | bytes 524320 | tf_op jit(solution)/shard_map/all_to_all | solution.py:48
  30.8 4.0 %all-to-all-start.1 = ((bf16[4,1024,256]{2,1,0:T(8,128)(2,1)}), bf16[4,1024,256]{2,1,0:T(8,128)(2,1)S(1)}, u32[]{:S(2)}, u32[]{:S(2)}) async-start(bf16[4,1024,256]{2,1,0:T(8,128)(2,1)} %broadcast_in_dim.26), calls=%async_computation.1 | async-start | bytes 4194304 | tf_op jit(solution)/shard_map/all_to_all | solution.py:48
  34.8 5.7 %broadcast_select_fusion = (bf16[8192,256]{1,0:T(8,128)(2,1)}, bf16[8192,256]{1,0:T(8,128)(2,1)}) fusion(bf16[8192,256]{1,0:T(8,128)(2,1)} %param.16, bf16[8192,256]{1,0:T(8,128)(2,1)} %param.15, pred[]{:T(512)S(6)} %eq.13), kind=kLoop, calls=%fused_computation.2 | loop fusion | flops 4194304 | bytes 16777216 | tf_op jit(solution)/shard_map/jit(_where)/select_n | solution.py:204
  41.3 19.1 %all-to-all-done.1 = bf16[4,1024,256]{2,1,0:T(8,128)(2,1)S(1)} async-done(((bf16[4,1024,256]{2,1,0:T(8,128)(2,1)}), bf16[4,1024,256]{2,1,0:T(8,128)(2,1)S(1)}, u32[]{:S(2)}, u32[]{:S(2)}) %all-to-all-start.1) | async-done | bytes 2097184 | tf_op jit(solution)/shard_map/all_to_all | solution.py:48
  60.4 3.1 %constant_dynamic-update-slice_fusion.16 = (bf16[1280,256]{1,0:T(8,128)(2,1)S(1)}, bf16[256,256]{1,0:T(8,128)(2,1)S(1)}) fusion(bf16[256,4096]{1,0:T(8,128)(2,1)} %collective-permute-done.3, bf16[4096,256]{1,0:T(8,128)(2,1)S(1)} %bitcast.40), kind=kOutput, calls=%fused_computation.69 | convolution fusion | flops 536936448 | bytes 4456448 | tf_op jit(solution)/shard_map/dot_general | solution.py:218
  63.6 2.7 %collective-permute-start.5 = (bf16[256,256]{1,0:T(8,128)(2,1)S(1)}, bf16[256,256]{1,0:T(8,128)(2,1)S(1)}, u32[]{:S(2)}, u32[]{:S(2)}) collective-permute-start(bf16[256,256]{1,0:T(8,128)(2,1)S(1)} %get-tuple-element.126), channel_id=1, source_target_pairs={{0,7},{1,0},{2,1},{3,2},{4,3},{5,4},{6,5},{7,6},{8,15},{9,8},{10,9... | collective-permute-start | bytes 393224 | tf_op jit(solution)/shard_map/ppermute | solution.py:38
  72.3 2.7 %collective-permute-start.11 = (bf16[128,256]{1,0:T(8,128)(2,1)S(1)}, bf16[128,256]{1,0:T(8,128)(2,1)S(1)}, u32[]{:S(2)}, u32[]{:S(2)}) collective-permute-start(bf16[128,256]{1,0:T(8,128)(2,1)S(1)} %slice.107), channel_id=1, source_target_pairs={{0,24},{1,25},{2,26},{3,27},{4,28},{5,29},{6,30},{7,31},{8,0},{9,1... | collective-permute-start | bytes 196616 | tf_op jit(solution)/shard_map/ppermute | solution.py:38
  74.9 2.7 %collective-permute-start.9 = (bf16[256,256]{1,0:T(8,128)(2,1)S(1)}, bf16[256,256]{1,0:T(8,128)(2,1)S(1)}, u32[]{:S(2)}, u32[]{:S(2)}) collective-permute-start(bf16[256,256]{1,0:T(8,128)(2,1)S(1)} %collective-permute-done.5), channel_id=1, source_target_pairs={{0,7},{1,0},{2,1},{3,2},{4,3},{5,4},{6,5},{7,6},{8,15},{9,8},{10,9... | collective-permute-start | bytes 393224 | tf_op jit(solution)/shard_map/ppermute | solution.py:38
  77.7 2.6 %collective-permute-done.8 = bf16[256,256]{1,0:T(8,128)(2,1)S(1)} collective-permute-done((bf16[256,256]{1,0:T(8,128)(2,1)S(1)}, bf16[256,256]{1,0:T(8,128)(2,1)S(1)}, u32[]{:S(2)}, u32[]{:S(2)}) %collective-permute-start.8) | collective-permute-done | bytes 131104 | tf_op jit(solution)/shard_map/ppermute | solution.py:38
  81.4 2.7 %collective-permute-start.13 = (bf16[1280,256]{1,0:T(8,128)(2,1)S(1)}, bf16[1280,256]{1,0:T(8,128)(2,1)S(1)}, u32[]{:S(2)}, u32[]{:S(2)}) collective-permute-start(bf16[1280,256]{1,0:T(8,128)(2,1)S(1)} %get-tuple-element.54), channel_id=1, source_target_pairs={{0,7},{1,0},{2,1},{3,2},{4,3},{5,4},{6,5},{7,6},{8,15},{9,8},{10,9... | collective-permute-start | bytes 1966088 | tf_op jit(solution)/shard_map/ppermute | solution.py:38
  84.0 2.7 %collective-permute-start.15 = (bf16[1280,256]{1,0:T(8,128)(2,1)S(1)}, bf16[1280,256]{1,0:T(8,128)(2,1)S(1)}, u32[]{:S(2)}, u32[]{:S(2)}) collective-permute-start(bf16[1280,256]{1,0:T(8,128)(2,1)S(1)} %get-tuple-element.55.refs_1_), channel_id=1, source_target_pairs={{0,24},{1,25},{2,26},{3,27},{4,28},{5,29},{6,30},{7,31},{8,0},{9,1... | collective-permute-start | bytes 1966088 | tf_op jit(solution)/shard_map/ppermute | solution.py:38
  86.7 7.3 %collective-permute-done.12.refs_2_ = bf16[1280,256]{1,0:T(8,128)(2,1)S(1)} collective-permute-done((bf16[1280,256]{1,0:T(8,128)(2,1)S(1)}, bf16[1280,256]{1,0:T(8,128)(2,1)S(1)}, u32[]{:S(2)}, u32[]{:S(2)}) %collective-permute-start.12) | collective-permute-done | bytes 655392 | tf_op jit(solution)/shard_map/ppermute | solution.py:38
  97.3 2.7 %collective-permute-start.17 = (bf16[1152,256]{1,0:T(8,128)(2,1)S(1)}, bf16[1152,256]{1,0:T(8,128)(2,1)S(1)}, u32[]{:S(2)}, u32[]{:S(2)}) collective-permute-start(bf16[1152,256]{1,0:T(8,128)(2,1)S(1)} %concatenate.91), channel_id=1, source_target_pairs={{0,7},{1,0},{2,1},{3,2},{4,3},{5,4},{6,5},{7,6},{8,15},{9,8},{10,9... | collective-permute-start | bytes 1769480 | tf_op jit(solution)/shard_map/ppermute | solution.py:38
  99.9 2.7 %collective-permute-start.19 = (bf16[1152,256]{1,0:T(8,128)(2,1)S(1)}, bf16[1152,256]{1,0:T(8,128)(2,1)S(1)}, u32[]{:S(2)}, u32[]{:S(2)}) collective-permute-start(bf16[1152,256]{1,0:T(8,128)(2,1)S(1)} %get-tuple-element.63), channel_id=1, source_target_pairs={{0,24},{1,25},{2,26},{3,27},{4,28},{5,29},{6,30},{7,31},{8,0},{9,1... | collective-permute-start | bytes 1769480 | tf_op jit(solution)/shard_map/ppermute | solution.py:38
  102.6 4.6 %collective-permute-done.16.refs_6_ = bf16[1152,256]{1,0:T(8,128)(2,1)S(1)} collective-permute-done((bf16[1152,256]{1,0:T(8,128)(2,1)S(1)}, bf16[1152,256]{1,0:T(8,128)(2,1)S(1)}, u32[]{:S(2)}, u32[]{:S(2)}) %collective-permute-start.16) | collective-permute-done | bytes 589856 | tf_op jit(solution)/shard_map/ppermute | solution.py:38
  107.2 3.0 %collective-permute-done.18.refs_8_ = bf16[1152,256]{1,0:T(8,128)(2,1)S(1)} collective-permute-done((bf16[1152,256]{1,0:T(8,128)(2,1)S(1)}, bf16[1152,256]{1,0:T(8,128)(2,1)S(1)}, u32[]{:S(2)}, u32[]{:S(2)}) %collective-permute-start.18) | collective-permute-done | bytes 589856 | tf_op jit(solution)/shard_map/ppermute | solution.py:38
  113.5 2.7 %collective-permute-start.21 = (bf16[1024,256]{1,0:T(8,128)(2,1)}, bf16[1024,256]{1,0:T(8,128)(2,1)S(1)}, u32[]{:S(2)}, u32[]{:S(2)}) collective-permute-start(bf16[1024,256]{1,0:T(8,128)(2,1)} %slice.115), channel_id=1, source_target_pairs={{0,7},{1,0},{2,1},{3,2},{4,3},{5,4},{6,5},{7,6},{8,15},{9,8},{10,9... | collective-permute-start | bytes 1572872 | tf_op jit(solution)/shard_map/ppermute | solution.py:38
  116.2 8.9 %collective-permute-start = (bf16[4096,256]{1,0:T(8,128)(2,1)}, bf16[4096,256]{1,0:T(8,128)(2,1)}, u32[]{:S(2)}, u32[]{:S(2)}) collective-permute-start(bf16[4096,256]{1,0:T(8,128)(2,1)} %bitcast.42), channel_id=1, source_target_pairs={{0,32},{32,0},{64,96},{96,64},{128,160},{160,128},{192,224},{224,1... | collective-permute-start | bytes 6291464 | tf_op jit(solution)/shard_map/ppermute | solution.py:42
  128.2 2.9 %collective-permute-done.23.refs_3_ = bf16[512,256]{1,0:T(8,128)(2,1)S(1)} collective-permute-done((bf16[512,256]{1,0:T(8,128)(2,1)}, bf16[512,256]{1,0:T(8,128)(2,1)S(1)}, u32[]{:S(2)}, u32[]{:S(2)}) %collective-permute-start.23) | collective-permute-done | bytes 262176 | tf_op jit(solution)/shard_map/ppermute | solution.py:38
  131.3 2.7 %collective-permute-start.25 = (bf16[512,256]{1,0:T(8,128)(2,1)S(1)}, bf16[512,256]{1,0:T(8,128)(2,1)S(1)}, u32[]{:S(2)}, u32[]{:S(2)}) collective-permute-start(bf16[512,256]{1,0:T(8,128)(2,1)S(1)} %slice.121), channel_id=1, source_target_pairs={{0,7},{1,0},{2,1},{3,2},{4,3},{5,4},{6,5},{7,6},{8,15},{9,8},{10,9... | collective-permute-start | bytes 786440 | tf_op jit(solution)/shard_map/ppermute | solution.py:38
  134.0 2.7 %collective-permute-start.26 = (bf16[128,256]{1,0:T(8,128)(2,1)S(1)}, bf16[128,256]{1,0:T(8,128)(2,1)S(1)}, u32[]{:S(2)}, u32[]{:S(2)}) collective-permute-start(bf16[128,256]{1,0:T(8,128)(2,1)S(1)} %slice.122), channel_id=1, source_target_pairs={{0,8},{1,9},{2,10},{3,11},{4,12},{5,13},{6,14},{7,15},{8,16},{9,17... | collective-permute-start | bytes 196616 | tf_op jit(solution)/shard_map/ppermute | solution.py:38
  137.3 2.8 %collective-permute-start.1 = (f32[2,32,256]{2,1,0:T(8,128)}, f32[2,32,256]{2,1,0:T(8,128)S(1)}, u32[]{:S(2)}, u32[]{:S(2)}) collective-permute-start(f32[2,32,256]{2,1,0:T(8,128)} %pad_maximum_fusion.8), channel_id=1, source_target_pairs={{0,32},{32,0},{64,96},{96,64},{128,160},{160,128},{192,224},{224,1... | collective-permute-start | bytes 196616 | tf_op jit(solution)/shard_map/ppermute | solution.py:42
  146.7 11.7 %shard_map.181.refs_8_ = f32[256,256]{1,0:T(8,128)S(1)} custom-call(s32[54]{0:T(128)S(1)} %fusion.34.blocks_ref, bf16[8192,256]{1,0:T(8,128)(2,1)S(1)} %copy-done, bf16[8192,256]{1,0:T(8,128)(2,1)} %collective-permute-done.2.grads_partner, bf16[1024,256]{1,0:T(8,128)(2,1)S(1)} %copy-done.9, bf16[1280,256]{1,0:T(8,128)(2,1)S(1)} %copy-done.11, ...), custom_call_target="tpu_custom_call" | custom-call | flops 1577058304 | bytes 12320768 | tf_op jit(solution)/shard_map/pallas_call | solution.py:172
  158.5 6.7 %shard_map.182 = f32[256,256]{1,0:T(8,128)} custom-call(s32[23]{0:T(128)S(1)} %fusion.33.blocks_ref, bf16[8192,256]{1,0:T(8,128)(2,1)S(1)} %copy-done.1, bf16[8192,256]{1,0:T(8,128)(2,1)} %collective-permute-done.2.grads_partner, bf16[1024,256]{1,0:T(8,128)(2,1)S(1)} %collective-permute-done.20.refs_0_, ...), custom_call_target="tpu_custom_call" | custom-call | flops 570425344 | bytes 4456448 | tf_op jit(solution)/shard_map/pallas_call | solution.py:172
  165.2 4.3 %all-to-all-start.2 = ((f32[4,64,256]{2,1,0:T(8,128)}), f32[4,64,256]{2,1,0:T(8,128)S(1)}, u32[]{:S(2)}, u32[]{:S(2)}) async-start(f32[4,64,256]{2,1,0:T(8,128)} %bitcast.5), calls=%async_computation.2 | async-start | bytes 524288 | tf_op jit(solution)/shard_map/all_to_all | solution.py:224
  169.5 5.5 %all-to-all-done.2 = f32[4,64,256]{2,1,0:T(8,128)S(1)} async-done(((f32[4,64,256]{2,1,0:T(8,128)}), f32[4,64,256]{2,1,0:T(8,128)S(1)}, u32[]{:S(2)}, u32[]{:S(2)}) %all-to-all-start.2) | async-done | bytes 262176 | tf_op jit(solution)/shard_map/all_to_all | solution.py:224
  175.8 3.3 %all-to-all-start.3 = ((bf16[4,64,256]{2,1,0:T(8,128)(2,1)}), bf16[4,64,256]{2,1,0:T(8,128)(2,1)S(1)}, u32[]{:S(2)}, u32[]{:S(2)}) async-start(bf16[4,64,256]{2,1,0:T(8,128)(2,1)} %broadcast_in_dim.29), calls=%async_computation.3 | async-start | bytes 262144 | tf_op jit(solution)/shard_map/all_to_all | solution.py:48
  179.2 5.0 %collective-permute-start.29 = (f32[2,32,256]{2,1,0:T(8,128)S(1)}, f32[2,32,256]{2,1,0:T(8,128)S(1)}, u32[]{:S(2)}, u32[]{:S(2)}) collective-permute-start(f32[2,32,256]{2,1,0:T(8,128)S(1)} %pad_maximum_fusion.9), channel_id=1, source_target_pairs={{0,32},{32,0},{64,96},{96,64},{128,160},{160,128},{192,224},{224,1... | collective-permute-start | bytes 196616 | tf_op jit(solution)/shard_map/ppermute | solution.py:42
  184.1 5.8 %collective-permute-start.28 = (bf16[256,256]{1,0:T(8,128)(2,1)S(1)}, bf16[256,256]{1,0:T(8,128)(2,1)S(1)}, u32[]{:S(2)}, u32[]{:S(2)}) collective-permute-start(bf16[256,256]{1,0:T(8,128)(2,1)S(1)} %bitcast.46), channel_id=1, source_target_pairs={{0,32},{32,0},{64,96},{96,64},{128,160},{160,128},{192,224},{224,1... | collective-permute-start | bytes 393224 | tf_op jit(solution)/shard_map/ppermute | solution.py:42
  193.0 3.6 %convolution_convert_fusion.1 = bf16[4096,256]{1,0:T(8,128)(2,1)} fusion(bf16[4096,256]{1,0:T(8,128)(2,1)S(1)} %bitcast.44, bf16[4096,256]{1,0:T(8,128)(2,1)} %collective-permute-done, pred[]{:T(512)S(6)} %eq.13, bf16[256,256]{1,0:T(8,128)(2,1)S(1)} %bitcast.48, bf16[256,256]{1,0:T(8,128)(2,1)S(1)} %collective-permute-done.28), kind=kOutput, calls=%fused_computation.1 | convolution fusion | flops 539033600 | bytes 6553601 | tf_op jit(solution)/shard_map/dot_general | solution.py:245
  (138 shorter events, 32.7 us)
Async XLA Ops:
  2.3 27.0 %all-to-all-start = ((bf16[8,128,256]{2,1,0:T(8,128)(2,1)}), bf16[8,128,256]{2,1,0:T(8,128)(2,1)S(1)}, u32[]{:S(2)}, u32[]{:S(2)}) async-start(bf16[8,128,256]{2,1,0:T(8,128)(2,1)} %broadcast_in_dim.24), calls=%async_computation | async-start | bytes 1048576 | tf_op jit(solution)/shard_map/all_to_all | solution.py:48
  14.5 26.8 %collective-permute-start.3 = (bf16[256,4096]{1,0:T(8,128)(2,1)}, bf16[256,4096]{1,0:T(8,128)(2,1)}, u32[]{:S(2)}, u32[]{:S(2)}) collective-permute-start(bf16[256,4096]{1,0:T(8,128)(2,1)} %broadcast_select_fusion.2), channel_id=1, source_target_pairs={{0,32},{32,0},{64,96},{96,64},{128,160},{160,128},{192,224},{224,1... | collective-permute-start | bytes 6291464 | tf_op jit(solution)/shard_map/ppermute | solution.py:42
  30.8 29.6 %all-to-all-start.1 = ((bf16[4,1024,256]{2,1,0:T(8,128)(2,1)}), bf16[4,1024,256]{2,1,0:T(8,128)(2,1)S(1)}, u32[]{:S(2)}, u32[]{:S(2)}) async-start(bf16[4,1024,256]{2,1,0:T(8,128)(2,1)} %broadcast_in_dim.26), calls=%async_computation.1 | async-start | bytes 4194304 | tf_op jit(solution)/shard_map/all_to_all | solution.py:48
  40.5 96.8 %collective-permute-start.2 = (bf16[8192,256]{1,0:T(8,128)(2,1)}, bf16[8192,256]{1,0:T(8,128)(2,1)}, u32[]{:S(2)}, u32[]{:S(2)}) collective-permute-start(bf16[8192,256]{1,0:T(8,128)(2,1)} %get-tuple-element.86), channel_id=1, source_target_pairs={{0,32},{32,0},{64,96},{96,64},{128,160},{160,128},{192,224},{224,1... | collective-permute-start | bytes 12582920 | tf_op jit(solution)/shard_map/ppermute | solution.py:42
  63.5 6.3 %collective-permute-start.4 = (bf16[256,256]{1,0:T(8,128)(2,1)S(1)}, bf16[256,256]{1,0:T(8,128)(2,1)S(1)}, u32[]{:S(2)}, u32[]{:S(2)}) collective-permute-start(bf16[256,256]{1,0:T(8,128)(2,1)S(1)} %get-tuple-element.126), channel_id=1, source_target_pairs={{0,1},{1,2},{2,3},{3,4},{4,5},{5,6},{6,7},{7,0},{8,9},{9,10},{10,1... | collective-permute-start | bytes 393224 | tf_op jit(solution)/shard_map/ppermute | solution.py:38
  63.6 6.2 %collective-permute-start.5 = (bf16[256,256]{1,0:T(8,128)(2,1)S(1)}, bf16[256,256]{1,0:T(8,128)(2,1)S(1)}, u32[]{:S(2)}, u32[]{:S(2)}) collective-permute-start(bf16[256,256]{1,0:T(8,128)(2,1)S(1)} %get-tuple-element.126), channel_id=1, source_target_pairs={{0,7},{1,0},{2,1},{3,2},{4,3},{5,4},{6,5},{7,6},{8,15},{9,8},{10,9... | collective-permute-start | bytes 393224 | tf_op jit(solution)/shard_map/ppermute | solution.py:38
  72.2 5.5 %collective-permute-start.10 = (bf16[128,256]{1,0:T(8,128)(2,1)S(1)}, bf16[128,256]{1,0:T(8,128)(2,1)S(1)}, u32[]{:S(2)}, u32[]{:S(2)}) collective-permute-start(bf16[128,256]{1,0:T(8,128)(2,1)S(1)} %slice.106), channel_id=1, source_target_pairs={{0,8},{1,9},{2,10},{3,11},{4,12},{5,13},{6,14},{7,15},{8,16},{9,17... | collective-permute-start | bytes 196616 | tf_op jit(solution)/shard_map/ppermute | solution.py:38
  72.3 5.4 %collective-permute-start.11 = (bf16[128,256]{1,0:T(8,128)(2,1)S(1)}, bf16[128,256]{1,0:T(8,128)(2,1)S(1)}, u32[]{:S(2)}, u32[]{:S(2)}) collective-permute-start(bf16[128,256]{1,0:T(8,128)(2,1)S(1)} %slice.107), channel_id=1, source_target_pairs={{0,24},{1,25},{2,26},{3,27},{4,28},{5,29},{6,30},{7,31},{8,0},{9,1... | collective-permute-start | bytes 196616 | tf_op jit(solution)/shard_map/ppermute | solution.py:38
  74.9 5.3 %collective-permute-start.8 = (bf16[256,256]{1,0:T(8,128)(2,1)S(1)}, bf16[256,256]{1,0:T(8,128)(2,1)S(1)}, u32[]{:S(2)}, u32[]{:S(2)}) collective-permute-start(bf16[256,256]{1,0:T(8,128)(2,1)S(1)} %collective-permute-done.4), channel_id=1, source_target_pairs={{0,1},{1,2},{2,3},{3,4},{4,5},{5,6},{6,7},{7,0},{8,9},{9,10},{10,1... | collective-permute-start | bytes 393224 | tf_op jit(solution)/shard_map/ppermute | solution.py:38
  74.9 5.3 %collective-permute-start.9 = (bf16[256,256]{1,0:T(8,128)(2,1)S(1)}, bf16[256,256]{1,0:T(8,128)(2,1)S(1)}, u32[]{:S(2)}, u32[]{:S(2)}) collective-permute-start(bf16[256,256]{1,0:T(8,128)(2,1)S(1)} %collective-permute-done.5), channel_id=1, source_target_pairs={{0,7},{1,0},{2,1},{3,2},{4,3},{5,4},{6,5},{7,6},{8,15},{9,8},{10,9... | collective-permute-start | bytes 393224 | tf_op jit(solution)/shard_map/ppermute | solution.py:38
  81.4 12.6 %collective-permute-start.12 = (bf16[1280,256]{1,0:T(8,128)(2,1)S(1)}, bf16[1280,256]{1,0:T(8,128)(2,1)S(1)}, u32[]{:S(2)}, u32[]{:S(2)}) collective-permute-start(bf16[1280,256]{1,0:T(8,128)(2,1)S(1)} %get-tuple-element.53), channel_id=1, source_target_pairs={{0,1},{1,2},{2,3},{3,4},{4,5},{5,6},{6,7},{7,0},{8,9},{9,10},{10,1... | collective-permute-start | bytes 1966088 | tf_op jit(solution)/shard_map/ppermute | solution.py:38
  81.4 12.6 %collective-permute-start.13 = (bf16[1280,256]{1,0:T(8,128)(2,1)S(1)}, bf16[1280,256]{1,0:T(8,128)(2,1)S(1)}, u32[]{:S(2)}, u32[]{:S(2)}) collective-permute-start(bf16[1280,256]{1,0:T(8,128)(2,1)S(1)} %get-tuple-element.54), channel_id=1, source_target_pairs={{0,7},{1,0},{2,1},{3,2},{4,3},{5,4},{6,5},{7,6},{8,15},{9,8},{10,9... | collective-permute-start | bytes 1966088 | tf_op jit(solution)/shard_map/ppermute | solution.py:38
  84.0 12.1 %collective-permute-start.14 = (bf16[1280,256]{1,0:T(8,128)(2,1)S(1)}, bf16[1280,256]{1,0:T(8,128)(2,1)S(1)}, u32[]{:S(2)}, u32[]{:S(2)}) collective-permute-start(bf16[1280,256]{1,0:T(8,128)(2,1)S(1)} %get-tuple-element.55.refs_1_), channel_id=1, source_target_pairs={{0,8},{1,9},{2,10},{3,11},{4,12},{5,13},{6,14},{7,15},{8,16},{9,17... | collective-permute-start | bytes 1966088 | tf_op jit(solution)/shard_map/ppermute | solution.py:38
  84.0 12.1 %collective-permute-start.15 = (bf16[1280,256]{1,0:T(8,128)(2,1)S(1)}, bf16[1280,256]{1,0:T(8,128)(2,1)S(1)}, u32[]{:S(2)}, u32[]{:S(2)}) collective-permute-start(bf16[1280,256]{1,0:T(8,128)(2,1)S(1)} %get-tuple-element.55.refs_1_), channel_id=1, source_target_pairs={{0,24},{1,25},{2,26},{3,27},{4,28},{5,29},{6,30},{7,31},{8,0},{9,1... | collective-permute-start | bytes 1966088 | tf_op jit(solution)/shard_map/ppermute | solution.py:38
  97.2 10.0 %collective-permute-start.16 = (bf16[1152,256]{1,0:T(8,128)(2,1)S(1)}, bf16[1152,256]{1,0:T(8,128)(2,1)S(1)}, u32[]{:S(2)}, u32[]{:S(2)}) collective-permute-start(bf16[1152,256]{1,0:T(8,128)(2,1)S(1)} %pad_maximum_fusion.4), channel_id=1, source_target_pairs={{0,1},{1,2},{2,3},{3,4},{4,5},{5,6},{6,7},{7,0},{8,9},{9,10},{10,1... | collective-permute-start | bytes 1769480 | tf_op jit(solution)/shard_map/ppermute | solution.py:38
  97.3 9.9 %collective-permute-start.17 = (bf16[1152,256]{1,0:T(8,128)(2,1)S(1)}, bf16[1152,256]{1,0:T(8,128)(2,1)S(1)}, u32[]{:S(2)}, u32[]{:S(2)}) collective-permute-start(bf16[1152,256]{1,0:T(8,128)(2,1)S(1)} %concatenate.91), channel_id=1, source_target_pairs={{0,7},{1,0},{2,1},{3,2},{4,3},{5,4},{6,5},{7,6},{8,15},{9,8},{10,9... | collective-permute-start | bytes 1769480 | tf_op jit(solution)/shard_map/ppermute | solution.py:38
  99.9 10.2 %collective-permute-start.18 = (bf16[1152,256]{1,0:T(8,128)(2,1)S(1)}, bf16[1152,256]{1,0:T(8,128)(2,1)S(1)}, u32[]{:S(2)}, u32[]{:S(2)}) collective-permute-start(bf16[1152,256]{1,0:T(8,128)(2,1)S(1)} %get-tuple-element.62), channel_id=1, source_target_pairs={{0,8},{1,9},{2,10},{3,11},{4,12},{5,13},{6,14},{7,15},{8,16},{9,17... | collective-permute-start | bytes 1769480 | tf_op jit(solution)/shard_map/ppermute | solution.py:38
  99.9 10.2 %collective-permute-start.19 = (bf16[1152,256]{1,0:T(8,128)(2,1)S(1)}, bf16[1152,256]{1,0:T(8,128)(2,1)S(1)}, u32[]{:S(2)}, u32[]{:S(2)}) collective-permute-start(bf16[1152,256]{1,0:T(8,128)(2,1)S(1)} %get-tuple-element.63), channel_id=1, source_target_pairs={{0,24},{1,25},{2,26},{3,27},{4,28},{5,29},{6,30},{7,31},{8,0},{9,1... | collective-permute-start | bytes 1769480 | tf_op jit(solution)/shard_map/ppermute | solution.py:38
  112.9 12.3 %collective-permute-start.22 = (bf16[512,256]{1,0:T(8,128)(2,1)}, bf16[512,256]{1,0:T(8,128)(2,1)S(1)}, u32[]{:S(2)}, u32[]{:S(2)}) collective-permute-start(bf16[512,256]{1,0:T(8,128)(2,1)} %get-tuple-element.70), channel_id=1, source_target_pairs={{0,8},{1,9},{2,10},{3,11},{4,12},{5,13},{6,14},{7,15},{8,16},{9,17... | collective-permute-start | bytes 786440 | tf_op jit(solution)/shard_map/ppermute | solution.py:38
  113.5 17.7 %collective-permute-start.20 = (bf16[1024,256]{1,0:T(8,128)(2,1)}, bf16[1024,256]{1,0:T(8,128)(2,1)S(1)}, u32[]{:S(2)}, u32[]{:S(2)}) collective-permute-start(bf16[1024,256]{1,0:T(8,128)(2,1)} %slice.114), channel_id=1, source_target_pairs={{0,1},{1,2},{2,3},{3,4},{4,5},{5,6},{6,7},{7,0},{8,9},{9,10},{10,1... | collective-permute-start | bytes 1572872 | tf_op jit(solution)/shard_map/ppermute | solution.py:38
  113.5 17.6 %collective-permute-start.21 = (bf16[1024,256]{1,0:T(8,128)(2,1)}, bf16[1024,256]{1,0:T(8,128)(2,1)S(1)}, u32[]{:S(2)}, u32[]{:S(2)}) collective-permute-start(bf16[1024,256]{1,0:T(8,128)(2,1)} %slice.115), channel_id=1, source_target_pairs={{0,7},{1,0},{2,1},{3,2},{4,3},{5,4},{6,5},{7,6},{8,15},{9,8},{10,9... | collective-permute-start | bytes 1572872 | tf_op jit(solution)/shard_map/ppermute | solution.py:38
  116.2 74.4 %collective-permute-start = (bf16[4096,256]{1,0:T(8,128)(2,1)}, bf16[4096,256]{1,0:T(8,128)(2,1)}, u32[]{:S(2)}, u32[]{:S(2)}) collective-permute-start(bf16[4096,256]{1,0:T(8,128)(2,1)} %bitcast.42), channel_id=1, source_target_pairs={{0,32},{32,0},{64,96},{96,64},{128,160},{160,128},{192,224},{224,1... | collective-permute-start | bytes 6291464 | tf_op jit(solution)/shard_map/ppermute | solution.py:42
  125.1 6.0 %collective-permute-start.23 = (bf16[512,256]{1,0:T(8,128)(2,1)}, bf16[512,256]{1,0:T(8,128)(2,1)S(1)}, u32[]{:S(2)}, u32[]{:S(2)}) collective-permute-start(bf16[512,256]{1,0:T(8,128)(2,1)} %get-tuple-element.71), channel_id=1, source_target_pairs={{0,24},{1,25},{2,26},{3,27},{4,28},{5,29},{6,30},{7,31},{8,0},{9,1... | collective-permute-start | bytes 786440 | tf_op jit(solution)/shard_map/ppermute | solution.py:38
  131.2 27.2 %collective-permute-start.24 = (bf16[512,256]{1,0:T(8,128)(2,1)S(1)}, bf16[512,256]{1,0:T(8,128)(2,1)S(1)}, u32[]{:S(2)}, u32[]{:S(2)}) collective-permute-start(bf16[512,256]{1,0:T(8,128)(2,1)S(1)} %slice.120), channel_id=1, source_target_pairs={{0,1},{1,2},{2,3},{3,4},{4,5},{5,6},{6,7},{7,0},{8,9},{9,10},{10,1... | collective-permute-start | bytes 786440 | tf_op jit(solution)/shard_map/ppermute | solution.py:38
  131.3 27.2 %collective-permute-start.25 = (bf16[512,256]{1,0:T(8,128)(2,1)S(1)}, bf16[512,256]{1,0:T(8,128)(2,1)S(1)}, u32[]{:S(2)}, u32[]{:S(2)}) collective-permute-start(bf16[512,256]{1,0:T(8,128)(2,1)S(1)} %slice.121), channel_id=1, source_target_pairs={{0,7},{1,0},{2,1},{3,2},{4,3},{5,4},{6,5},{7,6},{8,15},{9,8},{10,9... | collective-permute-start | bytes 786440 | tf_op jit(solution)/shard_map/ppermute | solution.py:38
  134.0 6.1 %collective-permute-start.26 = (bf16[128,256]{1,0:T(8,128)(2,1)S(1)}, bf16[128,256]{1,0:T(8,128)(2,1)S(1)}, u32[]{:S(2)}, u32[]{:S(2)}) collective-permute-start(bf16[128,256]{1,0:T(8,128)(2,1)S(1)} %slice.122), channel_id=1, source_target_pairs={{0,8},{1,9},{2,10},{3,11},{4,12},{5,13},{6,14},{7,15},{8,16},{9,17... | collective-permute-start | bytes 196616 | tf_op jit(solution)/shard_map/ppermute | solution.py:38
  137.3 32.2 %collective-permute-start.1 = (f32[2,32,256]{2,1,0:T(8,128)}, f32[2,32,256]{2,1,0:T(8,128)S(1)}, u32[]{:S(2)}, u32[]{:S(2)}) collective-permute-start(f32[2,32,256]{2,1,0:T(8,128)} %pad_maximum_fusion.8), channel_id=1, source_target_pairs={{0,32},{32,0},{64,96},{96,64},{128,160},{160,128},{192,224},{224,1... | collective-permute-start | bytes 196616 | tf_op jit(solution)/shard_map/ppermute | solution.py:42
  140.1 18.3 %collective-permute-start.27 = (bf16[128,256]{1,0:T(8,128)(2,1)S(1)}, bf16[128,256]{1,0:T(8,128)(2,1)S(1)}, u32[]{:S(2)}, u32[]{:S(2)}) collective-permute-start(bf16[128,256]{1,0:T(8,128)(2,1)S(1)} %slice.123), channel_id=1, source_target_pairs={{0,24},{1,25},{2,26},{3,27},{4,28},{5,29},{6,30},{7,31},{8,0},{9,1... | collective-permute-start | bytes 196616 | tf_op jit(solution)/shard_map/ppermute | solution.py:38
  165.2 9.9 %all-to-all-start.2 = ((f32[4,64,256]{2,1,0:T(8,128)}), f32[4,64,256]{2,1,0:T(8,128)S(1)}, u32[]{:S(2)}, u32[]{:S(2)}) async-start(f32[4,64,256]{2,1,0:T(8,128)} %bitcast.5), calls=%async_computation.2 | async-start | bytes 524288 | tf_op jit(solution)/shard_map/all_to_all | solution.py:224
  175.8 8.4 %all-to-all-start.3 = ((bf16[4,64,256]{2,1,0:T(8,128)(2,1)}), bf16[4,64,256]{2,1,0:T(8,128)(2,1)S(1)}, u32[]{:S(2)}, u32[]{:S(2)}) async-start(bf16[4,64,256]{2,1,0:T(8,128)(2,1)} %broadcast_in_dim.29), calls=%async_computation.3 | async-start | bytes 262144 | tf_op jit(solution)/shard_map/all_to_all | solution.py:48
  179.2 10.8 %collective-permute-start.29 = (f32[2,32,256]{2,1,0:T(8,128)S(1)}, f32[2,32,256]{2,1,0:T(8,128)S(1)}, u32[]{:S(2)}, u32[]{:S(2)}) collective-permute-start(f32[2,32,256]{2,1,0:T(8,128)S(1)} %pad_maximum_fusion.9), channel_id=1, source_target_pairs={{0,32},{32,0},{64,96},{96,64},{128,160},{160,128},{192,224},{224,1... | collective-permute-start | bytes 196616 | tf_op jit(solution)/shard_map/ppermute | solution.py:42
  184.1 6.8 %collective-permute-start.28 = (bf16[256,256]{1,0:T(8,128)(2,1)S(1)}, bf16[256,256]{1,0:T(8,128)(2,1)S(1)}, u32[]{:S(2)}, u32[]{:S(2)}) collective-permute-start(bf16[256,256]{1,0:T(8,128)(2,1)S(1)} %bitcast.46), channel_id=1, source_target_pairs={{0,32},{32,0},{64,96},{96,64},{128,160},{160,128},{192,224},{224,1... | collective-permute-start | bytes 393224 | tf_op jit(solution)/shard_map/ppermute | solution.py:42
  (25 other events, 338.9 us)

commit v2 on v0

v2 whole, which is shorter than its diff:
```python
import functools

import jax
import jax.numpy as jnp
from jax import lax
from jax.experimental import pallas as pl
from jax.experimental.pallas import tpu as pltpu
from jax.sharding import PartitionSpec as P

beta_one = 0.9
beta_two = 0.999
correct_one = 1.0 - 0.9**10
correct_two = 1.0 - 0.999**10
adam_eps = 1e-08

NX, NZ, NY = 4, 8, 4
TOK = 256
SEG = 128
PART = TOK // SEG
R = 256

GROUPS_Z = [[x * NZ + z for z in range(NZ)] for x in range(NX)]
GROUPS_X = [[x * NZ + z for x in range(NX)] for z in range(NZ)]

bar = lax.optimization_barrier


def adam_moments(low, first, second):
    new_first = beta_one * first + (1.0 - beta_one) * low
    new_second = beta_two * second + (1.0 - beta_two) * low * low
    direction = new_first / correct_one / (jnp.sqrt(new_second / correct_two) + adam_eps)
    return (new_first, new_second, direction.astype(jnp.bfloat16))


def shift(a, dx, dz):
    perm = [
        (x * NZ + z, (x + dx) % NX * NZ + (z + dz) % NZ) for x in range(NX) for z in range(NZ)
    ]
    return lax.ppermute(a, "mp", perm)


def other_core(a):
    return lax.ppermute(a, "dp", [(d, d ^ 1) for d in range(2 * NY)])


def gather_direct(a, axis, groups=None):
    n = len(groups[0]) if groups else lax.axis_size(axis)
    many = jnp.broadcast_to(a[None], (n, *a.shape))
    got = lax.all_to_all(many, axis, 0, 0, axis_index_groups=groups, tiled=True)
    return got.reshape(n * a.shape[0], *a.shape[1:])


class Piece:
    def __init__(self, array, segments):
        self.array, self.segments = array, segments

    def moved(self, dx, dz):
        return Piece(
            shift(self.array, dx, dz), [(p, x + dx, z + dz, k) for p, x, z, k in self.segments]
        )

    def cut(self, start, count):
        return Piece(self.array[start : start + count], self.segments[start : start + count])

    def halves(self):
        half = len(self.segments) // 2
        return self.cut(0, half), self.cut(half, half)


def stack(pieces):
    return Piece(
        jnp.concatenate([p.array for p in pieces], 0), [s for p in pieces for s in p.segments]
    )


def together(*pieces):
    arrays = bar(tuple(p.array for p in pieces))
    return [Piece(a, p.segments) for a, p in zip(arrays, pieces)]


def with_low(pieces, low):
    *arrays, low = bar((*[p.array for p in pieces], low))
    return [Piece(a, p.segments) for a, p in zip(arrays, pieces)], low


def gather_low(proj_in, proj_out, add):
    n = PART
    a, b = (Piece(array, [(part, 0, 0, k) for k in range(n)]) for part, array in enumerate((proj_in, proj_out)))
    zp, zm, xp, xm = together(b.moved(0, 1), b.moved(0, -1), a.moved(1, 0), a.moved(-1, 0))
    zp2, zm2, x2a, x2b = together(
        zp.moved(0, 1), zm.moved(0, -1), xp.halves()[0].moved(1, 0), xm.halves()[1].moved(-1, 0)
    )
    four = [a, xp, xm, x2a, x2b]
    up, down, side = together(
        stack([zp2, *four]), stack([zm2, *four]), stack([b, zp, zm, zp2, zm2])
    )
    sent = [Piece(up.array, [None] * n + up.segments[n:]), side]
    up, down, xp5, xm5 = together(
        up.moved(0, 1), down.moved(0, -1), side.moved(1, 0), side.moved(-1, 0)
    )
    low = add(sent, None)
    zp3, fp = up.cut(0, n), up.cut(n, 4 * n)
    zm3, fm = down.cut(0, n), down.cut(n, 4 * n)
    s, low = with_low(
        [
            stack([zp3.halves()[0], fp]),
            stack([zm3.halves()[1], fm]),
            stack([xp5.halves()[0], zp3, zm3]),
            stack([xm5.halves()[1], zp3, zm3]),
        ],
        low,
    )
    u4, d4, p4, m4 = together(
        s[0].moved(0, 1), s[1].moved(0, -1), s[2].moved(1, 0), s[3].moved(-1, 0)
    )
    low = add([up, down, xp5, xm5], low)
    h = n // 2
    u4a, d4a = u4.cut(0, h), d4.cut(0, h)
    y3p, y3m = p4.cut(5 * h, 2 * n), m4.cut(5 * h, 2 * n)
    s, low = with_low(
        [
            u4.cut(h, 4 * n),
            d4.cut(h, 4 * n),
            stack([u4a, d4a, y3p.halves()[0]]),
            stack([u4a, d4a, y3m.halves()[1]]),
        ],
        low,
    )
    u5, d5, p5, m5 = together(
        s[0].moved(0, 1), s[1].moved(0, -1), s[2].moved(1, 0), s[3].moved(-1, 0)
    )
    low = add([u4, d4, p4, m4], low)
    s, low = with_low([u5.halves()[0], d5.halves()[1], p5.cut(0, h), m5.cut(h, h)], low)
    last = together(s[0].moved(0, 1), s[1].moved(0, -1), s[2].moved(1, 0), s[3].moved(-1, 0))
    low = add([u5, d5, p5, m5], low)
    return add(last, low)


def low_kernel(count, runs, has_start, table, grad_in, acts_out, *refs):
    pieces, (out_ref, held, arrived) = refs[:count], refs[-3:]
    copies, at = [], 0
    for index, (_, _, part, first, segments) in enumerate(runs):
        row = pl.multiple_of(table[index] * TOK + first * SEG, SEG)
        rows = segments * SEG
        copies.append(
            pltpu.make_async_copy(
                (grad_in, acts_out)[part].at[pl.ds(row, rows)],
                held.at[pl.ds(at, rows)],
                arrived.at[index],
            )
        )
        copies[-1].start()
        at += rows
    totals = [refs[count][:, part].reshape(R, 256) if has_start else None for part in (0, 1)]
    at, index = 0, 0
    while index < len(runs):
        left, (piece, _, part, _, _), rows = [], runs[index], 0
        while index < len(runs) and (runs[index][0], runs[index][2]) == (piece, part):
            _, offset, _, _, segments = runs[index]
            copies[index].wait()
            left += [pieces[piece][offset + k] for k in range(segments)]
            rows += segments * SEG
            index += 1
        left = jnp.concatenate(left, 1) if len(left) > 1 else left[0]
        product = jnp.dot(left, held[pl.ds(at, rows)], preferred_element_type=jnp.float32)
        totals[part] = product if totals[part] is None else totals[part] + product
        at += rows
    for part in (0, 1):
        out_ref[:, part] = totals[part].reshape(out_ref.shape[0], -1, 256)


def low_of(grads, pieces, start):
    x, z = lax.axis_index("mp") // NZ, lax.axis_index("mp") % NZ
    runs, dxs, dzs = [], [], []
    for index, piece in enumerate(pieces):
        for offset, segment in enumerate(piece.segments):
            if segment is None:
                continue
            part, dx, dz, k = segment
            joins = (
                runs
                and runs[-1][0] == index
                and runs[-1][2] == part
                and (dxs[-1], dzs[-1]) == (dx, dz)
                and runs[-1][3] + runs[-1][4] == k
            )
            if joins:
                runs[-1] = (*runs[-1][:4], runs[-1][4] + 1)
            else:
                runs.append((index, offset, part, k, 1))
                dxs.append(dx)
                dzs.append(dz)
    rows = SEG * sum(run[4] for run in runs)
    blocks = (x - jnp.array(dxs, jnp.int32) + NX) % NX * NZ + (
        z - jnp.array(dzs, jnp.int32) + NZ
    ) % NZ
    vmem = pl.BlockSpec(memory_space=pltpu.VMEM)
    starts = [] if start is None else [start]
    return pl.pallas_call(
        functools.partial(low_kernel, len(pieces), runs, bool(starts)),
        out_shape=jax.ShapeDtypeStruct((2 * NY, 2, R // NY // 2, 256), jnp.float32),
        in_specs=[pl.BlockSpec(memory_space=pltpu.SMEM)]
        + [pl.BlockSpec(memory_space=pltpu.HBM)] * 2
        + [vmem] * (len(pieces) + len(starts)),
        out_specs=vmem,
        scratch_shapes=[
            pltpu.VMEM((rows, 256), jnp.bfloat16),
            pltpu.SemaphoreType.DMA((len(runs),)),
        ],
        compiler_params=pltpu.CompilerParams(vmem_limit_bytes=16 << 20),
        cost_estimate=pl.CostEstimate(
            flops=2 * rows * R * 256, bytes_accessed=rows * 1024, transcendentals=0
        ),
    )(blocks, *grads, *[p.array for p in pieces], *starts)


def project_kernel(core, acts_in, grad_out, basis_own, basis_other, *outs):
    def run(bases):
        for left, basis, out in zip((acts_in, grad_out), bases, outs):
            proj = jnp.dot(left[...], basis[...], preferred_element_type=jnp.float32)
            proj = proj.T.astype(jnp.bfloat16)
            for j in range(PART):
                out[j] = proj[:, j * SEG : (j + 1) * SEG]

    @pl.when(core[0] == 0)
    def _():
        run((basis_own, basis_other))

    @pl.when(core[0] == 1)
    def _():
        run((basis_other, basis_own))


def project(core, acts_in, grad_out, basis_own, basis_other):
    vmem = pl.BlockSpec(memory_space=pltpu.VMEM)
    return pl.pallas_call(
        project_kernel,
        out_shape=[jax.ShapeDtypeStruct((PART, R, SEG), jnp.bfloat16)] * 2,
        in_specs=[pl.BlockSpec(memory_space=pltpu.SMEM)] + [vmem] * 4,
        out_specs=[vmem] * 2,
        compiler_params=pltpu.CompilerParams(vmem_limit_bytes=16 << 20),
        cost_estimate=pl.CostEstimate(
            flops=4 * TOK * acts_in.shape[1] * R, bytes_accessed=8 << 20, transcendentals=0
        ),
    )(core[None], acts_in, grad_out, basis_own, basis_other)


def body(
    acts_in,
    grad_in,
    acts_out,
    grad_out,
    basis_in,
    basis_out,
    first_in,
    second_in,
    first_out,
    second_out,
):
    core = lax.axis_index("dp") % 2

    def mine(a, b):
        return jnp.where(core == 0, a, b)

    along_z = gather_direct(mine(basis_in, basis_out), "mp", GROUPS_Z)
    basis_own = gather_direct(along_z, "mp", GROUPS_X)
    basis_other = other_core(basis_own)
    low = gather_low(
        *project(core, acts_in, grad_out, basis_own, basis_other),
        functools.partial(low_of, (grad_in, acts_out)),
    )
    shares = lax.all_to_all(low, "dp", 0, 0, tiled=True)
    share = functools.reduce(jnp.add, [shares[d] for d in range(shares.shape[0])])
    new_first_in, new_second_in, step_in = adam_moments(share[0], first_in, second_in)
    new_first_out, new_second_out, step_out = adam_moments(share[1], first_out, second_out)
    steps = gather_direct(jnp.stack([step_in, step_out])[None], "dp")
    delta_in = jnp.dot(
        mine(basis_own, basis_other),
        steps[:, 0].reshape(R, 256),
        preferred_element_type=jnp.float32,
    )
    delta_out = lax.dot_general(
        steps[:, 1].reshape(R, 256),
        mine(basis_other, basis_own),
        (((0,), (1,)), ((), ())),
        preferred_element_type=jnp.float32,
    )
    return (
        delta_in.astype(jnp.bfloat16),
        delta_out.astype(jnp.bfloat16),
        new_first_in,
        new_second_in,
        new_first_out,
        new_second_out,
    )


def solution(mesh):
    in_specs = (
        P(("dp", "mp"), None),
        P("dp", "mp"),
        P("dp", "mp"),
        P(("dp", "mp"), None),
        P("mp", None),
        P("mp", None),
        P("dp", "mp"),
        P("dp", "mp"),
        P("dp", "mp"),
        P("dp", "mp"),
    )
    out_specs = (
        P(None, "mp"),
        P("mp", None),
        P("dp", "mp"),
        P("dp", "mp"),
        P("dp", "mp"),
        P("dp", "mp"),
    )
    return jax.shard_map(body, mesh=mesh, in_specs=in_specs, out_specs=out_specs, check_vma=False)
```

time: 436 us -> 178 us (0.41)
  waiting for transfers between devices: 358 us -> 10.1 us
  blocking collectives: 31.1 us -> 85.5 us
  starting transfers between devices: 0.24 us -> 35.3 us
  Pallas kernels: 0 us -> 25.2 us
  matrix products: 24.8 us -> 4.21 us
  between operations: 14.2 us -> 1.25 us
  local copies, waits for them, and re-layouts: 4.1 us -> 14.2 us
    all_gather x4 -> x0, waiting for transfers between devices: 311 us -> none  [the longest x1 79.8 us: body(): lax.all_gather(proj_out, 'mp', axis=0, tiled=True)]
    all_to_all x0 -> x4, blocking collectives: none -> 85.5 us  [the longest x3 62.2 us: gather_direct(): got = lax.all_to_all(many, axis, 0, 0, axis_index_groups=groups, tiled=True)]
    reduce_scatter x2 -> x0, waiting for transfers between devices: 46.2 us -> none  [the longest x1 28.1 us: body(): lax.psum_scatter(low_out, 'dp', scatter_dimension=0, tiled=True)]
    ppermute x0 -> x25, starting transfers between devices: none -> 35.3 us  [the longest x24 31.4 us: shift(): return lax.ppermute(a, 'mp', perm)]
    all_gather x2 -> x0, blocking collectives: 31.1 us -> none  [the longest x1 15.6 us: body(): lax.all_gather(step_in, 'dp', axis=0, tiled=True)]
    pallas_call x0 -> x6, Pallas kernels: none -> 25.2 us  [the longest x5 23.8 us: low_of(): pl.pallas_call(functools.partial(low_kernel, len(pieces), runs, bool(star...]
    dot_general x6 -> x2, matrix products: 24.8 us -> 4.21 us  [the longest x1 2.12 us: body(): lax.dot_general(steps[:, 1].reshape(R, 256), mine(basis_other, basis_own)...]
    ppermute x0 -> x25, waiting for transfers between devices: none -> 10.1 us  [the longest x24 6.3 us: shift(): return lax.ppermute(a, 'mp', perm)]
  transfers between devices with their start and end apart: 6 -> 25, of which waited for: 6 -> 7; matrix products, arithmetic and copies ran while one was open for 4% -> 1% of each run, Pallas kernels for 0% -> 12%
where the time goes in v2:
time: 178 us
  blocking collectives  85.5 us (48%)
  starting transfers between devices  35.3 us (20%)
  Pallas kernels  25.2 us (14%)
  local copies, waits for them, and re-layouts  14.2 us (8%)
  waiting for transfers between devices  10.1 us (6%)
  matrix products  4.21 us (2%)
  other arithmetic  1.84 us (1%)
    all_to_all x3, blocking collectives, gather_direct(): got = lax.all_to_all(many, axis, 0, 0, axis_index_groups=groups, tiled=True)  62.2 us
    ppermute x24, starting transfers between devices, shift(): return lax.ppermute(a, 'mp', perm)  31.4 us
    pallas_call x5, Pallas kernels, low_of(): pl.pallas_call(functools.partial(low_kernel, len(pieces), runs, bool(star...  23.8 us
    all_to_all x1, blocking collectives, body(): shares = lax.all_to_all(low, 'dp', 0, 0, tiled=True)  23.3 us
    unnamed x52, local copies, waits for them, and re-layouts  10.1 us
    ppermute x24, waiting for transfers between devices, shift(): return lax.ppermute(a, 'mp', perm)  6.3 us
    ppermute x1, starting transfers between devices, other_core(): return lax.ppermute(a, 'dp', [(d, d ^ 1) for d in range(2 * NY)])  3.95 us
    ppermute x1, waiting for transfers between devices, other_core(): return lax.ppermute(a, 'dp', [(d, d ^ 1) for d in range(2 * NY)])  3.79 us
  transfers between devices with their start and end apart: 25, of which 7 were waited for; matrix products, arithmetic and copies ran while one was open for 1% of the time, Pallas kernels for 12%

profile of v2, /device:TPU:1, one launch (start us, length us, event | category | flops | bytes accessed | tf_op | source)
XLA Modules:
  0.0 177.6 jit_solution(4068806203800381607)
XLA Ops:
  1.6 24.8 %all_to_all.20 = bf16[8,128,256]{2,1,0:T(8,128)(2,1)S(1)} all-to-all(bf16[8,128,256]{2,1,0:T(8,128)(2,1)S(1)} %broadcast_in_dim.10), channel_id=1, replica_groups={{0,1,2,3,4,5,6,7},{8,9,10,11,12,13,14,15},{16,17,18,19,20,21,22,23},{24..., dimensions={0} | all-to-all | bytes 1048576 | tf_op jit(solution)/shard_map/all_to_all | solution.py:49
  26.5 27.4 %all_to_all.21 = bf16[4,1024,256]{2,1,0:T(8,128)(2,1)S(1)} all-to-all(bf16[4,1024,256]{2,1,0:T(8,128)(2,1)S(1)} %broadcast_in_dim.23), channel_id=1, replica_groups={{0,8,16,24},{1,9,17,25},{2,10,18,26},{3,11,19,27},{4,12,20,28},{5,13,21..., dimensions={0} | all-to-all | bytes 4194304 | tf_op jit(solution)/shard_map/all_to_all | solution.py:49
  53.9 3.9 %collective-permute-start = (bf16[4096,256]{1,0:T(8,128)(2,1)S(1)}, bf16[4096,256]{1,0:T(8,128)(2,1)S(1)}, u32[]{:S(2)}, u32[]{:S(2)}) collective-permute-start(bf16[4096,256]{1,0:T(8,128)(2,1)S(1)} %bitcast.28), channel_id=1, source_target_pairs={{0,32},{32,0},{64,96},{96,64},{128,160},{160,128},{192,224},{224,1... | collective-permute-start | bytes 6291464 | tf_op jit(solution)/shard_map/ppermute | solution.py:43
  57.9 3.8 %collective-permute-done.basis_other = bf16[4096,256]{1,0:T(8,128)(2,1)S(1)} collective-permute-done((bf16[4096,256]{1,0:T(8,128)(2,1)S(1)}, bf16[4096,256]{1,0:T(8,128)(2,1)S(1)}, u32[]{:S(2)}, u32[]{:S(2)}) %collective-permute-start) | collective-permute-done | bytes 2097184 | tf_op jit(solution)/shard_map/ppermute | solution.py:43
  61.7 1.4 shard_map.235
  63.2 2.7 %collective-permute-start.2 = (bf16[2,256,128]{2,1,0:T(8,128)(2,1)S(1)}, bf16[2,256,128]{2,1,0:T(8,128)(2,1)S(1)}, u32[]{:S(2)}, u32[]{:S(2)}) collective-permute-start(bf16[2,256,128]{2,1,0:T(8,128)(2,1)S(1)} %get-tuple-element.50), channel_id=1, source_target_pairs={{0,7},{1,0},{2,1},{3,2},{4,3},{5,4},{6,5},{7,6},{8,15},{9,8},{10,9... | collective-permute-start | bytes 393224 | tf_op jit(solution)/shard_map/ppermute | solution.py:39
  66.1 2.4 %collective-permute-start.4 = (bf16[2,256,128]{2,1,0:T(8,128)(2,1)S(1)}, bf16[2,256,128]{2,1,0:T(8,128)(2,1)S(1)}, u32[]{:S(2)}, u32[]{:S(2)}) collective-permute-start(bf16[2,256,128]{2,1,0:T(8,128)(2,1)S(1)} %get-tuple-element.51), channel_id=1, source_target_pairs={{0,24},{1,25},{2,26},{3,27},{4,28},{5,29},{6,30},{7,31},{8,0},{9,1... | collective-permute-start | bytes 393224 | tf_op jit(solution)/shard_map/ppermute | solution.py:39
  69.2 1.7 collective-permute-done.3
  70.9 2.7 %collective-permute-start.6 = (bf16[2,256,128]{2,1,0:T(8,128)(2,1)S(1)}, bf16[2,256,128]{2,1,0:T(8,128)(2,1)S(1)}, u32[]{:S(2)}, u32[]{:S(2)}) collective-permute-start(bf16[2,256,128]{2,1,0:T(8,128)(2,1)S(1)} %collective-permute-done.2), channel_id=1, source_target_pairs={{0,7},{1,0},{2,1},{3,2},{4,3},{5,4},{6,5},{7,6},{8,15},{9,8},{10,9... | collective-permute-start | bytes 393224 | tf_op jit(solution)/shard_map/ppermute | solution.py:39
  73.6 2.8 %collective-permute-start.8 = (bf16[1,256,128]{2,1,0:T(8,128)(2,1)S(1)}, bf16[1,256,128]{2,1,0:T(8,128)(2,1)S(1)}, u32[]{:S(2)}, u32[]{:S(2)}) collective-permute-start(bf16[1,256,128]{2,1,0:T(8,128)(2,1)S(1)} %slice.100), channel_id=1, source_target_pairs={{0,24},{1,25},{2,26},{3,27},{4,28},{5,29},{6,30},{7,31},{8,0},{9,1... | collective-permute-start | bytes 196616 | tf_op jit(solution)/shard_map/ppermute | solution.py:39
  84.1 2.1 %collective-permute-start.12 = (bf16[10,256,128]{2,1,0:T(8,128)(2,1)}, bf16[10,256,128]{2,1,0:T(8,128)(2,1)}, u32[]{:S(2)}, u32[]{:S(2)}) collective-permute-start(bf16[10,256,128]{2,1,0:T(8,128)(2,1)} %get-tuple-element.62.refs_1_), channel_id=1, source_target_pairs={{0,24},{1,25},{2,26},{3,27},{4,28},{5,29},{6,30},{7,31},{8,0},{9,1... | collective-permute-start | bytes 1966088 | tf_op jit(solution)/shard_map/ppermute | solution.py:39
  86.3 1.2 collective-permute-start.9
  87.5 2.2 %copy-done = bf16[8192,256]{1,0:T(8,128)(2,1)S(1)} copy-done((bf16[8192,256]{1,0:T(8,128)(2,1)S(1)}, bf16[8192,256]{1,0:T(8,128)(2,1)}, u32[]{:S(2)}) %copy-start) | copy-done | bytes 4194328
  89.7 2.2 %copy-done.2 = bf16[8192,256]{1,0:T(8,128)(2,1)S(1)} copy-done((bf16[8192,256]{1,0:T(8,128)(2,1)S(1)}, bf16[8192,256]{1,0:T(8,128)(2,1)}, u32[]{:S(2)}) %copy-start.2) | copy-done | bytes 4194328
  91.8 4.1 %shard_map.236.refs_4_ = f32[8,2,32,256]{3,2,1,0:T(8,128)S(1)} custom-call(s32[10]{0:T(128)S(1)} %fusion.9.table, bf16[8192,256]{1,0:T(8,128)(2,1)S(1)} %copy-done, bf16[8192,256]{1,0:T(8,128)(2,1)S(1)} %copy-done.2, bf16[10,256,128]{2,1,0:T(8,128)(2,1)} %get-tuple-element.60.refs_0_, bf16[10,256,128]{2,1,0:T(8,128)(2,1)} %get-tuple-element.62.refs_1_), custom_call_target="tpu_custom_call" | custom-call | flops 301989888 | bytes 2359296 | tf_op jit(solution)/shard_map/pallas_call | solution.py:199
  96.2 1.3 collective-permute-done.11.refs_2_
  97.5 2.1 %collective-permute-done.9.refs_0_ = bf16[10,256,128]{2,1,0:T(8,128)(2,1)S(1)} collective-permute-done((bf16[10,256,128]{2,1,0:T(8,128)(2,1)}, bf16[10,256,128]{2,1,0:T(8,128)(2,1)S(1)}, u32[]{:S(2)}, u32[]{:S(2)}) %collective-permute-start.9) | collective-permute-done | bytes 655392 | tf_op jit(solution)/shard_map/ppermute | solution.py:39
  99.8 1.1 slice.103
  102.4 2.7 %collective-permute-start.14 = (bf16[9,256,128]{2,1,0:T(8,128)(2,1)S(1)}, bf16[9,256,128]{2,1,0:T(8,128)(2,1)S(1)}, u32[]{:S(2)}, u32[]{:S(2)}) collective-permute-start(bf16[9,256,128]{2,1,0:T(8,128)(2,1)S(1)} %concatenate.31), channel_id=1, source_target_pairs={{0,7},{1,0},{2,1},{3,2},{4,3},{5,4},{6,5},{7,6},{8,15},{9,8},{10,9... | collective-permute-start | bytes 1769480 | tf_op jit(solution)/shard_map/ppermute | solution.py:39
  105.1 2.7 %collective-permute-start.16 = (bf16[9,256,128]{2,1,0:T(8,128)(2,1)S(1)}, bf16[9,256,128]{2,1,0:T(8,128)(2,1)S(1)}, u32[]{:S(2)}, u32[]{:S(2)}) collective-permute-start(bf16[9,256,128]{2,1,0:T(8,128)(2,1)S(1)} %get-tuple-element.70), channel_id=1, source_target_pairs={{0,24},{1,25},{2,26},{3,27},{4,28},{5,29},{6,30},{7,31},{8,0},{9,1... | collective-permute-start | bytes 1769480 | tf_op jit(solution)/shard_map/ppermute | solution.py:39
  107.8 7.2 %shard_map.237.refs_4_ = f32[8,2,32,256]{3,2,1,0:T(8,128)S(1)} custom-call(s32[22]{0:T(128)S(1)} %get-tuple-element.123.table, bf16[8192,256]{1,0:T(8,128)(2,1)S(1)} %copy-done.1, bf16[8192,256]{1,0:T(8,128)(2,1)S(1)} %copy-done.3, bf16[10,256,128]{2,1,0:T(8,128)(2,1)S(1)} %collective-permute-done.9.refs_0_, ...), custom_call_target="tpu_custom_call" | custom-call | flops 671088640 | bytes 5242880 | tf_op jit(solution)/shard_map/pallas_call | solution.py:199
  115.7 2.7 %collective-permute-start.18 = (bf16[8,256,128]{2,1,0:T(8,128)(2,1)S(1)}, bf16[8,256,128]{2,1,0:T(8,128)(2,1)S(1)}, u32[]{:S(2)}, u32[]{:S(2)}) collective-permute-start(bf16[8,256,128]{2,1,0:T(8,128)(2,1)S(1)} %slice.108), channel_id=1, source_target_pairs={{0,7},{1,0},{2,1},{3,2},{4,3},{5,4},{6,5},{7,6},{8,15},{9,8},{10,9... | collective-permute-start | bytes 1572872 | tf_op jit(solution)/shard_map/ppermute | solution.py:39
  118.3 2.7 %collective-permute-start.20 = (bf16[4,256,128]{2,1,0:T(8,128)(2,1)S(1)}, bf16[4,256,128]{2,1,0:T(8,128)(2,1)S(1)}, u32[]{:S(2)}, u32[]{:S(2)}) collective-permute-start(bf16[4,256,128]{2,1,0:T(8,128)(2,1)S(1)} %get-tuple-element.79), channel_id=1, source_target_pairs={{0,24},{1,25},{2,26},{3,27},{4,28},{5,29},{6,30},{7,31},{8,0},{9,1... | collective-permute-start | bytes 786440 | tf_op jit(solution)/shard_map/ppermute | solution.py:39
  121.1 6.1 %shard_map.238.refs_4_ = f32[8,2,32,256]{3,2,1,0:T(8,128)S(1)} custom-call(s32[22]{0:T(128)S(1)} %get-tuple-element.124.table, bf16[8192,256]{1,0:T(8,128)(2,1)S(1)} %copy-done.1, bf16[8192,256]{1,0:T(8,128)(2,1)S(1)} %copy-done.3, bf16[9,256,128]{2,1,0:T(8,128)(2,1)S(1)} %collective-permute-done.13.refs_0_, ...), custom_call_target="tpu_custom_call" | custom-call | flops 603979776 | bytes 4718592 | tf_op jit(solution)/shard_map/pallas_call | solution.py:199
  127.4 2.7 %collective-permute-start.22 = (bf16[4,256,128]{2,1,0:T(8,128)(2,1)S(1)}, bf16[4,256,128]{2,1,0:T(8,128)(2,1)S(1)}, u32[]{:S(2)}, u32[]{:S(2)}) collective-permute-start(bf16[4,256,128]{2,1,0:T(8,128)(2,1)S(1)} %slice.114), channel_id=1, source_target_pairs={{0,7},{1,0},{2,1},{3,2},{4,3},{5,4},{6,5},{7,6},{8,15},{9,8},{10,9... | collective-permute-start | bytes 786440 | tf_op jit(solution)/shard_map/ppermute | solution.py:39
  130.0 2.7 %collective-permute-start.24 = (bf16[1,256,128]{2,1,0:T(8,128)(2,1)S(1)}, bf16[1,256,128]{2,1,0:T(8,128)(2,1)S(1)}, u32[]{:S(2)}, u32[]{:S(2)}) collective-permute-start(bf16[1,256,128]{2,1,0:T(8,128)(2,1)S(1)} %slice.116), channel_id=1, source_target_pairs={{0,24},{1,25},{2,26},{3,27},{4,28},{5,29},{6,30},{7,31},{8,0},{9,1... | collective-permute-start | bytes 196616 | tf_op jit(solution)/shard_map/ppermute | solution.py:39
  132.7 4.1 %shard_map.239.refs_4_ = f32[8,2,32,256]{3,2,1,0:T(8,128)S(1)} custom-call(s32[16]{0:T(128)S(1)} %fusion.12.table, bf16[8192,256]{1,0:T(8,128)(2,1)S(1)} %copy-done.1, bf16[8192,256]{1,0:T(8,128)(2,1)S(1)} %copy-done.3, bf16[8,256,128]{2,1,0:T(8,128)(2,1)S(1)} %collective-permute-done.17.refs_0_, bf16[8,256,128]{2,1,0:T(8,128)(2,1)S(1)} %collective-permute-done.18.refs_1_, ...), custom_call_target="tpu_custom_call" | custom-call | flops 402653184 | bytes 3145728 | tf_op jit(solution)/shard_map/pallas_call | solution.py:199
  137.0 2.3 %shard_map.240 = f32[8,2,32,256]{3,2,1,0:T(8,128)S(1)} custom-call(s32[7]{0:T(128)S(1)} %fusion.8.table, bf16[8192,256]{1,0:T(8,128)(2,1)S(1)} %copy-done.1, bf16[8192,256]{1,0:T(8,128)(2,1)S(1)} %copy-done.3, bf16[4,256,128]{2,1,0:T(8,128)(2,1)S(1)} %collective-permute-done.21.refs_0_, bf16[4,256,128]{2,1,0:T(8,128)(2,1)S(1)} %collective-permute-done.22.refs_1_, ...), custom_call_target="tpu_custom_call" | custom-call | flops 167772160 | bytes 1310720 | tf_op jit(solution)/shard_map/pallas_call | solution.py:199
  139.3 23.3 %all_to_all.22 = f32[8,2,32,256]{3,2,1,0:T(8,128)S(1)} all-to-all(f32[8,2,32,256]{3,2,1,0:T(8,128)S(1)} %shard_map.240), channel_id=1, replica_groups=mesh['dp'=8,'mp'=32] {'dp'}, dimensions={0} | all-to-all | bytes 1048576 | tf_op jit(solution)/shard_map/all_to_all | solution.py:272
  163.4 9.9 %all_to_all.23 = bf16[8,1,2,32,256]{4,3,2,1,0:T(8,128)(2,1)S(1)} all-to-all(bf16[8,1,2,32,256]{4,3,2,1,0:T(8,128)(2,1)S(1)} %broadcast_in_dim.25), channel_id=1, replica_groups=mesh['dp'=8,'mp'=32] {'dp'}, dimensions={0} | all-to-all | bytes 524288 | tf_op jit(solution)/shard_map/all_to_all | solution.py:49
  173.4 2.1 %convolution_convert_fusion = bf16[256,4096]{1,0:T(8,128)(2,1)} fusion(bf16[256,256]{1,0:T(8,128)(2,1)S(1)} %bitcast.35, bf16[4096,256]{1,0:T(8,128)(2,1)S(1)} %copy-done.5, bf16[4096,256]{1,0:T(8,128)(2,1)S(1)} %bitcast.30, pred[]{:T(512)S(6)} %eq.26), kind=kOutput, calls=%fused_computation | convolution fusion | flops 538968064 | bytes 6422529 | tf_op jit(solution)/shard_map/dot_general | solution.py:282
  175.5 2.1 %convolution_convert_fusion.1 = bf16[4096,256]{1,0:T(8,128)(2,1)} fusion(bf16[256,256]{1,0:T(8,128)(2,1)S(1)} %bitcast.34, bf16[4096,256]{1,0:T(8,128)(2,1)S(1)} %bitcast.31, bf16[4096,256]{1,0:T(8,128)(2,1)S(1)} %copy-done.5, pred[]{:T(512)S(6)} %eq.26), kind=kOutput, calls=%fused_computation.1 | convolution fusion | flops 538968064 | bytes 6422529 | tf_op jit(solution)/shard_map/dot_general | solution.py:277
  (117 shorter events, 13.4 us)
Async XLA Ops:
  26.5 35.2 %copy-start.6 = (bf16[256,4096]{1,0:T(8,128)(2,1)S(1)}, bf16[256,4096]{1,0:T(8,128)(2,1)}, u32[]{:S(2)}) copy-start(bf16[256,4096]{1,0:T(8,128)(2,1)} %acts_in.1) | copy-start | bytes 6291460
  26.5 35.2 %copy-start.7 = (bf16[256,4096]{1,0:T(8,128)(2,1)S(1)}, bf16[256,4096]{1,0:T(8,128)(2,1)}, u32[]{:S(2)}) copy-start(bf16[256,4096]{1,0:T(8,128)(2,1)} %grad_out.1) | copy-start | bytes 6291460
  53.9 7.7 %collective-permute-start = (bf16[4096,256]{1,0:T(8,128)(2,1)S(1)}, bf16[4096,256]{1,0:T(8,128)(2,1)S(1)}, u32[]{:S(2)}, u32[]{:S(2)}) collective-permute-start(bf16[4096,256]{1,0:T(8,128)(2,1)S(1)} %bitcast.28), channel_id=1, source_target_pairs={{0,32},{32,0},{64,96},{96,64},{128,160},{160,128},{192,224},{224,1... | collective-permute-start | bytes 6291464 | tf_op jit(solution)/shard_map/ppermute | solution.py:43
  63.1 6.1 %collective-permute-start.1 = (bf16[2,256,128]{2,1,0:T(8,128)(2,1)S(1)}, bf16[2,256,128]{2,1,0:T(8,128)(2,1)S(1)}, u32[]{:S(2)}, u32[]{:S(2)}) collective-permute-start(bf16[2,256,128]{2,1,0:T(8,128)(2,1)S(1)} %get-tuple-element.50), channel_id=1, source_target_pairs={{0,1},{1,2},{2,3},{3,4},{4,5},{5,6},{6,7},{7,0},{8,9},{9,10},{10,1... | collective-permute-start | bytes 393224 | tf_op jit(solution)/shard_map/ppermute | solution.py:39
  63.2 6.0 %collective-permute-start.2 = (bf16[2,256,128]{2,1,0:T(8,128)(2,1)S(1)}, bf16[2,256,128]{2,1,0:T(8,128)(2,1)S(1)}, u32[]{:S(2)}, u32[]{:S(2)}) collective-permute-start(bf16[2,256,128]{2,1,0:T(8,128)(2,1)S(1)} %get-tuple-element.50), channel_id=1, source_target_pairs={{0,7},{1,0},{2,1},{3,2},{4,3},{5,4},{6,5},{7,6},{8,15},{9,8},{10,9... | collective-permute-start | bytes 393224 | tf_op jit(solution)/shard_map/ppermute | solution.py:39
  65.9 5.0 %collective-permute-start.3 = (bf16[2,256,128]{2,1,0:T(8,128)(2,1)S(1)}, bf16[2,256,128]{2,1,0:T(8,128)(2,1)S(1)}, u32[]{:S(2)}, u32[]{:S(2)}) collective-permute-start(bf16[2,256,128]{2,1,0:T(8,128)(2,1)S(1)} %get-tuple-element.51), channel_id=1, source_target_pairs={{0,8},{1,9},{2,10},{3,11},{4,12},{5,13},{6,14},{7,15},{8,16},{9,17... | collective-permute-start | bytes 393224 | tf_op jit(solution)/shard_map/ppermute | solution.py:39
  66.1 4.7 %collective-permute-start.4 = (bf16[2,256,128]{2,1,0:T(8,128)(2,1)S(1)}, bf16[2,256,128]{2,1,0:T(8,128)(2,1)S(1)}, u32[]{:S(2)}, u32[]{:S(2)}) collective-permute-start(bf16[2,256,128]{2,1,0:T(8,128)(2,1)S(1)} %get-tuple-element.51), channel_id=1, source_target_pairs={{0,24},{1,25},{2,26},{3,27},{4,28},{5,29},{6,30},{7,31},{8,0},{9,1... | collective-permute-start | bytes 393224 | tf_op jit(solution)/shard_map/ppermute | solution.py:39
  70.9 7.3 %collective-permute-start.5 = (bf16[2,256,128]{2,1,0:T(8,128)(2,1)S(1)}, bf16[2,256,128]{2,1,0:T(8,128)(2,1)S(1)}, u32[]{:S(2)}, u32[]{:S(2)}) collective-permute-start(bf16[2,256,128]{2,1,0:T(8,128)(2,1)S(1)} %collective-permute-done.1), channel_id=1, source_target_pairs={{0,1},{1,2},{2,3},{3,4},{4,5},{5,6},{6,7},{7,0},{8,9},{9,10},{10,1... | collective-permute-start | bytes 393224 | tf_op jit(solution)/shard_map/ppermute | solution.py:39
  70.9 7.3 %collective-permute-start.6 = (bf16[2,256,128]{2,1,0:T(8,128)(2,1)S(1)}, bf16[2,256,128]{2,1,0:T(8,128)(2,1)S(1)}, u32[]{:S(2)}, u32[]{:S(2)}) collective-permute-start(bf16[2,256,128]{2,1,0:T(8,128)(2,1)S(1)} %collective-permute-done.2), channel_id=1, source_target_pairs={{0,7},{1,0},{2,1},{3,2},{4,3},{5,4},{6,5},{7,6},{8,15},{9,8},{10,9... | collective-permute-start | bytes 393224 | tf_op jit(solution)/shard_map/ppermute | solution.py:39
  73.6 4.6 %collective-permute-start.7 = (bf16[1,256,128]{2,1,0:T(8,128)(2,1)S(1)}, bf16[1,256,128]{2,1,0:T(8,128)(2,1)S(1)}, u32[]{:S(2)}, u32[]{:S(2)}) collective-permute-start(bf16[1,256,128]{2,1,0:T(8,128)(2,1)S(1)} %slice.99), channel_id=1, source_target_pairs={{0,8},{1,9},{2,10},{3,11},{4,12},{5,13},{6,14},{7,15},{8,16},{9,17... | collective-permute-start | bytes 196616 | tf_op jit(solution)/shard_map/ppermute | solution.py:39
  73.6 4.6 %collective-permute-start.8 = (bf16[1,256,128]{2,1,0:T(8,128)(2,1)S(1)}, bf16[1,256,128]{2,1,0:T(8,128)(2,1)S(1)}, u32[]{:S(2)}, u32[]{:S(2)}) collective-permute-start(bf16[1,256,128]{2,1,0:T(8,128)(2,1)S(1)} %slice.100), channel_id=1, source_target_pairs={{0,24},{1,25},{2,26},{3,27},{4,28},{5,29},{6,30},{7,31},{8,0},{9,1... | collective-permute-start | bytes 196616 | tf_op jit(solution)/shard_map/ppermute | solution.py:39
  83.2 13.0 %collective-permute-start.10 = (bf16[10,256,128]{2,1,0:T(8,128)(2,1)}, bf16[10,256,128]{2,1,0:T(8,128)(2,1)S(1)}, u32[]{:S(2)}, u32[]{:S(2)}) collective-permute-start(bf16[10,256,128]{2,1,0:T(8,128)(2,1)} %get-tuple-element.61), channel_id=1, source_target_pairs={{0,7},{1,0},{2,1},{3,2},{4,3},{5,4},{6,5},{7,6},{8,15},{9,8},{10,9... | collective-permute-start | bytes 1966088 | tf_op jit(solution)/shard_map/ppermute | solution.py:39
  83.6 13.9 %collective-permute-start.11 = (bf16[10,256,128]{2,1,0:T(8,128)(2,1)}, bf16[10,256,128]{2,1,0:T(8,128)(2,1)}, u32[]{:S(2)}, u32[]{:S(2)}) collective-permute-start(bf16[10,256,128]{2,1,0:T(8,128)(2,1)} %get-tuple-element.62.refs_1_), channel_id=1, source_target_pairs={{0,8},{1,9},{2,10},{3,11},{4,12},{5,13},{6,14},{7,15},{8,16},{9,17... | collective-permute-start | bytes 1966088 | tf_op jit(solution)/shard_map/ppermute | solution.py:39
  84.1 13.4 %collective-permute-start.12 = (bf16[10,256,128]{2,1,0:T(8,128)(2,1)}, bf16[10,256,128]{2,1,0:T(8,128)(2,1)}, u32[]{:S(2)}, u32[]{:S(2)}) collective-permute-start(bf16[10,256,128]{2,1,0:T(8,128)(2,1)} %get-tuple-element.62.refs_1_), channel_id=1, source_target_pairs={{0,24},{1,25},{2,26},{3,27},{4,28},{5,29},{6,30},{7,31},{8,0},{9,1... | collective-permute-start | bytes 1966088 | tf_op jit(solution)/shard_map/ppermute | solution.py:39
  86.3 13.4 %collective-permute-start.9 = (bf16[10,256,128]{2,1,0:T(8,128)(2,1)}, bf16[10,256,128]{2,1,0:T(8,128)(2,1)S(1)}, u32[]{:S(2)}, u32[]{:S(2)}) collective-permute-start(bf16[10,256,128]{2,1,0:T(8,128)(2,1)} %get-tuple-element.60.refs_0_), channel_id=1, source_target_pairs={{0,1},{1,2},{2,3},{3,4},{4,5},{5,6},{6,7},{7,0},{8,9},{9,10},{10,1... | collective-permute-start | bytes 1966088 | tf_op jit(solution)/shard_map/ppermute | solution.py:39
  102.3 12.7 %collective-permute-start.13 = (bf16[9,256,128]{2,1,0:T(8,128)(2,1)S(1)}, bf16[9,256,128]{2,1,0:T(8,128)(2,1)S(1)}, u32[]{:S(2)}, u32[]{:S(2)}) collective-permute-start(bf16[9,256,128]{2,1,0:T(8,128)(2,1)S(1)} %get-tuple-element.67), channel_id=1, source_target_pairs={{0,1},{1,2},{2,3},{3,4},{4,5},{5,6},{6,7},{7,0},{8,9},{9,10},{10,1... | collective-permute-start | bytes 1769480 | tf_op jit(solution)/shard_map/ppermute | solution.py:39
  102.4 12.6 %collective-permute-start.14 = (bf16[9,256,128]{2,1,0:T(8,128)(2,1)S(1)}, bf16[9,256,128]{2,1,0:T(8,128)(2,1)S(1)}, u32[]{:S(2)}, u32[]{:S(2)}) collective-permute-start(bf16[9,256,128]{2,1,0:T(8,128)(2,1)S(1)} %concatenate.31), channel_id=1, source_target_pairs={{0,7},{1,0},{2,1},{3,2},{4,3},{5,4},{6,5},{7,6},{8,15},{9,8},{10,9... | collective-permute-start | bytes 1769480 | tf_op jit(solution)/shard_map/ppermute | solution.py:39
  105.1 10.3 %collective-permute-start.15 = (bf16[9,256,128]{2,1,0:T(8,128)(2,1)S(1)}, bf16[9,256,128]{2,1,0:T(8,128)(2,1)S(1)}, u32[]{:S(2)}, u32[]{:S(2)}) collective-permute-start(bf16[9,256,128]{2,1,0:T(8,128)(2,1)S(1)} %get-tuple-element.69), channel_id=1, source_target_pairs={{0,8},{1,9},{2,10},{3,11},{4,12},{5,13},{6,14},{7,15},{8,16},{9,17... | collective-permute-start | bytes 1769480 | tf_op jit(solution)/shard_map/ppermute | solution.py:39
  105.1 10.3 %collective-permute-start.16 = (bf16[9,256,128]{2,1,0:T(8,128)(2,1)S(1)}, bf16[9,256,128]{2,1,0:T(8,128)(2,1)S(1)}, u32[]{:S(2)}, u32[]{:S(2)}) collective-permute-start(bf16[9,256,128]{2,1,0:T(8,128)(2,1)S(1)} %get-tuple-element.70), channel_id=1, source_target_pairs={{0,24},{1,25},{2,26},{3,27},{4,28},{5,29},{6,30},{7,31},{8,0},{9,1... | collective-permute-start | bytes 1769480 | tf_op jit(solution)/shard_map/ppermute | solution.py:39
  115.6 11.6 %collective-permute-start.17 = (bf16[8,256,128]{2,1,0:T(8,128)(2,1)S(1)}, bf16[8,256,128]{2,1,0:T(8,128)(2,1)S(1)}, u32[]{:S(2)}, u32[]{:S(2)}) collective-permute-start(bf16[8,256,128]{2,1,0:T(8,128)(2,1)S(1)} %slice.107), channel_id=1, source_target_pairs={{0,1},{1,2},{2,3},{3,4},{4,5},{5,6},{6,7},{7,0},{8,9},{9,10},{10,1... | collective-permute-start | bytes 1572872 | tf_op jit(solution)/shard_map/ppermute | solution.py:39
  115.7 11.5 %collective-permute-start.18 = (bf16[8,256,128]{2,1,0:T(8,128)(2,1)S(1)}, bf16[8,256,128]{2,1,0:T(8,128)(2,1)S(1)}, u32[]{:S(2)}, u32[]{:S(2)}) collective-permute-start(bf16[8,256,128]{2,1,0:T(8,128)(2,1)S(1)} %slice.108), channel_id=1, source_target_pairs={{0,7},{1,0},{2,1},{3,2},{4,3},{5,4},{6,5},{7,6},{8,15},{9,8},{10,9... | collective-permute-start | bytes 1572872 | tf_op jit(solution)/shard_map/ppermute | solution.py:39
  118.3 8.8 %collective-permute-start.19 = (bf16[4,256,128]{2,1,0:T(8,128)(2,1)S(1)}, bf16[4,256,128]{2,1,0:T(8,128)(2,1)S(1)}, u32[]{:S(2)}, u32[]{:S(2)}) collective-permute-start(bf16[4,256,128]{2,1,0:T(8,128)(2,1)S(1)} %get-tuple-element.78), channel_id=1, source_target_pairs={{0,8},{1,9},{2,10},{3,11},{4,12},{5,13},{6,14},{7,15},{8,16},{9,17... | collective-permute-start | bytes 786440 | tf_op jit(solution)/shard_map/ppermute | solution.py:39
  118.3 8.8 %collective-permute-start.20 = (bf16[4,256,128]{2,1,0:T(8,128)(2,1)S(1)}, bf16[4,256,128]{2,1,0:T(8,128)(2,1)S(1)}, u32[]{:S(2)}, u32[]{:S(2)}) collective-permute-start(bf16[4,256,128]{2,1,0:T(8,128)(2,1)S(1)} %get-tuple-element.79), channel_id=1, source_target_pairs={{0,24},{1,25},{2,26},{3,27},{4,28},{5,29},{6,30},{7,31},{8,0},{9,1... | collective-permute-start | bytes 786440 | tf_op jit(solution)/shard_map/ppermute | solution.py:39
  127.3 9.7 %collective-permute-start.21 = (bf16[4,256,128]{2,1,0:T(8,128)(2,1)S(1)}, bf16[4,256,128]{2,1,0:T(8,128)(2,1)S(1)}, u32[]{:S(2)}, u32[]{:S(2)}) collective-permute-start(bf16[4,256,128]{2,1,0:T(8,128)(2,1)S(1)} %slice.113), channel_id=1, source_target_pairs={{0,1},{1,2},{2,3},{3,4},{4,5},{5,6},{6,7},{7,0},{8,9},{9,10},{10,1... | collective-permute-start | bytes 786440 | tf_op jit(solution)/shard_map/ppermute | solution.py:39
  127.4 9.6 %collective-permute-start.22 = (bf16[4,256,128]{2,1,0:T(8,128)(2,1)S(1)}, bf16[4,256,128]{2,1,0:T(8,128)(2,1)S(1)}, u32[]{:S(2)}, u32[]{:S(2)}) collective-permute-start(bf16[4,256,128]{2,1,0:T(8,128)(2,1)S(1)} %slice.114), channel_id=1, source_target_pairs={{0,7},{1,0},{2,1},{3,2},{4,3},{5,4},{6,5},{7,6},{8,15},{9,8},{10,9... | collective-permute-start | bytes 786440 | tf_op jit(solution)/shard_map/ppermute | solution.py:39
  130.0 6.9 %collective-permute-start.23 = (bf16[1,256,128]{2,1,0:T(8,128)(2,1)S(1)}, bf16[1,256,128]{2,1,0:T(8,128)(2,1)S(1)}, u32[]{:S(2)}, u32[]{:S(2)}) collective-permute-start(bf16[1,256,128]{2,1,0:T(8,128)(2,1)S(1)} %slice.115), channel_id=1, source_target_pairs={{0,8},{1,9},{2,10},{3,11},{4,12},{5,13},{6,14},{7,15},{8,16},{9,17... | collective-permute-start | bytes 196616 | tf_op jit(solution)/shard_map/ppermute | solution.py:39
  130.0 6.9 %collective-permute-start.24 = (bf16[1,256,128]{2,1,0:T(8,128)(2,1)S(1)}, bf16[1,256,128]{2,1,0:T(8,128)(2,1)S(1)}, u32[]{:S(2)}, u32[]{:S(2)}) collective-permute-start(bf16[1,256,128]{2,1,0:T(8,128)(2,1)S(1)} %slice.116), channel_id=1, source_target_pairs={{0,24},{1,25},{2,26},{3,27},{4,28},{5,29},{6,30},{7,31},{8,0},{9,1... | collective-permute-start | bytes 196616 | tf_op jit(solution)/shard_map/ppermute | solution.py:39
  136.9 25.8 %copy-start.8 = (f32[32,256]{1,0:T(8,128)S(1)}, f32[32,256]{1,0:T(8,128)}, u32[]{:S(2)}) copy-start(f32[32,256]{1,0:T(8,128)} %param.26) | copy-start | bytes 98308
  136.9 25.8 %copy-start.9 = (f32[32,256]{1,0:T(8,128)S(1)}, f32[32,256]{1,0:T(8,128)}, u32[]{:S(2)}) copy-start(f32[32,256]{1,0:T(8,128)} %param.27) | copy-start | bytes 98308
  136.9 25.8 %copy-start.10 = (f32[32,256]{1,0:T(8,128)S(1)}, f32[32,256]{1,0:T(8,128)}, u32[]{:S(2)}) copy-start(f32[32,256]{1,0:T(8,128)} %param.29) | copy-start | bytes 98308
  136.9 25.8 %copy-start.11 = (f32[32,256]{1,0:T(8,128)S(1)}, f32[32,256]{1,0:T(8,128)}, u32[]{:S(2)}) copy-start(f32[32,256]{1,0:T(8,128)} %param.28) | copy-start | bytes 98308
  139.3 34.0 %copy-start.5 = (bf16[4096,256]{1,0:T(8,128)(2,1)S(1)}, bf16[4096,256]{1,0:T(8,128)(2,1)}, u32[]{:S(2)}) copy-start(bf16[4096,256]{1,0:T(8,128)(2,1)} %copy-done.4) | copy-start | bytes 6291460
  (15 other events, 141.0 us)

commit v3 on v2

v3 whole, which is shorter than its diff:
```python
import functools

import jax
import jax.numpy as jnp
from jax import lax
from jax.experimental import pallas as pl
from jax.experimental.pallas import tpu as pltpu
from jax.sharding import PartitionSpec as P

beta_one = 0.9
beta_two = 0.999
correct_one = 1.0 - 0.9**10
correct_two = 1.0 - 0.999**10
adam_eps = 1e-08

NX, NZ, NY = 4, 8, 4
TOK = 256
SEG = 128
PART = TOK // SEG
R = 256

GROUPS_Z = [[x * NZ + z for z in range(NZ)] for x in range(NX)]
GROUPS_Y = [[y * 2 + c for y in range(NY)] for c in range(2)]
GROUPS_X = [[x * NZ + z for x in range(NX)] for z in range(NZ)]

bar = lax.optimization_barrier


def adam_moments(low, first, second):
    new_first = beta_one * first + (1.0 - beta_one) * low
    new_second = beta_two * second + (1.0 - beta_two) * low * low
    direction = new_first / correct_one / (jnp.sqrt(new_second / correct_two) + adam_eps)
    return (new_first, new_second, direction.astype(jnp.bfloat16))


def shift(a, dx, dz):
    perm = [
        (x * NZ + z, (x + dx) % NX * NZ + (z + dz) % NZ) for x in range(NX) for z in range(NZ)
    ]
    return lax.ppermute(a, "mp", perm)


def other_core(a):
    return lax.ppermute(a, "dp", [(d, d ^ 1) for d in range(2 * NY)])


def gather_direct(a, axis, groups=None):
    n = len(groups[0]) if groups else lax.axis_size(axis)
    many = jnp.broadcast_to(a[None], (n, *a.shape))
    got = lax.all_to_all(many, axis, 0, 0, axis_index_groups=groups, tiled=True)
    return got.reshape(n * a.shape[0], *a.shape[1:])


class Piece:
    def __init__(self, array, segments):
        self.array, self.segments = array, segments

    def moved(self, dx, dz):
        return Piece(
            shift(self.array, dx, dz), [(p, x + dx, z + dz, k) for p, x, z, k in self.segments]
        )

    def cut(self, start, count):
        return Piece(self.array[start : start + count], self.segments[start : start + count])

    def halves(self):
        half = len(self.segments) // 2
        return self.cut(0, half), self.cut(half, half)


def pack_kernel(layout, *refs):
    count = 1 + max(source for packed in layout for source, _, _ in packed)
    for packed, out in zip(layout, refs[count:]):
        at = 0
        for source, start, segments in packed:
            out[at : at + segments] = refs[source][start : start + segments]
            at += segments


def pack(sources, layout):
    vmem = pl.BlockSpec(memory_space=pltpu.VMEM)
    sizes = [sum(run[2] for run in packed) for packed in layout]
    arrays = pl.pallas_call(
        functools.partial(pack_kernel, layout),
        out_shape=[jax.ShapeDtypeStruct((size, R, SEG), jnp.bfloat16) for size in sizes],
        in_specs=[vmem] * len(sources),
        out_specs=[vmem] * len(layout),
        compiler_params=pltpu.CompilerParams(vmem_limit_bytes=20 << 20),
    )(*[p.array for p in sources])
    return [
        Piece(array, [s for source, at, n in packed for s in sources[source].segments[at : at + n]])
        for array, packed in zip(arrays, layout)
    ]


def stack(pieces):
    return Piece(
        jnp.concatenate([p.array for p in pieces], 0), [s for p in pieces for s in p.segments]
    )


def together(*pieces):
    arrays = bar(tuple(p.array for p in pieces))
    return [Piece(a, p.segments) for a, p in zip(arrays, pieces)]


def with_low(pieces, low):
    *arrays, low = bar((*[p.array for p in pieces], low))
    return [Piece(a, p.segments) for a, p in zip(arrays, pieces)], low


def gather_low(proj_in, proj_out, add):
    n = PART
    a, b = (Piece(array, [(part, 0, 0, k) for k in range(n)]) for part, array in enumerate((proj_in, proj_out)))
    zp, zm, xp, xm = together(b.moved(0, 1), b.moved(0, -1), a.moved(1, 0), a.moved(-1, 0))
    zp2, zm2, x2a, x2b = together(
        zp.moved(0, 1), zm.moved(0, -1), xp.halves()[0].moved(1, 0), xm.halves()[1].moved(-1, 0)
    )
    h = n // 2
    four = [(0, 0, n), (1, 0, n), (2, 0, n), (3, 0, h), (4, 0, h)]
    up, down, side = pack(
        [a, xp, xm, x2a, x2b, b, zp, zm, zp2, zm2],
        [
            [(8, 0, n), *four],
            [(9, 0, n), *four],
            [(k, 0, n) for k in range(5, 10)],
        ],
    )
    sent = [Piece(up.array, [None] * n + up.segments[n:]), side]
    up, down, xp5, xm5 = together(
        up.moved(0, 1), down.moved(0, -1), side.moved(1, 0), side.moved(-1, 0)
    )
    low = add(sent, None)
    (up, down, xp5, xm5), low = with_low([up, down, xp5, xm5], low)
    s = pack(
        [up, down, xp5, xm5],
        [
            [(0, 0, h), (0, n, 4 * n)],
            [(1, h, h), (1, n, 4 * n)],
            [(2, 0, 5 * h), (0, 0, n), (1, 0, n)],
            [(3, 5 * h, 5 * h), (0, 0, n), (1, 0, n)],
        ],
    )
    u4, d4, p4, m4 = together(
        s[0].moved(0, 1), s[1].moved(0, -1), s[2].moved(1, 0), s[3].moved(-1, 0)
    )
    low = add([up, down, xp5, xm5], low)
    z4 = stack([u4.cut(0, h), d4.cut(0, h)])
    y3p, y3m = p4.cut(5 * h, 2 * n), m4.cut(5 * h, 2 * n)
    s, low = with_low(
        [
            u4.cut(h, 4 * n),
            d4.cut(h, 4 * n),
            stack([z4, y3p.halves()[0]]),
            stack([z4, y3m.halves()[1]]),
            z4,
        ],
        low,
    )
    u5, d5, p5, m5, q5 = together(
        s[0].moved(0, 1), s[1].moved(0, -1), s[2].moved(1, 0), s[3].moved(-1, 0), s[4].moved(2, 0)
    )
    low = add([u4, d4, p4, m4], low)
    s, low = with_low([u5.halves()[0], d5.halves()[1]], low)
    last = together(s[0].moved(0, 1), s[1].moved(0, -1))
    low = add([u5, d5, p5, m5, q5], low)
    return add(last, low, True)


def both_ways(core, run, own, other):
    @pl.when(core == 0)
    def _():
        run(own, other)

    @pl.when(core == 1)
    def _():
        run(other, own)


def low_kernel(count, runs, has_start, last, table, grad_in, acts_out, *refs):
    pieces, out_ref = refs[:count], refs[-2 if last else -1]
    totals = [refs[count][:, part].reshape(R, 256) if has_start else None for part in (0, 1)]
    for index, (piece, offset, part, first, segments) in enumerate(runs):
        left = [pieces[piece][offset + k] for k in range(segments)]
        left = jnp.concatenate(left, 1) if segments > 1 else left[0]
        row = pl.multiple_of(table[index] * TOK + first * SEG, SEG)
        right = (grad_in, acts_out)[part][pl.ds(row, segments * SEG)]
        product = jnp.dot(left, right, preferred_element_type=jnp.float32)
        totals[part] = product if totals[part] is None else totals[part] + product
    if not last:
        for part in (0, 1):
            out_ref[:, part] = totals[part].reshape(out_ref.shape[0], -1, 256)
        return

    def split(keep, give):
        for part in (0, 1):
            rows = totals[part].reshape(NY, 2, -1, 256)
            keep[:, part], give[:, part] = rows[:, 0], rows[:, 1]

    both_ways(table[len(runs)], split, refs[-2], refs[-1])


def low_of(grads, core, pieces, start, last=False):
    x, z = lax.axis_index("mp") // NZ, lax.axis_index("mp") % NZ
    runs, dxs, dzs = [], [], []
    for index, piece in enumerate(pieces):
        for offset, segment in enumerate(piece.segments):
            if segment is None:
                continue
            part, dx, dz, k = segment
            joins = (
                runs
                and runs[-1][0] == index
                and runs[-1][2] == part
                and (dxs[-1], dzs[-1]) == (dx, dz)
                and runs[-1][3] + runs[-1][4] == k
            )
            if joins:
                runs[-1] = (*runs[-1][:4], runs[-1][4] + 1)
            else:
                runs.append((index, offset, part, k, 1))
                dxs.append(dx)
                dzs.append(dz)
    rows = SEG * sum(run[4] for run in runs)
    blocks = (x - jnp.array(dxs, jnp.int32) + NX) % NX * NZ + (
        z - jnp.array(dzs, jnp.int32) + NZ
    ) % NZ
    vmem = pl.BlockSpec(memory_space=pltpu.VMEM)
    starts = [] if start is None else [start]
    return pl.pallas_call(
        functools.partial(low_kernel, len(pieces), runs, bool(starts), last),
        out_shape=[jax.ShapeDtypeStruct((NY, 2, R // NY // 2, 256), jnp.float32)] * 2
        if last
        else jax.ShapeDtypeStruct((2 * NY, 2, R // NY // 2, 256), jnp.float32),
        in_specs=[pl.BlockSpec(memory_space=pltpu.SMEM)]
        + [vmem] * (2 + len(pieces) + len(starts)),
        out_specs=[vmem] * 2 if last else vmem,
        compiler_params=pltpu.CompilerParams(vmem_limit_bytes=20 << 20),
        cost_estimate=pl.CostEstimate(
            flops=2 * rows * R * 256, bytes_accessed=rows * 1024, transcendentals=0
        ),
    )(jnp.append(blocks, core), *grads, *[p.array for p in pieces], *starts)


def spread_along_x(own):
    h = own.shape[0] // 2
    ahead, behind = shift(own, 1, 0), shift(own, -1, 0)
    own_other = other_core(own)
    ahead, behind, own_other = bar((ahead, behind, own_other))
    far = shift(ahead[:h], 1, 0), shift(behind[h:], -1, 0)
    near_other = other_core(ahead), other_core(behind)
    places = [(0, 0), (1, 0), (-1, 0), (2, 0), (2, h)]
    arrays = [own, ahead, behind, *far]
    others = [own_other, *near_other, *[other_core(f) for f in far]]
    return [(a, *p) for a, p in zip(arrays, places)], [(a, *p) for a, p in zip(others, places)]


def project_kernel(firsts, count, table, acts_in, grad_out, *refs):
    own, other, outs = refs[:count], refs[count : 2 * count], refs[2 * count : -2]
    held, arrived = refs[-2:]
    sizes = [part.shape[0] for part in own]
    copies = []
    for side, left in enumerate((acts_in, grad_out)):
        for k, size in enumerate(sizes):
            here = pl.multiple_of(table[1 + k] * (NZ * SEG) + firsts[k], SEG)
            copies.append(
                pltpu.make_async_copy(
                    left.at[:, pl.ds(here, size)],
                    held.at[side, :, pl.ds(sum(sizes[:k]), size)],
                    arrived.at[side, k],
                )
            )
            copies[-1].start()

    def run(*bases):
        for side, (parts, out) in enumerate(zip(bases, outs)):
            proj = None
            for k, part in enumerate(parts):
                copies[side * count + k].wait()
                at = sum(sizes[:k])
                product = jnp.dot(
                    held[side, :, at : at + sizes[k]], part[...], preferred_element_type=jnp.float32
                )
                proj = product if proj is None else proj + product
            proj = proj.T.astype(jnp.bfloat16)
            for j in range(PART):
                out[j] = proj[:, j * SEG : (j + 1) * SEG]

    both_ways(table[0], run, own, other)


def delta_kernel(firsts, count, table, steps, *refs):
    own, other = refs[:count], refs[count : 2 * count]
    delta_in, delta_out, held_in, held_out, left = refs[2 * count :]

    def run(parts_in, parts_out):
        copies = []

        def send(source, target, k):
            copies.append(pltpu.make_async_copy(source, target, left.at[len(copies)]))
            copies[-1].start()

        step = steps[:, 0].reshape(R, 256)
        for k, part in enumerate(parts_in):
            rows = part.shape[0]
            here = pl.ds(pl.multiple_of(table[1 + k] * (NZ * SEG) + firsts[k], SEG), rows)
            delta = jnp.dot(part[...], step, preferred_element_type=jnp.float32)
            held_in[here] = delta.astype(jnp.bfloat16)
            send(held_in.at[here], delta_in.at[here], k)
        step = steps[:, 1].reshape(R, 256).T
        for k, part in enumerate(parts_out):
            rows = part.shape[0]
            here = pl.ds(pl.multiple_of(table[1 + k] * (NZ * SEG) + firsts[k], SEG), rows)
            delta = lax.dot_general(
                step, part[...], (((1,), (1,)), ((), ())), preferred_element_type=jnp.float32
            )
            held_out[:, here] = delta.astype(jnp.bfloat16)
            send(held_out.at[:, here], delta_out.at[:, here], k)
        for copy in copies:
            copy.wait()

    both_ways(table[0], run, own, other)


def with_bases(kernel, out_shape, out_specs, scratch, flops, space, table, operands, own, other):
    vmem = pl.BlockSpec(memory_space=pltpu.VMEM)
    arrays = [a for a, _, _ in own + other]
    return pl.pallas_call(
        functools.partial(kernel, [first for _, _, first in own], len(own)),
        out_shape=out_shape,
        in_specs=[pl.BlockSpec(memory_space=pltpu.SMEM)]
        + [pl.BlockSpec(memory_space=space)] * len(operands)
        + [vmem] * len(arrays),
        out_specs=out_specs,
        scratch_shapes=scratch,
        compiler_params=pltpu.CompilerParams(vmem_limit_bytes=48 << 20),
        cost_estimate=pl.CostEstimate(flops=flops, bytes_accessed=8 << 20, transcendentals=0),
    )(table, *operands, *arrays)


def project(table, acts_in, grad_out, own, other):
    return with_bases(
        project_kernel,
        [jax.ShapeDtypeStruct((PART, R, SEG), jnp.bfloat16)] * 2,
        [pl.BlockSpec(memory_space=pltpu.VMEM)] * 2,
        [
            pltpu.VMEM((2, *acts_in.shape), jnp.bfloat16),
            pltpu.SemaphoreType.DMA((2, len(own))),
        ],
        4 * TOK * acts_in.shape[1] * R,
        pl.ANY,
        table,
        [acts_in, grad_out],
        own,
        other,
    )


def deltas(table, steps, own, other):
    width = NX * NZ * SEG
    shapes = [(width, 256), (256, width)]
    return with_bases(
        delta_kernel,
        [jax.ShapeDtypeStruct(shape, jnp.bfloat16) for shape in shapes],
        [pl.BlockSpec(memory_space=pl.ANY)] * 2,
        [pltpu.VMEM(shape, jnp.bfloat16) for shape in shapes]
        + [pltpu.SemaphoreType.DMA((2 * len(own),))],
        4 * 256 * width * R,
        pltpu.VMEM,
        table,
        [steps],
        own,
        other,
    )


def body(
    acts_in,
    grad_in,
    acts_out,
    grad_out,
    basis_in,
    basis_out,
    first_in,
    second_in,
    first_out,
    second_out,
):
    core = lax.axis_index("dp") % 2

    def mine(a, b):
        return jnp.where(core == 0, a, b)

    along_z = gather_direct(mine(basis_in, basis_out), "mp", GROUPS_Z)
    own, other = spread_along_x(along_z)
    x = lax.axis_index("mp") // NZ
    table = jnp.stack([core] + [(x - dx + NX) % NX for _, dx, _ in own])
    keep, give = gather_low(
        *project(table, acts_in, grad_out, own, other),
        functools.partial(low_of, (grad_in, acts_out), core),
    )
    shares = lax.all_to_all(
        keep + other_core(give), "dp", 0, 0, axis_index_groups=GROUPS_Y, tiled=True
    )
    share = (shares[0] + shares[1]) + (shares[2] + shares[3])
    new_first_in, new_second_in, step_in = adam_moments(share[0], first_in, second_in)
    new_first_out, new_second_out, step_out = adam_moments(share[1], first_out, second_out)
    steps = gather_direct(jnp.stack([step_in, step_out])[None], "dp")
    delta_in, delta_out = deltas(table, steps, own, other)
    return (
        delta_in,
        delta_out,
        new_first_in,
        new_second_in,
        new_first_out,
        new_second_out,
    )


def solution(mesh):
    in_specs = (
        P(("dp", "mp"), None),
        P("dp", "mp"),
        P("dp", "mp"),
        P(("dp", "mp"), None),
        P("mp", None),
        P("mp", None),
        P("dp", "mp"),
        P("dp", "mp"),
        P("dp", "mp"),
        P("dp", "mp"),
    )
    out_specs = (
        P(None, "mp"),
        P("mp", None),
        P("dp", "mp"),
        P("dp", "mp"),
        P("dp", "mp"),
        P("dp", "mp"),
    )
    return jax.shard_map(body, mesh=mesh, in_specs=in_specs, out_specs=out_specs, check_vma=False)
```

time: 178 us -> 166 us (0.933)
  blocking collectives: 85.5 us -> 45.3 us
  waiting for transfers between devices: 10.1 us -> 46.1 us
  starting transfers between devices: 35.3 us -> 46 us
  local copies, waits for them, and re-layouts: 14.2 us -> 4.83 us
  Pallas kernels: 25.2 us -> 19.8 us
  matrix products: 4.21 us -> 0 us
    ppermute x24 -> x27, waiting for transfers between devices: 6.3 us -> 43.5 us  [shift(): return lax.ppermute(a, 'mp', perm)]
    all_to_all x3 -> x2, blocking collectives: 62.2 us -> 35.5 us  [gather_direct(): got = lax.all_to_all(many, axis, 0, 0, axis_index_groups=groups, tiled=True)]
    pallas_call x5, Pallas kernels: 23.8 us -> 7.82 us  [low_of(): pl.pallas_call(functools.partial(low_kernel, len(pieces), runs, bool(star...]
    all_to_all x1, blocking collectives: 23.3 us -> 9.79 us  [body(): lax.all_to_all(keep + other_core(give), 'dp', 0, 0, axis_index_groups=GRO...]
    ppermute x1 -> x6, starting transfers between devices: 3.95 us -> 16.8 us  [other_core(): return lax.ppermute(a, 'dp', [(d, d ^ 1) for d in range(2 * NY)])]
    pallas_call x1 -> x4, Pallas kernels: 1.38 us -> 12 us  [the longest x2 9.34 us: with_bases(): pl.pallas_call(functools.partial(kernel, [first for _, _, first in own],...]
    unnamed x52, local copies, waits for them, and re-layouts: 10.1 us -> 4.5 us
    dot_general x2 -> x0, matrix products: 4.21 us -> none  [the longest x1 2.12 us: body(): lax.dot_general(steps[:, 1].reshape(R, 256), mine(basis_other, basis_own)...]
  transfers between devices with their start and end apart: 25 -> 33, of which waited for: 7 -> 18; matrix products, arithmetic and copies ran while one was open for 1% -> 0% of each run, Pallas kernels for 12% -> 4%
where the time goes in v3:
time: 166 us; the launch traced here: 165 us
  waiting for transfers between devices  46.1 us (28%)
  starting transfers between devices  46 us (28%)
  blocking collectives  45.3 us (27%)
  Pallas kernels  19.8 us (12%)
  local copies, waits for them, and re-layouts  4.83 us (3%)
  other arithmetic  2.02 us (1%)
    ppermute x27, waiting for transfers between devices, shift(): return lax.ppermute(a, 'mp', perm)  43.5 us
    all_to_all x2, blocking collectives, gather_direct(): got = lax.all_to_all(many, axis, 0, 0, axis_index_groups=groups, tiled=True)  35.5 us
    ppermute x27, starting transfers between devices, shift(): return lax.ppermute(a, 'mp', perm)  29.1 us
    ppermute x6, starting transfers between devices, other_core(): return lax.ppermute(a, 'dp', [(d, d ^ 1) for d in range(2 * NY)])  16.8 us
    all_to_all x1, blocking collectives, body(): lax.all_to_all(keep + other_core(give), 'dp', 0, 0, axis_index_groups=GRO...  9.79 us
    pallas_call x2, Pallas kernels, with_bases(): pl.pallas_call(functools.partial(kernel, [first for _, _, first in own],...  9.34 us
    pallas_call x5, Pallas kernels, low_of(): pl.pallas_call(functools.partial(low_kernel, len(pieces), runs, bool(star...  7.82 us
    unnamed x52, local copies, waits for them, and re-layouts  4.5 us
  transfers between devices with their start and end apart: 33, of which 18 were waited for; matrix products, arithmetic and copies ran while one was open for 0% of the time, Pallas kernels for 4%

profile of v3, /device:TPU:1, one launch (start us, length us, event | category | flops | bytes accessed | tf_op | source)
XLA Modules:
  0.0 165.4 jit_solution(3384363419727592640)
XLA Ops:
  1.6 24.8 %all_to_all.15 = bf16[8,128,256]{2,1,0:T(8,128)(2,1)S(1)} all-to-all(bf16[8,128,256]{2,1,0:T(8,128)(2,1)S(1)} %broadcast_in_dim.4), channel_id=1, replica_groups={{0,1,2,3,4,5,6,7},{8,9,10,11,12,13,14,15},{16,17,18,19,20,21,22,23},{24..., dimensions={0} | all-to-all | bytes 1048576 | tf_op jit(solution)/shard_map/all_to_all | solution.py:50
  26.4 2.5 %collective-permute-start.2 = (bf16[1024,256]{1,0:T(8,128)(2,1)S(1)}, bf16[1024,256]{1,0:T(8,128)(2,1)S(1)}, u32[]{:S(2)}, u32[]{:S(2)}) collective-permute-start(bf16[1024,256]{1,0:T(8,128)(2,1)S(1)} %bitcast.27), channel_id=1, source_target_pairs={{0,32},{32,0},{64,96},{96,64},{128,160},{160,128},{192,224},{224,1... | collective-permute-start | bytes 1572872 | tf_op jit(solution)/shard_map/ppermute | solution.py:44
  28.8 2.5 %collective-permute-start.1 = (bf16[1024,256]{1,0:T(8,128)(2,1)S(1)}, bf16[1024,256]{1,0:T(8,128)(2,1)S(1)}, u32[]{:S(2)}, u32[]{:S(2)}) collective-permute-start(bf16[1024,256]{1,0:T(8,128)(2,1)S(1)} %bitcast.28), channel_id=1, source_target_pairs={{0,24},{1,25},{2,26},{3,27},{4,28},{5,29},{6,30},{7,31},{8,0},{9,1... | collective-permute-start | bytes 1572872 | tf_op jit(solution)/shard_map/ppermute | solution.py:40
  31.3 11.3 %collective-permute-done.1.refs_2_ = bf16[1024,256]{1,0:T(8,128)(2,1)S(1)} collective-permute-done((bf16[1024,256]{1,0:T(8,128)(2,1)S(1)}, bf16[1024,256]{1,0:T(8,128)(2,1)S(1)}, u32[]{:S(2)}, u32[]{:S(2)}) %collective-permute-start.1) | collective-permute-done | bytes 524320 | tf_op jit(solution)/shard_map/ppermute | solution.py:40
  42.7 3.1 %collective-permute-done.refs_1_ = bf16[1024,256]{1,0:T(8,128)(2,1)S(1)} collective-permute-done((bf16[1024,256]{1,0:T(8,128)(2,1)S(1)}, bf16[1024,256]{1,0:T(8,128)(2,1)S(1)}, u32[]{:S(2)}, u32[]{:S(2)}) %collective-permute-start) | collective-permute-done | bytes 524320 | tf_op jit(solution)/shard_map/ppermute | solution.py:40
  47.4 1.7 %collective-permute-start.5 = (bf16[1024,256]{1,0:T(8,128)(2,1)S(1)}, bf16[1024,256]{1,0:T(8,128)(2,1)S(1)}, u32[]{:S(2)}, u32[]{:S(2)}) collective-permute-start(bf16[1024,256]{1,0:T(8,128)(2,1)S(1)} %collective-permute-done.refs_1_), channel_id=1, source_target_pairs={{0,32},{32,0},{64,96},{96,64},{128,160},{160,128},{192,224},{224,1... | collective-permute-start | bytes 1572872 | tf_op jit(solution)/shard_map/ppermute | solution.py:44
  49.1 3.6 %collective-permute-done.4.refs_4_ = bf16[512,256]{1,0:T(8,128)(2,1)S(1)} collective-permute-done((bf16[512,256]{1,0:T(8,128)(2,1)S(1)}, bf16[512,256]{1,0:T(8,128)(2,1)S(1)}, u32[]{:S(2)}, u32[]{:S(2)}) %collective-permute-start.4) | collective-permute-done | bytes 262176 | tf_op jit(solution)/shard_map/ppermute | solution.py:40
  52.6 1.9 %collective-permute-start.8 = (bf16[512,256]{1,0:T(8,128)(2,1)S(1)}, bf16[512,256]{1,0:T(8,128)(2,1)}, u32[]{:S(2)}, u32[]{:S(2)}) collective-permute-start(bf16[512,256]{1,0:T(8,128)(2,1)S(1)} %collective-permute-done.4.refs_4_), channel_id=1, source_target_pairs={{0,32},{32,0},{64,96},{96,64},{128,160},{160,128},{192,224},{224,1... | collective-permute-start | bytes 786440 | tf_op jit(solution)/shard_map/ppermute | solution.py:44
  54.6 1.7 %collective-permute-start.7 = (bf16[512,256]{1,0:T(8,128)(2,1)}, bf16[512,256]{1,0:T(8,128)(2,1)}, u32[]{:S(2)}, u32[]{:S(2)}) collective-permute-start(bf16[512,256]{1,0:T(8,128)(2,1)} %collective-permute-done.3.refs_3_), channel_id=1, source_target_pairs={{0,32},{32,0},{64,96},{96,64},{128,160},{160,128},{192,224},{224,1... | collective-permute-start | bytes 786440 | tf_op jit(solution)/shard_map/ppermute | solution.py:44
  57.8 5.7 %shard_map.235 = (bf16[2,256,128]{2,1,0:T(8,128)(2,1)S(1)}, bf16[2,256,128]{2,1,0:T(8,128)(2,1)S(1)}) custom-call(s32[6]{0:T(128)S(1)} %stack.33.table, bf16[256,4096]{1,0:T(8,128)(2,1)} %acts_in.1, bf16[256,4096]{1,0:T(8,128)(2,1)} %grad_out.1, bf16[1024,256]{1,0:T(8,128)(2,1)S(1)} %bitcast.30, bf16[1024,256]{1,0:T(8,128)(2,1)S(1)} %collective-permute-done.refs_1_, ...), custom_call_target="tpu_custom_call" | custom-call | flops 1073741824 | bytes 8388608 | tf_op jit(solution)/shard_map/pallas_call | solution.py:328
  66.6 1.8 %collective-permute-done.12.refs_2_ = bf16[2,256,128]{2,1,0:T(8,128)(2,1)S(1)} collective-permute-done((bf16[2,256,128]{2,1,0:T(8,128)(2,1)S(1)}, bf16[2,256,128]{2,1,0:T(8,128)(2,1)S(1)}, u32[]{:S(2)}, u32[]{:S(2)}) %collective-permute-start.12) | collective-permute-done | bytes 131104 | tf_op jit(solution)/shard_map/ppermute | solution.py:40
  70.7 2.4 %collective-permute-start.14 = (bf16[2,256,128]{2,1,0:T(8,128)(2,1)S(1)}, bf16[2,256,128]{2,1,0:T(8,128)(2,1)S(1)}, u32[]{:S(2)}, u32[]{:S(2)}) collective-permute-start(bf16[2,256,128]{2,1,0:T(8,128)(2,1)S(1)} %collective-permute-done.10.refs_7_), channel_id=1, source_target_pairs={{0,7},{1,0},{2,1},{3,2},{4,3},{5,4},{6,5},{7,6},{8,15},{9,8},{10,9... | collective-permute-start | bytes 393224 | tf_op jit(solution)/shard_map/ppermute | solution.py:40
  74.7 1.9 %collective-permute-done.16.refs_4_ = bf16[1,256,128]{2,1,0:T(8,128)(2,1)S(1)} collective-permute-done((bf16[1,256,128]{2,1,0:T(8,128)(2,1)S(1)}, bf16[1,256,128]{2,1,0:T(8,128)(2,1)S(1)}, u32[]{:S(2)}, u32[]{:S(2)}) %collective-permute-start.16) | collective-permute-done | bytes 65568 | tf_op jit(solution)/shard_map/ppermute | solution.py:40
  76.6 2.0 %collective-permute-done.15.refs_3_ = bf16[1,256,128]{2,1,0:T(8,128)(2,1)S(1)} collective-permute-done((bf16[1,256,128]{2,1,0:T(8,128)(2,1)S(1)}, bf16[1,256,128]{2,1,0:T(8,128)(2,1)S(1)}, u32[]{:S(2)}, u32[]{:S(2)}) %collective-permute-start.15) | collective-permute-done | bytes 65568 | tf_op jit(solution)/shard_map/ppermute | solution.py:40
  83.1 2.2 %copy-done = bf16[8192,256]{1,0:T(8,128)(2,1)S(1)} copy-done((bf16[8192,256]{1,0:T(8,128)(2,1)S(1)}, bf16[8192,256]{1,0:T(8,128)(2,1)}, u32[]{:S(2)}) %copy-start) | copy-done | bytes 4194328
  85.3 2.2 %copy-done.2 = bf16[8192,256]{1,0:T(8,128)(2,1)S(1)} copy-done((bf16[8192,256]{1,0:T(8,128)(2,1)S(1)}, bf16[8192,256]{1,0:T(8,128)(2,1)}, u32[]{:S(2)}) %copy-start.2) | copy-done | bytes 4194328
  87.5 2.0 %shard_map.237.refs_4_ = f32[8,2,32,256]{3,2,1,0:T(8,128)S(1)} custom-call(s32[11]{0:T(128)S(1)} %pad_add_fusion.1.table, bf16[8192,256]{1,0:T(8,128)(2,1)S(1)} %copy-done, bf16[8192,256]{1,0:T(8,128)(2,1)S(1)} %copy-done.2, bf16[10,256,128]{2,1,0:T(8,128)(2,1)} %get-tuple-element.72.refs_0_, bf16[10,256,128]{2,1,0:T(8,128)(2,1)} %get-tuple-element.74.refs_1_), custom_call_target="tpu_custom_call" | custom-call | flops 301989888 | bytes 2359296 | tf_op jit(solution)/shard_map/pallas_call | solution.py:230
  89.5 3.0 %collective-permute-done.18.refs_1_ = bf16[10,256,128]{2,1,0:T(8,128)(2,1)S(1)} collective-permute-done((bf16[10,256,128]{2,1,0:T(8,128)(2,1)}, bf16[10,256,128]{2,1,0:T(8,128)(2,1)S(1)}, u32[]{:S(2)}, u32[]{:S(2)}) %collective-permute-start.18) | collective-permute-done | bytes 655392 | tf_op jit(solution)/shard_map/ppermute | solution.py:40
  96.8 2.4 %collective-permute-start.22 = (bf16[9,256,128]{2,1,0:T(8,128)(2,1)S(1)}, bf16[9,256,128]{2,1,0:T(8,128)(2,1)S(1)}, u32[]{:S(2)}, u32[]{:S(2)}) collective-permute-start(bf16[9,256,128]{2,1,0:T(8,128)(2,1)S(1)} %get-tuple-element.84), channel_id=1, source_target_pairs={{0,7},{1,0},{2,1},{3,2},{4,3},{5,4},{6,5},{7,6},{8,15},{9,8},{10,9... | collective-permute-start | bytes 1769480 | tf_op jit(solution)/shard_map/ppermute | solution.py:40
  99.2 2.7 %collective-permute-start.24 = (bf16[9,256,128]{2,1,0:T(8,128)(2,1)S(1)}, bf16[9,256,128]{2,1,0:T(8,128)(2,1)S(1)}, u32[]{:S(2)}, u32[]{:S(2)}) collective-permute-start(bf16[9,256,128]{2,1,0:T(8,128)(2,1)S(1)} %get-tuple-element.86), channel_id=1, source_target_pairs={{0,24},{1,25},{2,26},{3,27},{4,28},{5,29},{6,30},{7,31},{8,0},{9,1... | collective-permute-start | bytes 1769480 | tf_op jit(solution)/shard_map/ppermute | solution.py:40
  102.1 2.2 %shard_map.239.refs_4_ = f32[8,2,32,256]{3,2,1,0:T(8,128)S(1)} custom-call(s32[23]{0:T(128)S(1)} %get-tuple-element.123.table, bf16[8192,256]{1,0:T(8,128)(2,1)S(1)} %copy-done.1, bf16[8192,256]{1,0:T(8,128)(2,1)S(1)} %copy-done.2, bf16[10,256,128]{2,1,0:T(8,128)(2,1)S(1)} %collective-permute-done.17.refs_0_, ...), custom_call_target="tpu_custom_call" | custom-call | flops 671088640 | bytes 5242880 | tf_op jit(solution)/shard_map/pallas_call | solution.py:230
  104.3 3.0 %collective-permute-done.21.refs_0_ = bf16[9,256,128]{2,1,0:T(8,128)(2,1)S(1)} collective-permute-done((bf16[9,256,128]{2,1,0:T(8,128)(2,1)S(1)}, bf16[9,256,128]{2,1,0:T(8,128)(2,1)S(1)}, u32[]{:S(2)}, u32[]{:S(2)}) %collective-permute-start.21) | collective-permute-done | bytes 589856 | tf_op jit(solution)/shard_map/ppermute | solution.py:40
  107.3 2.2 %collective-permute-done.23.refs_2_ = bf16[9,256,128]{2,1,0:T(8,128)(2,1)S(1)} collective-permute-done((bf16[9,256,128]{2,1,0:T(8,128)(2,1)S(1)}, bf16[9,256,128]{2,1,0:T(8,128)(2,1)S(1)}, u32[]{:S(2)}, u32[]{:S(2)}) %collective-permute-start.23) | collective-permute-done | bytes 589856 | tf_op jit(solution)/shard_map/ppermute | solution.py:40
  109.8 2.7 %collective-permute-start.26 = (bf16[8,256,128]{2,1,0:T(8,128)(2,1)S(1)}, bf16[8,256,128]{2,1,0:T(8,128)(2,1)S(1)}, u32[]{:S(2)}, u32[]{:S(2)}) collective-permute-start(bf16[8,256,128]{2,1,0:T(8,128)(2,1)S(1)} %slice.65), channel_id=1, source_target_pairs={{0,7},{1,0},{2,1},{3,2},{4,3},{5,4},{6,5},{7,6},{8,15},{9,8},{10,9... | collective-permute-start | bytes 1572872 | tf_op jit(solution)/shard_map/ppermute | solution.py:40
  113.7 2.1 %collective-permute-start.27 = (bf16[4,256,128]{2,1,0:T(8,128)(2,1)S(1)}, bf16[4,256,128]{2,1,0:T(8,128)(2,1)S(1)}, u32[]{:S(2)}, u32[]{:S(2)}) collective-permute-start(bf16[4,256,128]{2,1,0:T(8,128)(2,1)S(1)} %get-tuple-element.94), channel_id=1, source_target_pairs={{0,8},{1,9},{2,10},{3,11},{4,12},{5,13},{6,14},{7,15},{8,16},{9,17... | collective-permute-start | bytes 786440 | tf_op jit(solution)/shard_map/ppermute | solution.py:40
  117.9 3.0 %collective-permute-done.27.refs_2_ = bf16[4,256,128]{2,1,0:T(8,128)(2,1)S(1)} collective-permute-done((bf16[4,256,128]{2,1,0:T(8,128)(2,1)S(1)}, bf16[4,256,128]{2,1,0:T(8,128)(2,1)S(1)}, u32[]{:S(2)}, u32[]{:S(2)}) %collective-permute-start.27) | collective-permute-done | bytes 262176 | tf_op jit(solution)/shard_map/ppermute | solution.py:40
  121.5 2.7 %collective-permute-start.31 = (bf16[4,256,128]{2,1,0:T(8,128)(2,1)S(1)}, bf16[4,256,128]{2,1,0:T(8,128)(2,1)S(1)}, u32[]{:S(2)}, u32[]{:S(2)}) collective-permute-start(bf16[4,256,128]{2,1,0:T(8,128)(2,1)S(1)} %slice.71), channel_id=1, source_target_pairs={{0,7},{1,0},{2,1},{3,2},{4,3},{5,4},{6,5},{7,6},{8,15},{9,8},{10,9... | collective-permute-start | bytes 786440 | tf_op jit(solution)/shard_map/ppermute | solution.py:40
  125.7 3.3 %collective-permute-done.30.refs_0_ = bf16[4,256,128]{2,1,0:T(8,128)(2,1)S(1)} collective-permute-done((bf16[4,256,128]{2,1,0:T(8,128)(2,1)S(1)}, bf16[4,256,128]{2,1,0:T(8,128)(2,1)S(1)}, u32[]{:S(2)}, u32[]{:S(2)}) %collective-permute-start.30) | collective-permute-done | bytes 262176 | tf_op jit(solution)/shard_map/ppermute | solution.py:40
  130.0 9.1 %collective-permute-start.32 = (f32[4,2,32,256]{3,2,1,0:T(8,128)S(1)}, f32[4,2,32,256]{3,2,1,0:T(8,128)S(1)}, u32[]{:S(2)}, u32[]{:S(2)}) collective-permute-start(f32[4,2,32,256]{3,2,1,0:T(8,128)S(1)} %get-tuple-element.109), channel_id=1, source_target_pairs={{0,32},{32,0},{64,96},{96,64},{128,160},{160,128},{192,224},{224,1... | collective-permute-start | bytes 786440 | tf_op jit(solution)/shard_map/ppermute | solution.py:44
  140.2 9.8 %all_to_all.16 = f32[4,2,32,256]{3,2,1,0:T(8,128)S(1)} all-to-all(f32[4,2,32,256]{3,2,1,0:T(8,128)S(1)} %add.208), channel_id=1, replica_groups={{0,64,128,192},{32,96,160,224},{1,65,129,193},{33,97,161,225},{2,66,130..., dimensions={0} | all-to-all | bytes 524288 | tf_op jit(solution)/shard_map/all_to_all | solution.py:402
  150.8 10.7 %all_to_all.17 = bf16[8,1,2,32,256]{4,3,2,1,0:T(8,128)(2,1)S(1)} all-to-all(bf16[8,1,2,32,256]{4,3,2,1,0:T(8,128)(2,1)S(1)} %broadcast_in_dim.5), channel_id=1, replica_groups=mesh['dp'=8,'mp'=32] {'dp'}, dimensions={0} | all-to-all | bytes 524288 | tf_op jit(solution)/shard_map/all_to_all | solution.py:50
  161.5 3.6 %shard_map.243 = (bf16[4096,256]{1,0:T(8,128)(2,1)}, bf16[256,4096]{1,0:T(8,128)(2,1)}) custom-call(s32[6]{0:T(128)S(1)} %stack.33.table, bf16[8,2,32,256]{3,2,1,0:T(8,128)(2,1)S(1)} %bitcast.32, bf16[1024,256]{1,0:T(8,128)(2,1)S(1)} %bitcast.31, bf16[1024,256]{1,0:T(8,128)(2,1)S(1)} %collective-permute-done.refs_1_, ...), custom_call_target="tpu_custom_call" | custom-call | flops 1073741824 | bytes 8388608 | tf_op jit(solution)/shard_map/pallas_call | solution.py:328
  (129 shorter events, 28.4 us)
Async XLA Ops:
  26.4 4.9 %collective-permute-start.2 = (bf16[1024,256]{1,0:T(8,128)(2,1)S(1)}, bf16[1024,256]{1,0:T(8,128)(2,1)S(1)}, u32[]{:S(2)}, u32[]{:S(2)}) collective-permute-start(bf16[1024,256]{1,0:T(8,128)(2,1)S(1)} %bitcast.27), channel_id=1, source_target_pairs={{0,32},{32,0},{64,96},{96,64},{128,160},{160,128},{192,224},{224,1... | collective-permute-start | bytes 1572872 | tf_op jit(solution)/shard_map/ppermute | solution.py:44
  28.8 13.8 %collective-permute-start.1 = (bf16[1024,256]{1,0:T(8,128)(2,1)S(1)}, bf16[1024,256]{1,0:T(8,128)(2,1)S(1)}, u32[]{:S(2)}, u32[]{:S(2)}) collective-permute-start(bf16[1024,256]{1,0:T(8,128)(2,1)S(1)} %bitcast.28), channel_id=1, source_target_pairs={{0,24},{1,25},{2,26},{3,27},{4,28},{5,29},{6,30},{7,31},{8,0},{9,1... | collective-permute-start | bytes 1572872 | tf_op jit(solution)/shard_map/ppermute | solution.py:40
  31.3 14.4 %collective-permute-start = (bf16[1024,256]{1,0:T(8,128)(2,1)S(1)}, bf16[1024,256]{1,0:T(8,128)(2,1)S(1)}, u32[]{:S(2)}, u32[]{:S(2)}) collective-permute-start(bf16[1024,256]{1,0:T(8,128)(2,1)S(1)} %bitcast.29), channel_id=1, source_target_pairs={{0,8},{1,9},{2,10},{3,11},{4,12},{5,13},{6,14},{7,15},{8,16},{9,17... | collective-permute-start | bytes 1572872 | tf_op jit(solution)/shard_map/ppermute | solution.py:40
  45.8 6.9 %collective-permute-start.4 = (bf16[512,256]{1,0:T(8,128)(2,1)S(1)}, bf16[512,256]{1,0:T(8,128)(2,1)S(1)}, u32[]{:S(2)}, u32[]{:S(2)}) collective-permute-start(bf16[512,256]{1,0:T(8,128)(2,1)S(1)} %slice.61), channel_id=1, source_target_pairs={{0,24},{1,25},{2,26},{3,27},{4,28},{5,29},{6,30},{7,31},{8,0},{9,1... | collective-permute-start | bytes 786440 | tf_op jit(solution)/shard_map/ppermute | solution.py:40
  46.2 8.4 %collective-permute-start.3 = (bf16[512,256]{1,0:T(8,128)(2,1)S(1)}, bf16[512,256]{1,0:T(8,128)(2,1)}, u32[]{:S(2)}, u32[]{:S(2)}) collective-permute-start(bf16[512,256]{1,0:T(8,128)(2,1)S(1)} %slice.60), channel_id=1, source_target_pairs={{0,8},{1,9},{2,10},{3,11},{4,12},{5,13},{6,14},{7,15},{8,16},{9,17... | collective-permute-start | bytes 786440 | tf_op jit(solution)/shard_map/ppermute | solution.py:40
  47.4 10.4 %collective-permute-start.5 = (bf16[1024,256]{1,0:T(8,128)(2,1)S(1)}, bf16[1024,256]{1,0:T(8,128)(2,1)S(1)}, u32[]{:S(2)}, u32[]{:S(2)}) collective-permute-start(bf16[1024,256]{1,0:T(8,128)(2,1)S(1)} %collective-permute-done.refs_1_), channel_id=1, source_target_pairs={{0,32},{32,0},{64,96},{96,64},{128,160},{160,128},{192,224},{224,1... | collective-permute-start | bytes 1572872 | tf_op jit(solution)/shard_map/ppermute | solution.py:44
  49.1 8.7 %collective-permute-start.6 = (bf16[1024,256]{1,0:T(8,128)(2,1)S(1)}, bf16[1024,256]{1,0:T(8,128)(2,1)S(1)}, u32[]{:S(2)}, u32[]{:S(2)}) collective-permute-start(bf16[1024,256]{1,0:T(8,128)(2,1)S(1)} %collective-permute-done.1.refs_2_), channel_id=1, source_target_pairs={{0,32},{32,0},{64,96},{96,64},{128,160},{160,128},{192,224},{224,1... | collective-permute-start | bytes 1572872 | tf_op jit(solution)/shard_map/ppermute | solution.py:44
  52.6 3.7 %collective-permute-start.8 = (bf16[512,256]{1,0:T(8,128)(2,1)S(1)}, bf16[512,256]{1,0:T(8,128)(2,1)}, u32[]{:S(2)}, u32[]{:S(2)}) collective-permute-start(bf16[512,256]{1,0:T(8,128)(2,1)S(1)} %collective-permute-done.4.refs_4_), channel_id=1, source_target_pairs={{0,32},{32,0},{64,96},{96,64},{128,160},{160,128},{192,224},{224,1... | collective-permute-start | bytes 786440 | tf_op jit(solution)/shard_map/ppermute | solution.py:44
  63.6 4.8 %collective-permute-start.12 = (bf16[2,256,128]{2,1,0:T(8,128)(2,1)S(1)}, bf16[2,256,128]{2,1,0:T(8,128)(2,1)S(1)}, u32[]{:S(2)}, u32[]{:S(2)}) collective-permute-start(bf16[2,256,128]{2,1,0:T(8,128)(2,1)S(1)} %get-tuple-element.62.refs_0_), channel_id=1, source_target_pairs={{0,24},{1,25},{2,26},{3,27},{4,28},{5,29},{6,30},{7,31},{8,0},{9,1... | collective-permute-start | bytes 393224 | tf_op jit(solution)/shard_map/ppermute | solution.py:40
  63.8 5.6 %collective-permute-start.11 = (bf16[2,256,128]{2,1,0:T(8,128)(2,1)S(1)}, bf16[2,256,128]{2,1,0:T(8,128)(2,1)S(1)}, u32[]{:S(2)}, u32[]{:S(2)}) collective-permute-start(bf16[2,256,128]{2,1,0:T(8,128)(2,1)S(1)} %get-tuple-element.62.refs_0_), channel_id=1, source_target_pairs={{0,8},{1,9},{2,10},{3,11},{4,12},{5,13},{6,14},{7,15},{8,16},{9,17... | collective-permute-start | bytes 393224 | tf_op jit(solution)/shard_map/ppermute | solution.py:40
  65.1 4.3 %collective-permute-start.10 = (bf16[2,256,128]{2,1,0:T(8,128)(2,1)S(1)}, bf16[2,256,128]{2,1,0:T(8,128)(2,1)S(1)}, u32[]{:S(2)}, u32[]{:S(2)}) collective-permute-start(bf16[2,256,128]{2,1,0:T(8,128)(2,1)S(1)} %get-tuple-element.63.refs_5_), channel_id=1, source_target_pairs={{0,7},{1,0},{2,1},{3,2},{4,3},{5,4},{6,5},{7,6},{8,15},{9,8},{10,9... | collective-permute-start | bytes 393224 | tf_op jit(solution)/shard_map/ppermute | solution.py:40
  65.1 5.3 %collective-permute-start.9 = (bf16[2,256,128]{2,1,0:T(8,128)(2,1)S(1)}, bf16[2,256,128]{2,1,0:T(8,128)(2,1)S(1)}, u32[]{:S(2)}, u32[]{:S(2)}) collective-permute-start(bf16[2,256,128]{2,1,0:T(8,128)(2,1)S(1)} %get-tuple-element.63.refs_5_), channel_id=1, source_target_pairs={{0,1},{1,2},{2,3},{3,4},{4,5},{5,6},{6,7},{7,0},{8,9},{9,10},{10,1... | collective-permute-start | bytes 393224 | tf_op jit(solution)/shard_map/ppermute | solution.py:40
  70.4 8.2 %collective-permute-start.13 = (bf16[2,256,128]{2,1,0:T(8,128)(2,1)S(1)}, bf16[2,256,128]{2,1,0:T(8,128)(2,1)S(1)}, u32[]{:S(2)}, u32[]{:S(2)}) collective-permute-start(bf16[2,256,128]{2,1,0:T(8,128)(2,1)S(1)} %collective-permute-done.9.refs_6_), channel_id=1, source_target_pairs={{0,1},{1,2},{2,3},{3,4},{4,5},{5,6},{6,7},{7,0},{8,9},{9,10},{10,1... | collective-permute-start | bytes 393224 | tf_op jit(solution)/shard_map/ppermute | solution.py:40
  70.7 7.9 %collective-permute-start.14 = (bf16[2,256,128]{2,1,0:T(8,128)(2,1)S(1)}, bf16[2,256,128]{2,1,0:T(8,128)(2,1)S(1)}, u32[]{:S(2)}, u32[]{:S(2)}) collective-permute-start(bf16[2,256,128]{2,1,0:T(8,128)(2,1)S(1)} %collective-permute-done.10.refs_7_), channel_id=1, source_target_pairs={{0,7},{1,0},{2,1},{3,2},{4,3},{5,4},{6,5},{7,6},{8,15},{9,8},{10,9... | collective-permute-start | bytes 393224 | tf_op jit(solution)/shard_map/ppermute | solution.py:40
  73.1 3.5 %collective-permute-start.16 = (bf16[1,256,128]{2,1,0:T(8,128)(2,1)S(1)}, bf16[1,256,128]{2,1,0:T(8,128)(2,1)S(1)}, u32[]{:S(2)}, u32[]{:S(2)}) collective-permute-start(bf16[1,256,128]{2,1,0:T(8,128)(2,1)S(1)} %slice.63), channel_id=1, source_target_pairs={{0,24},{1,25},{2,26},{3,27},{4,28},{5,29},{6,30},{7,31},{8,0},{9,1... | collective-permute-start | bytes 196616 | tf_op jit(solution)/shard_map/ppermute | solution.py:40
  74.3 4.3 %collective-permute-start.15 = (bf16[1,256,128]{2,1,0:T(8,128)(2,1)S(1)}, bf16[1,256,128]{2,1,0:T(8,128)(2,1)S(1)}, u32[]{:S(2)}, u32[]{:S(2)}) collective-permute-start(bf16[1,256,128]{2,1,0:T(8,128)(2,1)S(1)} %slice.62), channel_id=1, source_target_pairs={{0,8},{1,9},{2,10},{3,11},{4,12},{5,13},{6,14},{7,15},{8,16},{9,17... | collective-permute-start | bytes 196616 | tf_op jit(solution)/shard_map/ppermute | solution.py:40
  80.1 12.5 %collective-permute-start.18 = (bf16[10,256,128]{2,1,0:T(8,128)(2,1)}, bf16[10,256,128]{2,1,0:T(8,128)(2,1)S(1)}, u32[]{:S(2)}, u32[]{:S(2)}) collective-permute-start(bf16[10,256,128]{2,1,0:T(8,128)(2,1)} %get-tuple-element.73), channel_id=1, source_target_pairs={{0,7},{1,0},{2,1},{3,2},{4,3},{5,4},{6,5},{7,6},{8,15},{9,8},{10,9... | collective-permute-start | bytes 1966088 | tf_op jit(solution)/shard_map/ppermute | solution.py:40
  80.1 13.7 %collective-permute-start.17 = (bf16[10,256,128]{2,1,0:T(8,128)(2,1)}, bf16[10,256,128]{2,1,0:T(8,128)(2,1)S(1)}, u32[]{:S(2)}, u32[]{:S(2)}) collective-permute-start(bf16[10,256,128]{2,1,0:T(8,128)(2,1)} %get-tuple-element.72.refs_0_), channel_id=1, source_target_pairs={{0,1},{1,2},{2,3},{3,4},{4,5},{5,6},{6,7},{7,0},{8,9},{9,10},{10,1... | collective-permute-start | bytes 1966088 | tf_op jit(solution)/shard_map/ppermute | solution.py:40
  81.5 12.2 %collective-permute-start.20 = (bf16[10,256,128]{2,1,0:T(8,128)(2,1)}, bf16[10,256,128]{2,1,0:T(8,128)(2,1)S(1)}, u32[]{:S(2)}, u32[]{:S(2)}) collective-permute-start(bf16[10,256,128]{2,1,0:T(8,128)(2,1)} %get-tuple-element.74.refs_1_), channel_id=1, source_target_pairs={{0,24},{1,25},{2,26},{3,27},{4,28},{5,29},{6,30},{7,31},{8,0},{9,1... | collective-permute-start | bytes 1966088 | tf_op jit(solution)/shard_map/ppermute | solution.py:40
  81.8 13.4 %collective-permute-start.19 = (bf16[10,256,128]{2,1,0:T(8,128)(2,1)}, bf16[10,256,128]{2,1,0:T(8,128)(2,1)}, u32[]{:S(2)}, u32[]{:S(2)}) collective-permute-start(bf16[10,256,128]{2,1,0:T(8,128)(2,1)} %get-tuple-element.74.refs_1_), channel_id=1, source_target_pairs={{0,8},{1,9},{2,10},{3,11},{4,12},{5,13},{6,14},{7,15},{8,16},{9,17... | collective-permute-start | bytes 1966088 | tf_op jit(solution)/shard_map/ppermute | solution.py:40
  96.5 10.8 %collective-permute-start.21 = (bf16[9,256,128]{2,1,0:T(8,128)(2,1)S(1)}, bf16[9,256,128]{2,1,0:T(8,128)(2,1)S(1)}, u32[]{:S(2)}, u32[]{:S(2)}) collective-permute-start(bf16[9,256,128]{2,1,0:T(8,128)(2,1)S(1)} %get-tuple-element.83), channel_id=1, source_target_pairs={{0,1},{1,2},{2,3},{3,4},{4,5},{5,6},{6,7},{7,0},{8,9},{9,10},{10,1... | collective-permute-start | bytes 1769480 | tf_op jit(solution)/shard_map/ppermute | solution.py:40
  96.8 10.5 %collective-permute-start.22 = (bf16[9,256,128]{2,1,0:T(8,128)(2,1)S(1)}, bf16[9,256,128]{2,1,0:T(8,128)(2,1)S(1)}, u32[]{:S(2)}, u32[]{:S(2)}) collective-permute-start(bf16[9,256,128]{2,1,0:T(8,128)(2,1)S(1)} %get-tuple-element.84), channel_id=1, source_target_pairs={{0,7},{1,0},{2,1},{3,2},{4,3},{5,4},{6,5},{7,6},{8,15},{9,8},{10,9... | collective-permute-start | bytes 1769480 | tf_op jit(solution)/shard_map/ppermute | solution.py:40
  99.2 10.2 %collective-permute-start.23 = (bf16[9,256,128]{2,1,0:T(8,128)(2,1)S(1)}, bf16[9,256,128]{2,1,0:T(8,128)(2,1)S(1)}, u32[]{:S(2)}, u32[]{:S(2)}) collective-permute-start(bf16[9,256,128]{2,1,0:T(8,128)(2,1)S(1)} %get-tuple-element.85), channel_id=1, source_target_pairs={{0,8},{1,9},{2,10},{3,11},{4,12},{5,13},{6,14},{7,15},{8,16},{9,17... | collective-permute-start | bytes 1769480 | tf_op jit(solution)/shard_map/ppermute | solution.py:40
  99.2 10.2 %collective-permute-start.24 = (bf16[9,256,128]{2,1,0:T(8,128)(2,1)S(1)}, bf16[9,256,128]{2,1,0:T(8,128)(2,1)S(1)}, u32[]{:S(2)}, u32[]{:S(2)}) collective-permute-start(bf16[9,256,128]{2,1,0:T(8,128)(2,1)S(1)} %get-tuple-element.86), channel_id=1, source_target_pairs={{0,24},{1,25},{2,26},{3,27},{4,28},{5,29},{6,30},{7,31},{8,0},{9,1... | collective-permute-start | bytes 1769480 | tf_op jit(solution)/shard_map/ppermute | solution.py:40
  109.7 11.6 %collective-permute-start.25 = (bf16[8,256,128]{2,1,0:T(8,128)(2,1)S(1)}, bf16[8,256,128]{2,1,0:T(8,128)(2,1)S(1)}, u32[]{:S(2)}, u32[]{:S(2)}) collective-permute-start(bf16[8,256,128]{2,1,0:T(8,128)(2,1)S(1)} %slice.64), channel_id=1, source_target_pairs={{0,1},{1,2},{2,3},{3,4},{4,5},{5,6},{6,7},{7,0},{8,9},{9,10},{10,1... | collective-permute-start | bytes 1572872 | tf_op jit(solution)/shard_map/ppermute | solution.py:40
  109.8 11.5 %collective-permute-start.26 = (bf16[8,256,128]{2,1,0:T(8,128)(2,1)S(1)}, bf16[8,256,128]{2,1,0:T(8,128)(2,1)S(1)}, u32[]{:S(2)}, u32[]{:S(2)}) collective-permute-start(bf16[8,256,128]{2,1,0:T(8,128)(2,1)S(1)} %slice.65), channel_id=1, source_target_pairs={{0,7},{1,0},{2,1},{3,2},{4,3},{5,4},{6,5},{7,6},{8,15},{9,8},{10,9... | collective-permute-start | bytes 1572872 | tf_op jit(solution)/shard_map/ppermute | solution.py:40
  112.5 5.5 %collective-permute-start.29 = (bf16[2,256,128]{2,1,0:T(8,128)(2,1)S(1)}, bf16[2,256,128]{2,1,0:T(8,128)(2,1)S(1)}, u32[]{:S(2)}, u32[]{:S(2)}) collective-permute-start(bf16[2,256,128]{2,1,0:T(8,128)(2,1)S(1)} %pad_maximum_fusion.3), channel_id=1, source_target_pairs={{0,16},{1,17},{2,18},{3,19},{4,20},{5,21},{6,22},{7,23},{8,24},{9,... | collective-permute-start | bytes 393224 | tf_op jit(solution)/shard_map/ppermute | solution.py:40
  113.7 7.3 %collective-permute-start.27 = (bf16[4,256,128]{2,1,0:T(8,128)(2,1)S(1)}, bf16[4,256,128]{2,1,0:T(8,128)(2,1)S(1)}, u32[]{:S(2)}, u32[]{:S(2)}) collective-permute-start(bf16[4,256,128]{2,1,0:T(8,128)(2,1)S(1)} %get-tuple-element.94), channel_id=1, source_target_pairs={{0,8},{1,9},{2,10},{3,11},{4,12},{5,13},{6,14},{7,15},{8,16},{9,17... | collective-permute-start | bytes 786440 | tf_op jit(solution)/shard_map/ppermute | solution.py:40
  115.8 5.5 %collective-permute-start.28 = (bf16[4,256,128]{2,1,0:T(8,128)(2,1)S(1)}, bf16[4,256,128]{2,1,0:T(8,128)(2,1)S(1)}, u32[]{:S(2)}, u32[]{:S(2)}) collective-permute-start(bf16[4,256,128]{2,1,0:T(8,128)(2,1)S(1)} %get-tuple-element.95), channel_id=1, source_target_pairs={{0,24},{1,25},{2,26},{3,27},{4,28},{5,29},{6,30},{7,31},{8,0},{9,1... | collective-permute-start | bytes 786440 | tf_op jit(solution)/shard_map/ppermute | solution.py:40
  121.4 7.6 %collective-permute-start.30 = (bf16[4,256,128]{2,1,0:T(8,128)(2,1)S(1)}, bf16[4,256,128]{2,1,0:T(8,128)(2,1)S(1)}, u32[]{:S(2)}, u32[]{:S(2)}) collective-permute-start(bf16[4,256,128]{2,1,0:T(8,128)(2,1)S(1)} %slice.70), channel_id=1, source_target_pairs={{0,1},{1,2},{2,3},{3,4},{4,5},{5,6},{6,7},{7,0},{8,9},{9,10},{10,1... | collective-permute-start | bytes 786440 | tf_op jit(solution)/shard_map/ppermute | solution.py:40
  121.5 7.5 %collective-permute-start.31 = (bf16[4,256,128]{2,1,0:T(8,128)(2,1)S(1)}, bf16[4,256,128]{2,1,0:T(8,128)(2,1)S(1)}, u32[]{:S(2)}, u32[]{:S(2)}) collective-permute-start(bf16[4,256,128]{2,1,0:T(8,128)(2,1)S(1)} %slice.71), channel_id=1, source_target_pairs={{0,7},{1,0},{2,1},{3,2},{4,3},{5,4},{6,5},{7,6},{8,15},{9,8},{10,9... | collective-permute-start | bytes 786440 | tf_op jit(solution)/shard_map/ppermute | solution.py:40
  130.0 10.2 %collective-permute-start.32 = (f32[4,2,32,256]{3,2,1,0:T(8,128)S(1)}, f32[4,2,32,256]{3,2,1,0:T(8,128)S(1)}, u32[]{:S(2)}, u32[]{:S(2)}) collective-permute-start(f32[4,2,32,256]{3,2,1,0:T(8,128)S(1)} %get-tuple-element.109), channel_id=1, source_target_pairs={{0,32},{32,0},{64,96},{96,64},{128,160},{160,128},{192,224},{224,1... | collective-permute-start | bytes 786440 | tf_op jit(solution)/shard_map/ppermute | solution.py:44
  (27 other events, 459.0 us)

commit v4 on v3

--- a/solution.py
+++ b/solution.py
@@ -245,9 +245,9 @@
 def spread_along_x(own):
     h = own.shape[0] // 2
     ahead, behind = shift(own, 1, 0), shift(own, -1, 0)
+    ahead, behind, own = bar((ahead, behind, own))
+    far = shift(ahead[:h], 1, 0), shift(behind[h:], -1, 0)
     own_other = other_core(own)
-    ahead, behind, own_other = bar((ahead, behind, own_other))
-    far = shift(ahead[:h], 1, 0), shift(behind[h:], -1, 0)
     near_other = other_core(ahead), other_core(behind)
     places = [(0, 0), (1, 0), (-1, 0), (2, 0), (2, h)]
     arrays = [own, ahead, behind, *far]

time: 166 us -> 163 us (0.982)
  waiting for transfers between devices: 46.1 us -> 40.9 us
  starting transfers between devices: 46 us -> 48.1 us
    ppermute x27, waiting for transfers between devices: 43.5 us -> 38.3 us  [shift(): return lax.ppermute(a, 'mp', perm)]
    ppermute x6, starting transfers between devices: 16.8 us -> 19 us  [other_core(): return lax.ppermute(a, 'dp', [(d, d ^ 1) for d in range(2 * NY)])]
  transfers between devices with their start and end apart: 33 -> 33, of which waited for: 18 -> 17; matrix products, arithmetic and copies ran while one was open for 0% -> 0% of each run, Pallas kernels for 4% -> 4%
where the time goes in v4:
time: 163 us; the launch traced here: 162 us
  starting transfers between devices  48.1 us (30%)
  blocking collectives  45.3 us (28%)
  waiting for transfers between devices  40.9 us (25%)
  Pallas kernels  20 us (12%)
  local copies, waits for them, and re-layouts  4.83 us (3%)
  other arithmetic  2.02 us (1%)
    ppermute x27, waiting for transfers between devices, shift(): return lax.ppermute(a, 'mp', perm)  38.3 us
    all_to_all x2, blocking collectives, gather_direct(): got = lax.all_to_all(many, axis, 0, 0, axis_index_groups=groups, tiled=True)  35.5 us
    ppermute x27, starting transfers between devices, shift(): return lax.ppermute(a, 'mp', perm)  29.1 us
    ppermute x6, starting transfers between devices, other_core(): return lax.ppermute(a, 'dp', [(d, d ^ 1) for d in range(2 * NY)])  19 us
    all_to_all x1, blocking collectives, body(): lax.all_to_all(keep + other_core(give), 'dp', 0, 0, axis_index_groups=GRO...  9.79 us
    pallas_call x2, Pallas kernels, with_bases(): pl.pallas_call(functools.partial(kernel, [first for _, _, first in own],...  9.51 us
    pallas_call x5, Pallas kernels, low_of(): pl.pallas_call(functools.partial(low_kernel, len(pieces), runs, bool(star...  7.82 us
    unnamed x52, local copies, waits for them, and re-layouts  4.5 us
  transfers between devices with their start and end apart: 33, of which 17 were waited for; matrix products, arithmetic and copies ran while one was open for 0% of the time, Pallas kernels for 4%

profile of v4, /device:TPU:1, one launch (start us, length us, event | category | flops | bytes accessed | tf_op | source)
XLA Modules:
  0.0 162.4 jit_solution(12344057538344903563)
XLA Ops:
  1.6 24.8 %all_to_all.15 = bf16[8,128,256]{2,1,0:T(8,128)(2,1)S(1)} all-to-all(bf16[8,128,256]{2,1,0:T(8,128)(2,1)S(1)} %broadcast_in_dim.4), channel_id=1, replica_groups={{0,1,2,3,4,5,6,7},{8,9,10,11,12,13,14,15},{16,17,18,19,20,21,22,23},{24..., dimensions={0} | all-to-all | bytes 1048576 | tf_op jit(solution)/shard_map/all_to_all | solution.py:50
  26.4 2.5 %collective-permute-start.1 = (bf16[1024,256]{1,0:T(8,128)(2,1)S(1)}, bf16[1024,256]{1,0:T(8,128)(2,1)S(1)}, u32[]{:S(2)}, u32[]{:S(2)}) collective-permute-start(bf16[1024,256]{1,0:T(8,128)(2,1)S(1)} %bitcast.27), channel_id=1, source_target_pairs={{0,24},{1,25},{2,26},{3,27},{4,28},{5,29},{6,30},{7,31},{8,0},{9,1... | collective-permute-start | bytes 1572872 | tf_op jit(solution)/shard_map/ppermute | solution.py:40
  28.8 8.8 %collective-permute-done.1.refs_2_ = bf16[1024,256]{1,0:T(8,128)(2,1)S(1)} collective-permute-done((bf16[1024,256]{1,0:T(8,128)(2,1)S(1)}, bf16[1024,256]{1,0:T(8,128)(2,1)S(1)}, u32[]{:S(2)}, u32[]{:S(2)}) %collective-permute-start.1) | collective-permute-done | bytes 524320 | tf_op jit(solution)/shard_map/ppermute | solution.py:40
  37.6 3.1 %collective-permute-done.refs_1_ = bf16[1024,256]{1,0:T(8,128)(2,1)S(1)} collective-permute-done((bf16[1024,256]{1,0:T(8,128)(2,1)S(1)}, bf16[1024,256]{1,0:T(8,128)(2,1)S(1)}, u32[]{:S(2)}, u32[]{:S(2)}) %collective-permute-start) | collective-permute-done | bytes 524320 | tf_op jit(solution)/shard_map/ppermute | solution.py:40
  42.4 4.2 %collective-permute-start.4 = (bf16[1024,256]{1,0:T(8,128)(2,1)S(1)}, bf16[1024,256]{1,0:T(8,128)(2,1)S(1)}, u32[]{:S(2)}, u32[]{:S(2)}) collective-permute-start(bf16[1024,256]{1,0:T(8,128)(2,1)S(1)} %bitcast.29), channel_id=1, source_target_pairs={{0,32},{32,0},{64,96},{96,64},{128,160},{160,128},{192,224},{224,1... | collective-permute-start | bytes 1572872 | tf_op jit(solution)/shard_map/ppermute | solution.py:44
  47.1 3.7 %collective-permute-start.8 = (bf16[512,256]{1,0:T(8,128)(2,1)S(1)}, bf16[512,256]{1,0:T(8,128)(2,1)}, u32[]{:S(2)}, u32[]{:S(2)}) collective-permute-start(bf16[512,256]{1,0:T(8,128)(2,1)S(1)} %collective-permute-done.3.refs_4_), channel_id=1, source_target_pairs={{0,32},{32,0},{64,96},{96,64},{128,160},{160,128},{192,224},{224,1... | collective-permute-start | bytes 786440 | tf_op jit(solution)/shard_map/ppermute | solution.py:44
  50.9 1.7 %collective-permute-start.7 = (bf16[512,256]{1,0:T(8,128)(2,1)}, bf16[512,256]{1,0:T(8,128)(2,1)}, u32[]{:S(2)}, u32[]{:S(2)}) collective-permute-start(bf16[512,256]{1,0:T(8,128)(2,1)} %collective-permute-done.2.refs_3_), channel_id=1, source_target_pairs={{0,32},{32,0},{64,96},{96,64},{128,160},{160,128},{192,224},{224,1... | collective-permute-start | bytes 786440 | tf_op jit(solution)/shard_map/ppermute | solution.py:44
  54.1 5.9 %shard_map.235 = (bf16[2,256,128]{2,1,0:T(8,128)(2,1)S(1)}, bf16[2,256,128]{2,1,0:T(8,128)(2,1)S(1)}) custom-call(s32[6]{0:T(128)S(1)} %stack.33.table, bf16[256,4096]{1,0:T(8,128)(2,1)} %acts_in.1, bf16[256,4096]{1,0:T(8,128)(2,1)} %grad_out.1, bf16[1024,256]{1,0:T(8,128)(2,1)S(1)} %bitcast.30, bf16[1024,256]{1,0:T(8,128)(2,1)S(1)} %collective-permute-done.refs_1_, ...), custom_call_target="tpu_custom_call" | custom-call | flops 1073741824 | bytes 8388608 | tf_op jit(solution)/shard_map/pallas_call | solution.py:328
  63.0 1.8 %collective-permute-done.12.refs_2_ = bf16[2,256,128]{2,1,0:T(8,128)(2,1)S(1)} collective-permute-done((bf16[2,256,128]{2,1,0:T(8,128)(2,1)S(1)}, bf16[2,256,128]{2,1,0:T(8,128)(2,1)S(1)}, u32[]{:S(2)}, u32[]{:S(2)}) %collective-permute-start.12) | collective-permute-done | bytes 131104 | tf_op jit(solution)/shard_map/ppermute | solution.py:40
  66.9 2.7 %collective-permute-start.14 = (bf16[2,256,128]{2,1,0:T(8,128)(2,1)S(1)}, bf16[2,256,128]{2,1,0:T(8,128)(2,1)S(1)}, u32[]{:S(2)}, u32[]{:S(2)}) collective-permute-start(bf16[2,256,128]{2,1,0:T(8,128)(2,1)S(1)} %collective-permute-done.10.refs_7_), channel_id=1, source_target_pairs={{0,7},{1,0},{2,1},{3,2},{4,3},{5,4},{6,5},{7,6},{8,15},{9,8},{10,9... | collective-permute-start | bytes 393224 | tf_op jit(solution)/shard_map/ppermute | solution.py:40
  69.6 1.6 collective-permute-start.16
  71.1 1.9 %collective-permute-done.16.refs_4_ = bf16[1,256,128]{2,1,0:T(8,128)(2,1)S(1)} collective-permute-done((bf16[1,256,128]{2,1,0:T(8,128)(2,1)S(1)}, bf16[1,256,128]{2,1,0:T(8,128)(2,1)S(1)}, u32[]{:S(2)}, u32[]{:S(2)}) %collective-permute-start.16) | collective-permute-done | bytes 65568 | tf_op jit(solution)/shard_map/ppermute | solution.py:40
  73.1 2.4 %collective-permute-done.15.refs_3_ = bf16[1,256,128]{2,1,0:T(8,128)(2,1)S(1)} collective-permute-done((bf16[1,256,128]{2,1,0:T(8,128)(2,1)S(1)}, bf16[1,256,128]{2,1,0:T(8,128)(2,1)S(1)}, u32[]{:S(2)}, u32[]{:S(2)}) %collective-permute-start.15) | collective-permute-done | bytes 65568 | tf_op jit(solution)/shard_map/ppermute | solution.py:40
  79.9 2.2 %copy-done = bf16[8192,256]{1,0:T(8,128)(2,1)S(1)} copy-done((bf16[8192,256]{1,0:T(8,128)(2,1)S(1)}, bf16[8192,256]{1,0:T(8,128)(2,1)}, u32[]{:S(2)}) %copy-start) | copy-done | bytes 4194328
  82.1 2.2 %copy-done.2 = bf16[8192,256]{1,0:T(8,128)(2,1)S(1)} copy-done((bf16[8192,256]{1,0:T(8,128)(2,1)S(1)}, bf16[8192,256]{1,0:T(8,128)(2,1)}, u32[]{:S(2)}) %copy-start.2) | copy-done | bytes 4194328
  84.3 2.0 %shard_map.237.refs_4_ = f32[8,2,32,256]{3,2,1,0:T(8,128)S(1)} custom-call(s32[11]{0:T(128)S(1)} %pad_add_fusion.1.table, bf16[8192,256]{1,0:T(8,128)(2,1)S(1)} %copy-done, bf16[8192,256]{1,0:T(8,128)(2,1)S(1)} %copy-done.2, bf16[10,256,128]{2,1,0:T(8,128)(2,1)} %get-tuple-element.72.refs_0_, bf16[10,256,128]{2,1,0:T(8,128)(2,1)} %get-tuple-element.74.refs_1_), custom_call_target="tpu_custom_call" | custom-call | flops 301989888 | bytes 2359296 | tf_op jit(solution)/shard_map/pallas_call | solution.py:230
  86.3 3.5 %collective-permute-done.18.refs_1_ = bf16[10,256,128]{2,1,0:T(8,128)(2,1)S(1)} collective-permute-done((bf16[10,256,128]{2,1,0:T(8,128)(2,1)}, bf16[10,256,128]{2,1,0:T(8,128)(2,1)S(1)}, u32[]{:S(2)}, u32[]{:S(2)}) %collective-permute-start.18) | collective-permute-done | bytes 655392 | tf_op jit(solution)/shard_map/ppermute | solution.py:40
  91.1 1.5 collective-permute-done.19.refs_2_
  94.2 2.4 %collective-permute-start.22 = (bf16[9,256,128]{2,1,0:T(8,128)(2,1)S(1)}, bf16[9,256,128]{2,1,0:T(8,128)(2,1)S(1)}, u32[]{:S(2)}, u32[]{:S(2)}) collective-permute-start(bf16[9,256,128]{2,1,0:T(8,128)(2,1)S(1)} %get-tuple-element.84), channel_id=1, source_target_pairs={{0,7},{1,0},{2,1},{3,2},{4,3},{5,4},{6,5},{7,6},{8,15},{9,8},{10,9... | collective-permute-start | bytes 1769480 | tf_op jit(solution)/shard_map/ppermute | solution.py:40
  96.6 2.7 %collective-permute-start.24 = (bf16[9,256,128]{2,1,0:T(8,128)(2,1)S(1)}, bf16[9,256,128]{2,1,0:T(8,128)(2,1)S(1)}, u32[]{:S(2)}, u32[]{:S(2)}) collective-permute-start(bf16[9,256,128]{2,1,0:T(8,128)(2,1)S(1)} %get-tuple-element.86), channel_id=1, source_target_pairs={{0,24},{1,25},{2,26},{3,27},{4,28},{5,29},{6,30},{7,31},{8,0},{9,1... | collective-permute-start | bytes 1769480 | tf_op jit(solution)/shard_map/ppermute | solution.py:40
  99.4 2.2 %shard_map.239.refs_4_ = f32[8,2,32,256]{3,2,1,0:T(8,128)S(1)} custom-call(s32[23]{0:T(128)S(1)} %get-tuple-element.123.table, bf16[8192,256]{1,0:T(8,128)(2,1)S(1)} %copy-done.1, bf16[8192,256]{1,0:T(8,128)(2,1)S(1)} %copy-done.2, bf16[10,256,128]{2,1,0:T(8,128)(2,1)S(1)} %collective-permute-done.17.refs_0_, ...), custom_call_target="tpu_custom_call" | custom-call | flops 671088640 | bytes 5242880 | tf_op jit(solution)/shard_map/pallas_call | solution.py:230
  101.6 3.5 %collective-permute-done.21.refs_0_ = bf16[9,256,128]{2,1,0:T(8,128)(2,1)S(1)} collective-permute-done((bf16[9,256,128]{2,1,0:T(8,128)(2,1)S(1)}, bf16[9,256,128]{2,1,0:T(8,128)(2,1)S(1)}, u32[]{:S(2)}, u32[]{:S(2)}) %collective-permute-start.21) | collective-permute-done | bytes 589856 | tf_op jit(solution)/shard_map/ppermute | solution.py:40
  105.1 2.1 %collective-permute-done.23.refs_2_ = bf16[9,256,128]{2,1,0:T(8,128)(2,1)S(1)} collective-permute-done((bf16[9,256,128]{2,1,0:T(8,128)(2,1)S(1)}, bf16[9,256,128]{2,1,0:T(8,128)(2,1)S(1)}, u32[]{:S(2)}, u32[]{:S(2)}) %collective-permute-start.23) | collective-permute-done | bytes 589856 | tf_op jit(solution)/shard_map/ppermute | solution.py:40
  107.5 2.7 %collective-permute-start.26 = (bf16[8,256,128]{2,1,0:T(8,128)(2,1)S(1)}, bf16[8,256,128]{2,1,0:T(8,128)(2,1)S(1)}, u32[]{:S(2)}, u32[]{:S(2)}) collective-permute-start(bf16[8,256,128]{2,1,0:T(8,128)(2,1)S(1)} %slice.65), channel_id=1, source_target_pairs={{0,7},{1,0},{2,1},{3,2},{4,3},{5,4},{6,5},{7,6},{8,15},{9,8},{10,9... | collective-permute-start | bytes 1572872 | tf_op jit(solution)/shard_map/ppermute | solution.py:40
  111.5 1.8 %collective-permute-start.27 = (bf16[4,256,128]{2,1,0:T(8,128)(2,1)S(1)}, bf16[4,256,128]{2,1,0:T(8,128)(2,1)S(1)}, u32[]{:S(2)}, u32[]{:S(2)}) collective-permute-start(bf16[4,256,128]{2,1,0:T(8,128)(2,1)S(1)} %get-tuple-element.94), channel_id=1, source_target_pairs={{0,8},{1,9},{2,10},{3,11},{4,12},{5,13},{6,14},{7,15},{8,16},{9,17... | collective-permute-start | bytes 786440 | tf_op jit(solution)/shard_map/ppermute | solution.py:40
  115.7 3.0 %collective-permute-done.27.refs_2_ = bf16[4,256,128]{2,1,0:T(8,128)(2,1)S(1)} collective-permute-done((bf16[4,256,128]{2,1,0:T(8,128)(2,1)S(1)}, bf16[4,256,128]{2,1,0:T(8,128)(2,1)S(1)}, u32[]{:S(2)}, u32[]{:S(2)}) %collective-permute-start.27) | collective-permute-done | bytes 262176 | tf_op jit(solution)/shard_map/ppermute | solution.py:40
  119.0 2.7 %collective-permute-start.31 = (bf16[4,256,128]{2,1,0:T(8,128)(2,1)S(1)}, bf16[4,256,128]{2,1,0:T(8,128)(2,1)S(1)}, u32[]{:S(2)}, u32[]{:S(2)}) collective-permute-start(bf16[4,256,128]{2,1,0:T(8,128)(2,1)S(1)} %slice.71), channel_id=1, source_target_pairs={{0,7},{1,0},{2,1},{3,2},{4,3},{5,4},{6,5},{7,6},{8,15},{9,8},{10,9... | collective-permute-start | bytes 786440 | tf_op jit(solution)/shard_map/ppermute | solution.py:40
  123.1 3.2 %collective-permute-done.30.refs_0_ = bf16[4,256,128]{2,1,0:T(8,128)(2,1)S(1)} collective-permute-done((bf16[4,256,128]{2,1,0:T(8,128)(2,1)S(1)}, bf16[4,256,128]{2,1,0:T(8,128)(2,1)S(1)}, u32[]{:S(2)}, u32[]{:S(2)}) %collective-permute-start.30) | collective-permute-done | bytes 262176 | tf_op jit(solution)/shard_map/ppermute | solution.py:40
  127.3 8.8 %collective-permute-start.32 = (f32[4,2,32,256]{3,2,1,0:T(8,128)S(1)}, f32[4,2,32,256]{3,2,1,0:T(8,128)S(1)}, u32[]{:S(2)}, u32[]{:S(2)}) collective-permute-start(f32[4,2,32,256]{3,2,1,0:T(8,128)S(1)} %get-tuple-element.109), channel_id=1, source_target_pairs={{0,32},{32,0},{64,96},{96,64},{128,160},{160,128},{192,224},{224,1... | collective-permute-start | bytes 786440 | tf_op jit(solution)/shard_map/ppermute | solution.py:44
  137.3 9.8 %all_to_all.16 = f32[4,2,32,256]{3,2,1,0:T(8,128)S(1)} all-to-all(f32[4,2,32,256]{3,2,1,0:T(8,128)S(1)} %add.208), channel_id=1, replica_groups={{0,64,128,192},{32,96,160,224},{1,65,129,193},{33,97,161,225},{2,66,130..., dimensions={0} | all-to-all | bytes 524288 | tf_op jit(solution)/shard_map/all_to_all | solution.py:402
  147.9 10.7 %all_to_all.17 = bf16[8,1,2,32,256]{4,3,2,1,0:T(8,128)(2,1)S(1)} all-to-all(bf16[8,1,2,32,256]{4,3,2,1,0:T(8,128)(2,1)S(1)} %broadcast_in_dim.5), channel_id=1, replica_groups=mesh['dp'=8,'mp'=32] {'dp'}, dimensions={0} | all-to-all | bytes 524288 | tf_op jit(solution)/shard_map/all_to_all | solution.py:50
  158.6 3.6 %shard_map.243 = (bf16[4096,256]{1,0:T(8,128)(2,1)}, bf16[256,4096]{1,0:T(8,128)(2,1)}) custom-call(s32[6]{0:T(128)S(1)} %stack.33.table, bf16[8,2,32,256]{3,2,1,0:T(8,128)(2,1)S(1)} %bitcast.32, bf16[1024,256]{1,0:T(8,128)(2,1)S(1)} %bitcast.31, bf16[1024,256]{1,0:T(8,128)(2,1)S(1)} %collective-permute-done.refs_1_, ...), custom_call_target="tpu_custom_call" | custom-call | flops 1073741824 | bytes 8388608 | tf_op jit(solution)/shard_map/pallas_call | solution.py:328
  (129 shorter events, 25.6 us)
Async XLA Ops:
  26.4 11.2 %collective-permute-start.1 = (bf16[1024,256]{1,0:T(8,128)(2,1)S(1)}, bf16[1024,256]{1,0:T(8,128)(2,1)S(1)}, u32[]{:S(2)}, u32[]{:S(2)}) collective-permute-start(bf16[1024,256]{1,0:T(8,128)(2,1)S(1)} %bitcast.27), channel_id=1, source_target_pairs={{0,24},{1,25},{2,26},{3,27},{4,28},{5,29},{6,30},{7,31},{8,0},{9,1... | collective-permute-start | bytes 1572872 | tf_op jit(solution)/shard_map/ppermute | solution.py:40
  28.8 11.9 %collective-permute-start = (bf16[1024,256]{1,0:T(8,128)(2,1)S(1)}, bf16[1024,256]{1,0:T(8,128)(2,1)S(1)}, u32[]{:S(2)}, u32[]{:S(2)}) collective-permute-start(bf16[1024,256]{1,0:T(8,128)(2,1)S(1)} %bitcast.28), channel_id=1, source_target_pairs={{0,8},{1,9},{2,10},{3,11},{4,12},{5,13},{6,14},{7,15},{8,16},{9,17... | collective-permute-start | bytes 1572872 | tf_op jit(solution)/shard_map/ppermute | solution.py:40
  40.8 6.4 %collective-permute-start.3 = (bf16[512,256]{1,0:T(8,128)(2,1)S(1)}, bf16[512,256]{1,0:T(8,128)(2,1)S(1)}, u32[]{:S(2)}, u32[]{:S(2)}) collective-permute-start(bf16[512,256]{1,0:T(8,128)(2,1)S(1)} %slice.61), channel_id=1, source_target_pairs={{0,24},{1,25},{2,26},{3,27},{4,28},{5,29},{6,30},{7,31},{8,0},{9,1... | collective-permute-start | bytes 786440 | tf_op jit(solution)/shard_map/ppermute | solution.py:40
  41.1 9.7 %collective-permute-start.2 = (bf16[512,256]{1,0:T(8,128)(2,1)S(1)}, bf16[512,256]{1,0:T(8,128)(2,1)}, u32[]{:S(2)}, u32[]{:S(2)}) collective-permute-start(bf16[512,256]{1,0:T(8,128)(2,1)S(1)} %slice.60), channel_id=1, source_target_pairs={{0,8},{1,9},{2,10},{3,11},{4,12},{5,13},{6,14},{7,15},{8,16},{9,17... | collective-permute-start | bytes 786440 | tf_op jit(solution)/shard_map/ppermute | solution.py:40
  42.4 11.7 %collective-permute-start.4 = (bf16[1024,256]{1,0:T(8,128)(2,1)S(1)}, bf16[1024,256]{1,0:T(8,128)(2,1)S(1)}, u32[]{:S(2)}, u32[]{:S(2)}) collective-permute-start(bf16[1024,256]{1,0:T(8,128)(2,1)S(1)} %bitcast.29), channel_id=1, source_target_pairs={{0,32},{32,0},{64,96},{96,64},{128,160},{160,128},{192,224},{224,1... | collective-permute-start | bytes 1572872 | tf_op jit(solution)/shard_map/ppermute | solution.py:44
  46.6 7.5 %collective-permute-start.5 = (bf16[1024,256]{1,0:T(8,128)(2,1)S(1)}, bf16[1024,256]{1,0:T(8,128)(2,1)S(1)}, u32[]{:S(2)}, u32[]{:S(2)}) collective-permute-start(bf16[1024,256]{1,0:T(8,128)(2,1)S(1)} %collective-permute-done.refs_1_), channel_id=1, source_target_pairs={{0,32},{32,0},{64,96},{96,64},{128,160},{160,128},{192,224},{224,1... | collective-permute-start | bytes 1572872 | tf_op jit(solution)/shard_map/ppermute | solution.py:44
  46.6 7.5 %collective-permute-start.6 = (bf16[1024,256]{1,0:T(8,128)(2,1)S(1)}, bf16[1024,256]{1,0:T(8,128)(2,1)S(1)}, u32[]{:S(2)}, u32[]{:S(2)}) collective-permute-start(bf16[1024,256]{1,0:T(8,128)(2,1)S(1)} %collective-permute-done.1.refs_2_), channel_id=1, source_target_pairs={{0,32},{32,0},{64,96},{96,64},{128,160},{160,128},{192,224},{224,1... | collective-permute-start | bytes 1572872 | tf_op jit(solution)/shard_map/ppermute | solution.py:44
  47.1 5.5 %collective-permute-start.8 = (bf16[512,256]{1,0:T(8,128)(2,1)S(1)}, bf16[512,256]{1,0:T(8,128)(2,1)}, u32[]{:S(2)}, u32[]{:S(2)}) collective-permute-start(bf16[512,256]{1,0:T(8,128)(2,1)S(1)} %collective-permute-done.3.refs_4_), channel_id=1, source_target_pairs={{0,32},{32,0},{64,96},{96,64},{128,160},{160,128},{192,224},{224,1... | collective-permute-start | bytes 786440 | tf_op jit(solution)/shard_map/ppermute | solution.py:44
  60.0 4.8 %collective-permute-start.12 = (bf16[2,256,128]{2,1,0:T(8,128)(2,1)S(1)}, bf16[2,256,128]{2,1,0:T(8,128)(2,1)S(1)}, u32[]{:S(2)}, u32[]{:S(2)}) collective-permute-start(bf16[2,256,128]{2,1,0:T(8,128)(2,1)S(1)} %get-tuple-element.62.refs_0_), channel_id=1, source_target_pairs={{0,24},{1,25},{2,26},{3,27},{4,28},{5,29},{6,30},{7,31},{8,0},{9,1... | collective-permute-start | bytes 393224 | tf_op jit(solution)/shard_map/ppermute | solution.py:40
  60.1 5.9 %collective-permute-start.11 = (bf16[2,256,128]{2,1,0:T(8,128)(2,1)S(1)}, bf16[2,256,128]{2,1,0:T(8,128)(2,1)S(1)}, u32[]{:S(2)}, u32[]{:S(2)}) collective-permute-start(bf16[2,256,128]{2,1,0:T(8,128)(2,1)S(1)} %get-tuple-element.62.refs_0_), channel_id=1, source_target_pairs={{0,8},{1,9},{2,10},{3,11},{4,12},{5,13},{6,14},{7,15},{8,16},{9,17... | collective-permute-start | bytes 393224 | tf_op jit(solution)/shard_map/ppermute | solution.py:40
  61.6 4.5 %collective-permute-start.10 = (bf16[2,256,128]{2,1,0:T(8,128)(2,1)S(1)}, bf16[2,256,128]{2,1,0:T(8,128)(2,1)S(1)}, u32[]{:S(2)}, u32[]{:S(2)}) collective-permute-start(bf16[2,256,128]{2,1,0:T(8,128)(2,1)S(1)} %get-tuple-element.63.refs_5_), channel_id=1, source_target_pairs={{0,7},{1,0},{2,1},{3,2},{4,3},{5,4},{6,5},{7,6},{8,15},{9,8},{10,9... | collective-permute-start | bytes 393224 | tf_op jit(solution)/shard_map/ppermute | solution.py:40
  61.6 5.3 %collective-permute-start.9 = (bf16[2,256,128]{2,1,0:T(8,128)(2,1)S(1)}, bf16[2,256,128]{2,1,0:T(8,128)(2,1)S(1)}, u32[]{:S(2)}, u32[]{:S(2)}) collective-permute-start(bf16[2,256,128]{2,1,0:T(8,128)(2,1)S(1)} %get-tuple-element.63.refs_5_), channel_id=1, source_target_pairs={{0,1},{1,2},{2,3},{3,4},{4,5},{5,6},{6,7},{7,0},{8,9},{9,10},{10,1... | collective-permute-start | bytes 393224 | tf_op jit(solution)/shard_map/ppermute | solution.py:40
  66.9 8.6 %collective-permute-start.13 = (bf16[2,256,128]{2,1,0:T(8,128)(2,1)S(1)}, bf16[2,256,128]{2,1,0:T(8,128)(2,1)S(1)}, u32[]{:S(2)}, u32[]{:S(2)}) collective-permute-start(bf16[2,256,128]{2,1,0:T(8,128)(2,1)S(1)} %collective-permute-done.9.refs_6_), channel_id=1, source_target_pairs={{0,1},{1,2},{2,3},{3,4},{4,5},{5,6},{6,7},{7,0},{8,9},{9,10},{10,1... | collective-permute-start | bytes 393224 | tf_op jit(solution)/shard_map/ppermute | solution.py:40
  66.9 8.6 %collective-permute-start.14 = (bf16[2,256,128]{2,1,0:T(8,128)(2,1)S(1)}, bf16[2,256,128]{2,1,0:T(8,128)(2,1)S(1)}, u32[]{:S(2)}, u32[]{:S(2)}) collective-permute-start(bf16[2,256,128]{2,1,0:T(8,128)(2,1)S(1)} %collective-permute-done.10.refs_7_), channel_id=1, source_target_pairs={{0,7},{1,0},{2,1},{3,2},{4,3},{5,4},{6,5},{7,6},{8,15},{9,8},{10,9... | collective-permute-start | bytes 393224 | tf_op jit(solution)/shard_map/ppermute | solution.py:40
  69.6 3.5 %collective-permute-start.16 = (bf16[1,256,128]{2,1,0:T(8,128)(2,1)S(1)}, bf16[1,256,128]{2,1,0:T(8,128)(2,1)S(1)}, u32[]{:S(2)}, u32[]{:S(2)}) collective-permute-start(bf16[1,256,128]{2,1,0:T(8,128)(2,1)S(1)} %slice.63), channel_id=1, source_target_pairs={{0,24},{1,25},{2,26},{3,27},{4,28},{5,29},{6,30},{7,31},{8,0},{9,1... | collective-permute-start | bytes 196616 | tf_op jit(solution)/shard_map/ppermute | solution.py:40
  71.1 4.3 %collective-permute-start.15 = (bf16[1,256,128]{2,1,0:T(8,128)(2,1)S(1)}, bf16[1,256,128]{2,1,0:T(8,128)(2,1)S(1)}, u32[]{:S(2)}, u32[]{:S(2)}) collective-permute-start(bf16[1,256,128]{2,1,0:T(8,128)(2,1)S(1)} %slice.62), channel_id=1, source_target_pairs={{0,8},{1,9},{2,10},{3,11},{4,12},{5,13},{6,14},{7,15},{8,16},{9,17... | collective-permute-start | bytes 196616 | tf_op jit(solution)/shard_map/ppermute | solution.py:40
  76.9 12.9 %collective-permute-start.18 = (bf16[10,256,128]{2,1,0:T(8,128)(2,1)}, bf16[10,256,128]{2,1,0:T(8,128)(2,1)S(1)}, u32[]{:S(2)}, u32[]{:S(2)}) collective-permute-start(bf16[10,256,128]{2,1,0:T(8,128)(2,1)} %get-tuple-element.73), channel_id=1, source_target_pairs={{0,7},{1,0},{2,1},{3,2},{4,3},{5,4},{6,5},{7,6},{8,15},{9,8},{10,9... | collective-permute-start | bytes 1966088 | tf_op jit(solution)/shard_map/ppermute | solution.py:40
  76.9 14.1 %collective-permute-start.17 = (bf16[10,256,128]{2,1,0:T(8,128)(2,1)}, bf16[10,256,128]{2,1,0:T(8,128)(2,1)S(1)}, u32[]{:S(2)}, u32[]{:S(2)}) collective-permute-start(bf16[10,256,128]{2,1,0:T(8,128)(2,1)} %get-tuple-element.72.refs_0_), channel_id=1, source_target_pairs={{0,1},{1,2},{2,3},{3,4},{4,5},{5,6},{6,7},{7,0},{8,9},{9,10},{10,1... | collective-permute-start | bytes 1966088 | tf_op jit(solution)/shard_map/ppermute | solution.py:40
  78.4 12.7 %collective-permute-start.20 = (bf16[10,256,128]{2,1,0:T(8,128)(2,1)}, bf16[10,256,128]{2,1,0:T(8,128)(2,1)S(1)}, u32[]{:S(2)}, u32[]{:S(2)}) collective-permute-start(bf16[10,256,128]{2,1,0:T(8,128)(2,1)} %get-tuple-element.74.refs_1_), channel_id=1, source_target_pairs={{0,24},{1,25},{2,26},{3,27},{4,28},{5,29},{6,30},{7,31},{8,0},{9,1... | collective-permute-start | bytes 1966088 | tf_op jit(solution)/shard_map/ppermute | solution.py:40
  78.7 13.9 %collective-permute-start.19 = (bf16[10,256,128]{2,1,0:T(8,128)(2,1)}, bf16[10,256,128]{2,1,0:T(8,128)(2,1)}, u32[]{:S(2)}, u32[]{:S(2)}) collective-permute-start(bf16[10,256,128]{2,1,0:T(8,128)(2,1)} %get-tuple-element.74.refs_1_), channel_id=1, source_target_pairs={{0,8},{1,9},{2,10},{3,11},{4,12},{5,13},{6,14},{7,15},{8,16},{9,17... | collective-permute-start | bytes 1966088 | tf_op jit(solution)/shard_map/ppermute | solution.py:40
  93.8 11.3 %collective-permute-start.21 = (bf16[9,256,128]{2,1,0:T(8,128)(2,1)S(1)}, bf16[9,256,128]{2,1,0:T(8,128)(2,1)S(1)}, u32[]{:S(2)}, u32[]{:S(2)}) collective-permute-start(bf16[9,256,128]{2,1,0:T(8,128)(2,1)S(1)} %get-tuple-element.83), channel_id=1, source_target_pairs={{0,1},{1,2},{2,3},{3,4},{4,5},{5,6},{6,7},{7,0},{8,9},{9,10},{10,1... | collective-permute-start | bytes 1769480 | tf_op jit(solution)/shard_map/ppermute | solution.py:40
  94.2 11.0 %collective-permute-start.22 = (bf16[9,256,128]{2,1,0:T(8,128)(2,1)S(1)}, bf16[9,256,128]{2,1,0:T(8,128)(2,1)S(1)}, u32[]{:S(2)}, u32[]{:S(2)}) collective-permute-start(bf16[9,256,128]{2,1,0:T(8,128)(2,1)S(1)} %get-tuple-element.84), channel_id=1, source_target_pairs={{0,7},{1,0},{2,1},{3,2},{4,3},{5,4},{6,5},{7,6},{8,15},{9,8},{10,9... | collective-permute-start | bytes 1769480 | tf_op jit(solution)/shard_map/ppermute | solution.py:40
  96.6 10.7 %collective-permute-start.23 = (bf16[9,256,128]{2,1,0:T(8,128)(2,1)S(1)}, bf16[9,256,128]{2,1,0:T(8,128)(2,1)S(1)}, u32[]{:S(2)}, u32[]{:S(2)}) collective-permute-start(bf16[9,256,128]{2,1,0:T(8,128)(2,1)S(1)} %get-tuple-element.85), channel_id=1, source_target_pairs={{0,8},{1,9},{2,10},{3,11},{4,12},{5,13},{6,14},{7,15},{8,16},{9,17... | collective-permute-start | bytes 1769480 | tf_op jit(solution)/shard_map/ppermute | solution.py:40
  96.6 10.7 %collective-permute-start.24 = (bf16[9,256,128]{2,1,0:T(8,128)(2,1)S(1)}, bf16[9,256,128]{2,1,0:T(8,128)(2,1)S(1)}, u32[]{:S(2)}, u32[]{:S(2)}) collective-permute-start(bf16[9,256,128]{2,1,0:T(8,128)(2,1)S(1)} %get-tuple-element.86), channel_id=1, source_target_pairs={{0,24},{1,25},{2,26},{3,27},{4,28},{5,29},{6,30},{7,31},{8,0},{9,1... | collective-permute-start | bytes 1769480 | tf_op jit(solution)/shard_map/ppermute | solution.py:40
  107.5 11.3 %collective-permute-start.25 = (bf16[8,256,128]{2,1,0:T(8,128)(2,1)S(1)}, bf16[8,256,128]{2,1,0:T(8,128)(2,1)S(1)}, u32[]{:S(2)}, u32[]{:S(2)}) collective-permute-start(bf16[8,256,128]{2,1,0:T(8,128)(2,1)S(1)} %slice.64), channel_id=1, source_target_pairs={{0,1},{1,2},{2,3},{3,4},{4,5},{5,6},{6,7},{7,0},{8,9},{9,10},{10,1... | collective-permute-start | bytes 1572872 | tf_op jit(solution)/shard_map/ppermute | solution.py:40
  107.5 11.3 %collective-permute-start.26 = (bf16[8,256,128]{2,1,0:T(8,128)(2,1)S(1)}, bf16[8,256,128]{2,1,0:T(8,128)(2,1)S(1)}, u32[]{:S(2)}, u32[]{:S(2)}) collective-permute-start(bf16[8,256,128]{2,1,0:T(8,128)(2,1)S(1)} %slice.65), channel_id=1, source_target_pairs={{0,7},{1,0},{2,1},{3,2},{4,3},{5,4},{6,5},{7,6},{8,15},{9,8},{10,9... | collective-permute-start | bytes 1572872 | tf_op jit(solution)/shard_map/ppermute | solution.py:40
  110.2 5.5 %collective-permute-start.29 = (bf16[2,256,128]{2,1,0:T(8,128)(2,1)S(1)}, bf16[2,256,128]{2,1,0:T(8,128)(2,1)S(1)}, u32[]{:S(2)}, u32[]{:S(2)}) collective-permute-start(bf16[2,256,128]{2,1,0:T(8,128)(2,1)S(1)} %pad_maximum_fusion.3), channel_id=1, source_target_pairs={{0,16},{1,17},{2,18},{3,19},{4,20},{5,21},{6,22},{7,23},{8,24},{9,... | collective-permute-start | bytes 393224 | tf_op jit(solution)/shard_map/ppermute | solution.py:40
  111.5 7.3 %collective-permute-start.27 = (bf16[4,256,128]{2,1,0:T(8,128)(2,1)S(1)}, bf16[4,256,128]{2,1,0:T(8,128)(2,1)S(1)}, u32[]{:S(2)}, u32[]{:S(2)}) collective-permute-start(bf16[4,256,128]{2,1,0:T(8,128)(2,1)S(1)} %get-tuple-element.94), channel_id=1, source_target_pairs={{0,8},{1,9},{2,10},{3,11},{4,12},{5,13},{6,14},{7,15},{8,16},{9,17... | collective-permute-start | bytes 786440 | tf_op jit(solution)/shard_map/ppermute | solution.py:40
  113.3 5.5 %collective-permute-start.28 = (bf16[4,256,128]{2,1,0:T(8,128)(2,1)S(1)}, bf16[4,256,128]{2,1,0:T(8,128)(2,1)S(1)}, u32[]{:S(2)}, u32[]{:S(2)}) collective-permute-start(bf16[4,256,128]{2,1,0:T(8,128)(2,1)S(1)} %get-tuple-element.95), channel_id=1, source_target_pairs={{0,24},{1,25},{2,26},{3,27},{4,28},{5,29},{6,30},{7,31},{8,0},{9,1... | collective-permute-start | bytes 786440 | tf_op jit(solution)/shard_map/ppermute | solution.py:40
  118.9 7.5 %collective-permute-start.30 = (bf16[4,256,128]{2,1,0:T(8,128)(2,1)S(1)}, bf16[4,256,128]{2,1,0:T(8,128)(2,1)S(1)}, u32[]{:S(2)}, u32[]{:S(2)}) collective-permute-start(bf16[4,256,128]{2,1,0:T(8,128)(2,1)S(1)} %slice.70), channel_id=1, source_target_pairs={{0,1},{1,2},{2,3},{3,4},{4,5},{5,6},{6,7},{7,0},{8,9},{9,10},{10,1... | collective-permute-start | bytes 786440 | tf_op jit(solution)/shard_map/ppermute | solution.py:40
  119.0 7.4 %collective-permute-start.31 = (bf16[4,256,128]{2,1,0:T(8,128)(2,1)S(1)}, bf16[4,256,128]{2,1,0:T(8,128)(2,1)S(1)}, u32[]{:S(2)}, u32[]{:S(2)}) collective-permute-start(bf16[4,256,128]{2,1,0:T(8,128)(2,1)S(1)} %slice.71), channel_id=1, source_target_pairs={{0,7},{1,0},{2,1},{3,2},{4,3},{5,4},{6,5},{7,6},{8,15},{9,8},{10,9... | collective-permute-start | bytes 786440 | tf_op jit(solution)/shard_map/ppermute | solution.py:40
  127.3 10.0 %collective-permute-start.32 = (f32[4,2,32,256]{3,2,1,0:T(8,128)S(1)}, f32[4,2,32,256]{3,2,1,0:T(8,128)S(1)}, u32[]{:S(2)}, u32[]{:S(2)}) collective-permute-start(f32[4,2,32,256]{3,2,1,0:T(8,128)S(1)} %get-tuple-element.109), channel_id=1, source_target_pairs={{0,32},{32,0},{64,96},{96,64},{128,160},{160,128},{192,224},{224,1... | collective-permute-start | bytes 786440 | tf_op jit(solution)/shard_map/ppermute | solution.py:44
  (27 other events, 438.1 us)

commit v5 on v4

--- a/solution.py
+++ b/solution.py
@@ -85,7 +85,7 @@
         out_shape=[jax.ShapeDtypeStruct((size, R, SEG), jnp.bfloat16) for size in sizes],
         in_specs=[vmem] * len(sources),
         out_specs=[vmem] * len(layout),
-        compiler_params=pltpu.CompilerParams(vmem_limit_bytes=20 << 20),
+        compiler_params=pltpu.CompilerParams(vmem_limit_bytes=10 << 20),
     )(*[p.array for p in sources])
     return [
         Piece(array, [s for source, at, n in packed for s in sources[source].segments[at : at + n]])
@@ -235,7 +235,7 @@
         in_specs=[pl.BlockSpec(memory_space=pltpu.SMEM)]
         + [vmem] * (2 + len(pieces) + len(starts)),
         out_specs=[vmem] * 2 if last else vmem,
-        compiler_params=pltpu.CompilerParams(vmem_limit_bytes=20 << 20),
+        compiler_params=pltpu.CompilerParams(vmem_limit_bytes=10 << 20),
         cost_estimate=pl.CostEstimate(
             flops=2 * rows * R * 256, bytes_accessed=rows * 1024, transcendentals=0
         ),

time: 163 us -> 163 us (level)
  transfers between devices with their start and end apart: 33 -> 33, of which waited for: 17 -> 18; matrix products, arithmetic and copies ran while one was open for 0% -> 0% of each run, Pallas kernels for 4% -> 4%
where the time goes in v5:
time: 163 us; the launch traced here: 162 us
  starting transfers between devices  48.1 us (30%)
  blocking collectives  45.3 us (28%)
  waiting for transfers between devices  40.9 us (25%)
  Pallas kernels  20 us (12%)
  local copies, waits for them, and re-layouts  4.83 us (3%)
  other arithmetic  2.02 us (1%)
    ppermute x27, waiting for transfers between devices, shift(): return lax.ppermute(a, 'mp', perm)  38.3 us
    all_to_all x2, blocking collectives, gather_direct(): got = lax.all_to_all(many, axis, 0, 0, axis_index_groups=groups, tiled=True)  35.5 us
    ppermute x27, starting transfers between devices, shift(): return lax.ppermute(a, 'mp', perm)  29.1 us
    ppermute x6, starting transfers between devices, other_core(): return lax.ppermute(a, 'dp', [(d, d ^ 1) for d in range(2 * NY)])  19 us
    all_to_all x1, blocking collectives, body(): lax.all_to_all(keep + other_core(give), 'dp', 0, 0, axis_index_groups=GRO...  9.79 us
    pallas_call x2, Pallas kernels, with_bases(): pl.pallas_call(functools.partial(kernel, [first for _, _, first in own],...  9.51 us
    pallas_call x5, Pallas kernels, low_of(): pl.pallas_call(functools.partial(low_kernel, len(pieces), runs, bool(star...  7.8 us
    unnamed x52, local copies, waits for them, and re-layouts  4.5 us
  transfers between devices with their start and end apart: 33, of which 18 were waited for; matrix products, arithmetic and copies ran while one was open for 0% of the time, Pallas kernels for 4%

profile of v5, /device:TPU:1, one launch (start us, length us, event | category | flops | bytes accessed | tf_op | source)
XLA Modules:
  0.0 162.4 jit_solution(6703333384133326063)
XLA Ops:
  1.6 24.8 %all_to_all.15 = bf16[8,128,256]{2,1,0:T(8,128)(2,1)S(1)} all-to-all(bf16[8,128,256]{2,1,0:T(8,128)(2,1)S(1)} %broadcast_in_dim.4), channel_id=1, replica_groups={{0,1,2,3,4,5,6,7},{8,9,10,11,12,13,14,15},{16,17,18,19,20,21,22,23},{24..., dimensions={0} | all-to-all | bytes 1048576 | tf_op jit(solution)/shard_map/all_to_all | solution.py:50
  26.4 2.5 %collective-permute-start.1 = (bf16[1024,256]{1,0:T(8,128)(2,1)S(1)}, bf16[1024,256]{1,0:T(8,128)(2,1)S(1)}, u32[]{:S(2)}, u32[]{:S(2)}) collective-permute-start(bf16[1024,256]{1,0:T(8,128)(2,1)S(1)} %bitcast.27), channel_id=1, source_target_pairs={{0,24},{1,25},{2,26},{3,27},{4,28},{5,29},{6,30},{7,31},{8,0},{9,1... | collective-permute-start | bytes 1572872 | tf_op jit(solution)/shard_map/ppermute | solution.py:40
  28.8 8.8 %collective-permute-done.1.refs_2_ = bf16[1024,256]{1,0:T(8,128)(2,1)S(1)} collective-permute-done((bf16[1024,256]{1,0:T(8,128)(2,1)S(1)}, bf16[1024,256]{1,0:T(8,128)(2,1)S(1)}, u32[]{:S(2)}, u32[]{:S(2)}) %collective-permute-start.1) | collective-permute-done | bytes 524320 | tf_op jit(solution)/shard_map/ppermute | solution.py:40
  37.6 3.1 %collective-permute-done.refs_1_ = bf16[1024,256]{1,0:T(8,128)(2,1)S(1)} collective-permute-done((bf16[1024,256]{1,0:T(8,128)(2,1)S(1)}, bf16[1024,256]{1,0:T(8,128)(2,1)S(1)}, u32[]{:S(2)}, u32[]{:S(2)}) %collective-permute-start) | collective-permute-done | bytes 524320 | tf_op jit(solution)/shard_map/ppermute | solution.py:40
  42.4 4.2 %collective-permute-start.4 = (bf16[1024,256]{1,0:T(8,128)(2,1)S(1)}, bf16[1024,256]{1,0:T(8,128)(2,1)S(1)}, u32[]{:S(2)}, u32[]{:S(2)}) collective-permute-start(bf16[1024,256]{1,0:T(8,128)(2,1)S(1)} %bitcast.29), channel_id=1, source_target_pairs={{0,32},{32,0},{64,96},{96,64},{128,160},{160,128},{192,224},{224,1... | collective-permute-start | bytes 1572872 | tf_op jit(solution)/shard_map/ppermute | solution.py:44
  47.1 3.7 %collective-permute-start.8 = (bf16[512,256]{1,0:T(8,128)(2,1)S(1)}, bf16[512,256]{1,0:T(8,128)(2,1)}, u32[]{:S(2)}, u32[]{:S(2)}) collective-permute-start(bf16[512,256]{1,0:T(8,128)(2,1)S(1)} %collective-permute-done.3.refs_4_), channel_id=1, source_target_pairs={{0,32},{32,0},{64,96},{96,64},{128,160},{160,128},{192,224},{224,1... | collective-permute-start | bytes 786440 | tf_op jit(solution)/shard_map/ppermute | solution.py:44
  50.9 1.7 %collective-permute-start.7 = (bf16[512,256]{1,0:T(8,128)(2,1)}, bf16[512,256]{1,0:T(8,128)(2,1)}, u32[]{:S(2)}, u32[]{:S(2)}) collective-permute-start(bf16[512,256]{1,0:T(8,128)(2,1)} %collective-permute-done.2.refs_3_), channel_id=1, source_target_pairs={{0,32},{32,0},{64,96},{96,64},{128,160},{160,128},{192,224},{224,1... | collective-permute-start | bytes 786440 | tf_op jit(solution)/shard_map/ppermute | solution.py:44
  54.1 5.9 %shard_map.235 = (bf16[2,256,128]{2,1,0:T(8,128)(2,1)S(1)}, bf16[2,256,128]{2,1,0:T(8,128)(2,1)S(1)}) custom-call(s32[6]{0:T(128)S(1)} %stack.33.table, bf16[256,4096]{1,0:T(8,128)(2,1)} %acts_in.1, bf16[256,4096]{1,0:T(8,128)(2,1)} %grad_out.1, bf16[1024,256]{1,0:T(8,128)(2,1)S(1)} %bitcast.30, bf16[1024,256]{1,0:T(8,128)(2,1)S(1)} %collective-permute-done.refs_1_, ...), custom_call_target="tpu_custom_call" | custom-call | flops 1073741824 | bytes 8388608 | tf_op jit(solution)/shard_map/pallas_call | solution.py:328
  63.0 1.8 %collective-permute-done.12.refs_2_ = bf16[2,256,128]{2,1,0:T(8,128)(2,1)S(1)} collective-permute-done((bf16[2,256,128]{2,1,0:T(8,128)(2,1)S(1)}, bf16[2,256,128]{2,1,0:T(8,128)(2,1)S(1)}, u32[]{:S(2)}, u32[]{:S(2)}) %collective-permute-start.12) | collective-permute-done | bytes 131104 | tf_op jit(solution)/shard_map/ppermute | solution.py:40
  66.9 2.7 %collective-permute-start.14 = (bf16[2,256,128]{2,1,0:T(8,128)(2,1)S(1)}, bf16[2,256,128]{2,1,0:T(8,128)(2,1)S(1)}, u32[]{:S(2)}, u32[]{:S(2)}) collective-permute-start(bf16[2,256,128]{2,1,0:T(8,128)(2,1)S(1)} %collective-permute-done.10.refs_7_), channel_id=1, source_target_pairs={{0,7},{1,0},{2,1},{3,2},{4,3},{5,4},{6,5},{7,6},{8,15},{9,8},{10,9... | collective-permute-start | bytes 393224 | tf_op jit(solution)/shard_map/ppermute | solution.py:40
  69.6 1.6 collective-permute-start.16
  71.1 1.9 %collective-permute-done.16.refs_4_ = bf16[1,256,128]{2,1,0:T(8,128)(2,1)S(1)} collective-permute-done((bf16[1,256,128]{2,1,0:T(8,128)(2,1)S(1)}, bf16[1,256,128]{2,1,0:T(8,128)(2,1)S(1)}, u32[]{:S(2)}, u32[]{:S(2)}) %collective-permute-start.16) | collective-permute-done | bytes 65568 | tf_op jit(solution)/shard_map/ppermute | solution.py:40
  73.1 2.4 %collective-permute-done.15.refs_3_ = bf16[1,256,128]{2,1,0:T(8,128)(2,1)S(1)} collective-permute-done((bf16[1,256,128]{2,1,0:T(8,128)(2,1)S(1)}, bf16[1,256,128]{2,1,0:T(8,128)(2,1)S(1)}, u32[]{:S(2)}, u32[]{:S(2)}) %collective-permute-start.15) | collective-permute-done | bytes 65568 | tf_op jit(solution)/shard_map/ppermute | solution.py:40
  79.9 2.2 %copy-done = bf16[8192,256]{1,0:T(8,128)(2,1)S(1)} copy-done((bf16[8192,256]{1,0:T(8,128)(2,1)S(1)}, bf16[8192,256]{1,0:T(8,128)(2,1)}, u32[]{:S(2)}) %copy-start) | copy-done | bytes 4194328
  82.1 2.2 %copy-done.2 = bf16[8192,256]{1,0:T(8,128)(2,1)S(1)} copy-done((bf16[8192,256]{1,0:T(8,128)(2,1)S(1)}, bf16[8192,256]{1,0:T(8,128)(2,1)}, u32[]{:S(2)}) %copy-start.2) | copy-done | bytes 4194328
  84.3 2.0 %shard_map.237.refs_4_ = f32[8,2,32,256]{3,2,1,0:T(8,128)S(1)} custom-call(s32[11]{0:T(128)S(1)} %pad_add_fusion.1.table, bf16[8192,256]{1,0:T(8,128)(2,1)S(1)} %copy-done, bf16[8192,256]{1,0:T(8,128)(2,1)S(1)} %copy-done.2, bf16[10,256,128]{2,1,0:T(8,128)(2,1)} %get-tuple-element.72.refs_0_, bf16[10,256,128]{2,1,0:T(8,128)(2,1)} %get-tuple-element.74.refs_1_), custom_call_target="tpu_custom_call" | custom-call | flops 301989888 | bytes 2359296 | tf_op jit(solution)/shard_map/pallas_call | solution.py:230
  86.3 3.5 %collective-permute-done.18.refs_1_ = bf16[10,256,128]{2,1,0:T(8,128)(2,1)S(1)} collective-permute-done((bf16[10,256,128]{2,1,0:T(8,128)(2,1)}, bf16[10,256,128]{2,1,0:T(8,128)(2,1)S(1)}, u32[]{:S(2)}, u32[]{:S(2)}) %collective-permute-start.18) | collective-permute-done | bytes 655392 | tf_op jit(solution)/shard_map/ppermute | solution.py:40
  91.1 1.5 collective-permute-done.19.refs_2_
  94.2 2.4 %collective-permute-start.22 = (bf16[9,256,128]{2,1,0:T(8,128)(2,1)S(1)}, bf16[9,256,128]{2,1,0:T(8,128)(2,1)S(1)}, u32[]{:S(2)}, u32[]{:S(2)}) collective-permute-start(bf16[9,256,128]{2,1,0:T(8,128)(2,1)S(1)} %get-tuple-element.84), channel_id=1, source_target_pairs={{0,7},{1,0},{2,1},{3,2},{4,3},{5,4},{6,5},{7,6},{8,15},{9,8},{10,9... | collective-permute-start | bytes 1769480 | tf_op jit(solution)/shard_map/ppermute | solution.py:40
  96.6 2.7 %collective-permute-start.24 = (bf16[9,256,128]{2,1,0:T(8,128)(2,1)S(1)}, bf16[9,256,128]{2,1,0:T(8,128)(2,1)S(1)}, u32[]{:S(2)}, u32[]{:S(2)}) collective-permute-start(bf16[9,256,128]{2,1,0:T(8,128)(2,1)S(1)} %get-tuple-element.86), channel_id=1, source_target_pairs={{0,24},{1,25},{2,26},{3,27},{4,28},{5,29},{6,30},{7,31},{8,0},{9,1... | collective-permute-start | bytes 1769480 | tf_op jit(solution)/shard_map/ppermute | solution.py:40
  99.4 2.2 %shard_map.239.refs_4_ = f32[8,2,32,256]{3,2,1,0:T(8,128)S(1)} custom-call(s32[23]{0:T(128)S(1)} %get-tuple-element.123.table, bf16[8192,256]{1,0:T(8,128)(2,1)S(1)} %copy-done.1, bf16[8192,256]{1,0:T(8,128)(2,1)S(1)} %copy-done.2, bf16[10,256,128]{2,1,0:T(8,128)(2,1)S(1)} %collective-permute-done.17.refs_0_, ...), custom_call_target="tpu_custom_call" | custom-call | flops 671088640 | bytes 5242880 | tf_op jit(solution)/shard_map/pallas_call | solution.py:230
  101.6 3.5 %collective-permute-done.21.refs_0_ = bf16[9,256,128]{2,1,0:T(8,128)(2,1)S(1)} collective-permute-done((bf16[9,256,128]{2,1,0:T(8,128)(2,1)S(1)}, bf16[9,256,128]{2,1,0:T(8,128)(2,1)S(1)}, u32[]{:S(2)}, u32[]{:S(2)}) %collective-permute-start.21) | collective-permute-done | bytes 589856 | tf_op jit(solution)/shard_map/ppermute | solution.py:40
  105.1 2.1 %collective-permute-done.23.refs_2_ = bf16[9,256,128]{2,1,0:T(8,128)(2,1)S(1)} collective-permute-done((bf16[9,256,128]{2,1,0:T(8,128)(2,1)S(1)}, bf16[9,256,128]{2,1,0:T(8,128)(2,1)S(1)}, u32[]{:S(2)}, u32[]{:S(2)}) %collective-permute-start.23) | collective-permute-done | bytes 589856 | tf_op jit(solution)/shard_map/ppermute | solution.py:40
  107.5 2.7 %collective-permute-start.26 = (bf16[8,256,128]{2,1,0:T(8,128)(2,1)S(1)}, bf16[8,256,128]{2,1,0:T(8,128)(2,1)S(1)}, u32[]{:S(2)}, u32[]{:S(2)}) collective-permute-start(bf16[8,256,128]{2,1,0:T(8,128)(2,1)S(1)} %slice.65), channel_id=1, source_target_pairs={{0,7},{1,0},{2,1},{3,2},{4,3},{5,4},{6,5},{7,6},{8,15},{9,8},{10,9... | collective-permute-start | bytes 1572872 | tf_op jit(solution)/shard_map/ppermute | solution.py:40
  111.5 1.8 %collective-permute-start.27 = (bf16[4,256,128]{2,1,0:T(8,128)(2,1)S(1)}, bf16[4,256,128]{2,1,0:T(8,128)(2,1)S(1)}, u32[]{:S(2)}, u32[]{:S(2)}) collective-permute-start(bf16[4,256,128]{2,1,0:T(8,128)(2,1)S(1)} %get-tuple-element.94), channel_id=1, source_target_pairs={{0,8},{1,9},{2,10},{3,11},{4,12},{5,13},{6,14},{7,15},{8,16},{9,17... | collective-permute-start | bytes 786440 | tf_op jit(solution)/shard_map/ppermute | solution.py:40
  115.7 3.0 %collective-permute-done.27.refs_2_ = bf16[4,256,128]{2,1,0:T(8,128)(2,1)S(1)} collective-permute-done((bf16[4,256,128]{2,1,0:T(8,128)(2,1)S(1)}, bf16[4,256,128]{2,1,0:T(8,128)(2,1)S(1)}, u32[]{:S(2)}, u32[]{:S(2)}) %collective-permute-start.27) | collective-permute-done | bytes 262176 | tf_op jit(solution)/shard_map/ppermute | solution.py:40
  119.0 2.7 %collective-permute-start.31 = (bf16[4,256,128]{2,1,0:T(8,128)(2,1)S(1)}, bf16[4,256,128]{2,1,0:T(8,128)(2,1)S(1)}, u32[]{:S(2)}, u32[]{:S(2)}) collective-permute-start(bf16[4,256,128]{2,1,0:T(8,128)(2,1)S(1)} %slice.71), channel_id=1, source_target_pairs={{0,7},{1,0},{2,1},{3,2},{4,3},{5,4},{6,5},{7,6},{8,15},{9,8},{10,9... | collective-permute-start | bytes 786440 | tf_op jit(solution)/shard_map/ppermute | solution.py:40
  123.1 3.2 %collective-permute-done.30.refs_0_ = bf16[4,256,128]{2,1,0:T(8,128)(2,1)S(1)} collective-permute-done((bf16[4,256,128]{2,1,0:T(8,128)(2,1)S(1)}, bf16[4,256,128]{2,1,0:T(8,128)(2,1)S(1)}, u32[]{:S(2)}, u32[]{:S(2)}) %collective-permute-start.30) | collective-permute-done | bytes 262176 | tf_op jit(solution)/shard_map/ppermute | solution.py:40
  127.3 8.8 %collective-permute-start.32 = (f32[4,2,32,256]{3,2,1,0:T(8,128)S(1)}, f32[4,2,32,256]{3,2,1,0:T(8,128)S(1)}, u32[]{:S(2)}, u32[]{:S(2)}) collective-permute-start(f32[4,2,32,256]{3,2,1,0:T(8,128)S(1)} %get-tuple-element.109), channel_id=1, source_target_pairs={{0,32},{32,0},{64,96},{96,64},{128,160},{160,128},{192,224},{224,1... | collective-permute-start | bytes 786440 | tf_op jit(solution)/shard_map/ppermute | solution.py:44
  137.3 9.8 %all_to_all.16 = f32[4,2,32,256]{3,2,1,0:T(8,128)S(1)} all-to-all(f32[4,2,32,256]{3,2,1,0:T(8,128)S(1)} %add.208), channel_id=1, replica_groups={{0,64,128,192},{32,96,160,224},{1,65,129,193},{33,97,161,225},{2,66,130..., dimensions={0} | all-to-all | bytes 524288 | tf_op jit(solution)/shard_map/all_to_all | solution.py:402
  147.9 10.7 %all_to_all.17 = bf16[8,1,2,32,256]{4,3,2,1,0:T(8,128)(2,1)S(1)} all-to-all(bf16[8,1,2,32,256]{4,3,2,1,0:T(8,128)(2,1)S(1)} %broadcast_in_dim.5), channel_id=1, replica_groups=mesh['dp'=8,'mp'=32] {'dp'}, dimensions={0} | all-to-all | bytes 524288 | tf_op jit(solution)/shard_map/all_to_all | solution.py:50
  158.6 3.6 %shard_map.243 = (bf16[4096,256]{1,0:T(8,128)(2,1)}, bf16[256,4096]{1,0:T(8,128)(2,1)}) custom-call(s32[6]{0:T(128)S(1)} %stack.33.table, bf16[8,2,32,256]{3,2,1,0:T(8,128)(2,1)S(1)} %bitcast.32, bf16[1024,256]{1,0:T(8,128)(2,1)S(1)} %bitcast.31, bf16[1024,256]{1,0:T(8,128)(2,1)S(1)} %collective-permute-done.refs_1_, ...), custom_call_target="tpu_custom_call" | custom-call | flops 1073741824 | bytes 8388608 | tf_op jit(solution)/shard_map/pallas_call | solution.py:328
  (129 shorter events, 25.6 us)
Async XLA Ops:
  26.4 11.2 %collective-permute-start.1 = (bf16[1024,256]{1,0:T(8,128)(2,1)S(1)}, bf16[1024,256]{1,0:T(8,128)(2,1)S(1)}, u32[]{:S(2)}, u32[]{:S(2)}) collective-permute-start(bf16[1024,256]{1,0:T(8,128)(2,1)S(1)} %bitcast.27), channel_id=1, source_target_pairs={{0,24},{1,25},{2,26},{3,27},{4,28},{5,29},{6,30},{7,31},{8,0},{9,1... | collective-permute-start | bytes 1572872 | tf_op jit(solution)/shard_map/ppermute | solution.py:40
  28.8 11.9 %collective-permute-start = (bf16[1024,256]{1,0:T(8,128)(2,1)S(1)}, bf16[1024,256]{1,0:T(8,128)(2,1)S(1)}, u32[]{:S(2)}, u32[]{:S(2)}) collective-permute-start(bf16[1024,256]{1,0:T(8,128)(2,1)S(1)} %bitcast.28), channel_id=1, source_target_pairs={{0,8},{1,9},{2,10},{3,11},{4,12},{5,13},{6,14},{7,15},{8,16},{9,17... | collective-permute-start | bytes 1572872 | tf_op jit(solution)/shard_map/ppermute | solution.py:40
  40.8 6.4 %collective-permute-start.3 = (bf16[512,256]{1,0:T(8,128)(2,1)S(1)}, bf16[512,256]{1,0:T(8,128)(2,1)S(1)}, u32[]{:S(2)}, u32[]{:S(2)}) collective-permute-start(bf16[512,256]{1,0:T(8,128)(2,1)S(1)} %slice.61), channel_id=1, source_target_pairs={{0,24},{1,25},{2,26},{3,27},{4,28},{5,29},{6,30},{7,31},{8,0},{9,1... | collective-permute-start | bytes 786440 | tf_op jit(solution)/shard_map/ppermute | solution.py:40
  41.1 9.7 %collective-permute-start.2 = (bf16[512,256]{1,0:T(8,128)(2,1)S(1)}, bf16[512,256]{1,0:T(8,128)(2,1)}, u32[]{:S(2)}, u32[]{:S(2)}) collective-permute-start(bf16[512,256]{1,0:T(8,128)(2,1)S(1)} %slice.60), channel_id=1, source_target_pairs={{0,8},{1,9},{2,10},{3,11},{4,12},{5,13},{6,14},{7,15},{8,16},{9,17... | collective-permute-start | bytes 786440 | tf_op jit(solution)/shard_map/ppermute | solution.py:40
  42.4 11.7 %collective-permute-start.4 = (bf16[1024,256]{1,0:T(8,128)(2,1)S(1)}, bf16[1024,256]{1,0:T(8,128)(2,1)S(1)}, u32[]{:S(2)}, u32[]{:S(2)}) collective-permute-start(bf16[1024,256]{1,0:T(8,128)(2,1)S(1)} %bitcast.29), channel_id=1, source_target_pairs={{0,32},{32,0},{64,96},{96,64},{128,160},{160,128},{192,224},{224,1... | collective-permute-start | bytes 1572872 | tf_op jit(solution)/shard_map/ppermute | solution.py:44
  46.6 7.5 %collective-permute-start.5 = (bf16[1024,256]{1,0:T(8,128)(2,1)S(1)}, bf16[1024,256]{1,0:T(8,128)(2,1)S(1)}, u32[]{:S(2)}, u32[]{:S(2)}) collective-permute-start(bf16[1024,256]{1,0:T(8,128)(2,1)S(1)} %collective-permute-done.refs_1_), channel_id=1, source_target_pairs={{0,32},{32,0},{64,96},{96,64},{128,160},{160,128},{192,224},{224,1... | collective-permute-start | bytes 1572872 | tf_op jit(solution)/shard_map/ppermute | solution.py:44
  46.6 7.5 %collective-permute-start.6 = (bf16[1024,256]{1,0:T(8,128)(2,1)S(1)}, bf16[1024,256]{1,0:T(8,128)(2,1)S(1)}, u32[]{:S(2)}, u32[]{:S(2)}) collective-permute-start(bf16[1024,256]{1,0:T(8,128)(2,1)S(1)} %collective-permute-done.1.refs_2_), channel_id=1, source_target_pairs={{0,32},{32,0},{64,96},{96,64},{128,160},{160,128},{192,224},{224,1... | collective-permute-start | bytes 1572872 | tf_op jit(solution)/shard_map/ppermute | solution.py:44
  47.1 5.5 %collective-permute-start.8 = (bf16[512,256]{1,0:T(8,128)(2,1)S(1)}, bf16[512,256]{1,0:T(8,128)(2,1)}, u32[]{:S(2)}, u32[]{:S(2)}) collective-permute-start(bf16[512,256]{1,0:T(8,128)(2,1)S(1)} %collective-permute-done.3.refs_4_), channel_id=1, source_target_pairs={{0,32},{32,0},{64,96},{96,64},{128,160},{160,128},{192,224},{224,1... | collective-permute-start | bytes 786440 | tf_op jit(solution)/shard_map/ppermute | solution.py:44
  60.0 4.8 %collective-permute-start.12 = (bf16[2,256,128]{2,1,0:T(8,128)(2,1)S(1)}, bf16[2,256,128]{2,1,0:T(8,128)(2,1)S(1)}, u32[]{:S(2)}, u32[]{:S(2)}) collective-permute-start(bf16[2,256,128]{2,1,0:T(8,128)(2,1)S(1)} %get-tuple-element.62.refs_0_), channel_id=1, source_target_pairs={{0,24},{1,25},{2,26},{3,27},{4,28},{5,29},{6,30},{7,31},{8,0},{9,1... | collective-permute-start | bytes 393224 | tf_op jit(solution)/shard_map/ppermute | solution.py:40
  60.1 5.9 %collective-permute-start.11 = (bf16[2,256,128]{2,1,0:T(8,128)(2,1)S(1)}, bf16[2,256,128]{2,1,0:T(8,128)(2,1)S(1)}, u32[]{:S(2)}, u32[]{:S(2)}) collective-permute-start(bf16[2,256,128]{2,1,0:T(8,128)(2,1)S(1)} %get-tuple-element.62.refs_0_), channel_id=1, source_target_pairs={{0,8},{1,9},{2,10},{3,11},{4,12},{5,13},{6,14},{7,15},{8,16},{9,17... | collective-permute-start | bytes 393224 | tf_op jit(solution)/shard_map/ppermute | solution.py:40
  61.6 4.5 %collective-permute-start.10 = (bf16[2,256,128]{2,1,0:T(8,128)(2,1)S(1)}, bf16[2,256,128]{2,1,0:T(8,128)(2,1)S(1)}, u32[]{:S(2)}, u32[]{:S(2)}) collective-permute-start(bf16[2,256,128]{2,1,0:T(8,128)(2,1)S(1)} %get-tuple-element.63.refs_5_), channel_id=1, source_target_pairs={{0,7},{1,0},{2,1},{3,2},{4,3},{5,4},{6,5},{7,6},{8,15},{9,8},{10,9... | collective-permute-start | bytes 393224 | tf_op jit(solution)/shard_map/ppermute | solution.py:40
  61.6 5.3 %collective-permute-start.9 = (bf16[2,256,128]{2,1,0:T(8,128)(2,1)S(1)}, bf16[2,256,128]{2,1,0:T(8,128)(2,1)S(1)}, u32[]{:S(2)}, u32[]{:S(2)}) collective-permute-start(bf16[2,256,128]{2,1,0:T(8,128)(2,1)S(1)} %get-tuple-element.63.refs_5_), channel_id=1, source_target_pairs={{0,1},{1,2},{2,3},{3,4},{4,5},{5,6},{6,7},{7,0},{8,9},{9,10},{10,1... | collective-permute-start | bytes 393224 | tf_op jit(solution)/shard_map/ppermute | solution.py:40
  66.9 8.6 %collective-permute-start.13 = (bf16[2,256,128]{2,1,0:T(8,128)(2,1)S(1)}, bf16[2,256,128]{2,1,0:T(8,128)(2,1)S(1)}, u32[]{:S(2)}, u32[]{:S(2)}) collective-permute-start(bf16[2,256,128]{2,1,0:T(8,128)(2,1)S(1)} %collective-permute-done.9.refs_6_), channel_id=1, source_target_pairs={{0,1},{1,2},{2,3},{3,4},{4,5},{5,6},{6,7},{7,0},{8,9},{9,10},{10,1... | collective-permute-start | bytes 393224 | tf_op jit(solution)/shard_map/ppermute | solution.py:40
  66.9 8.6 %collective-permute-start.14 = (bf16[2,256,128]{2,1,0:T(8,128)(2,1)S(1)}, bf16[2,256,128]{2,1,0:T(8,128)(2,1)S(1)}, u32[]{:S(2)}, u32[]{:S(2)}) collective-permute-start(bf16[2,256,128]{2,1,0:T(8,128)(2,1)S(1)} %collective-permute-done.10.refs_7_), channel_id=1, source_target_pairs={{0,7},{1,0},{2,1},{3,2},{4,3},{5,4},{6,5},{7,6},{8,15},{9,8},{10,9... | collective-permute-start | bytes 393224 | tf_op jit(solution)/shard_map/ppermute | solution.py:40
  69.6 3.5 %collective-permute-start.16 = (bf16[1,256,128]{2,1,0:T(8,128)(2,1)S(1)}, bf16[1,256,128]{2,1,0:T(8,128)(2,1)S(1)}, u32[]{:S(2)}, u32[]{:S(2)}) collective-permute-start(bf16[1,256,128]{2,1,0:T(8,128)(2,1)S(1)} %slice.63), channel_id=1, source_target_pairs={{0,24},{1,25},{2,26},{3,27},{4,28},{5,29},{6,30},{7,31},{8,0},{9,1... | collective-permute-start | bytes 196616 | tf_op jit(solution)/shard_map/ppermute | solution.py:40
  71.1 4.3 %collective-permute-start.15 = (bf16[1,256,128]{2,1,0:T(8,128)(2,1)S(1)}, bf16[1,256,128]{2,1,0:T(8,128)(2,1)S(1)}, u32[]{:S(2)}, u32[]{:S(2)}) collective-permute-start(bf16[1,256,128]{2,1,0:T(8,128)(2,1)S(1)} %slice.62), channel_id=1, source_target_pairs={{0,8},{1,9},{2,10},{3,11},{4,12},{5,13},{6,14},{7,15},{8,16},{9,17... | collective-permute-start | bytes 196616 | tf_op jit(solution)/shard_map/ppermute | solution.py:40
  76.9 12.9 %collective-permute-start.18 = (bf16[10,256,128]{2,1,0:T(8,128)(2,1)}, bf16[10,256,128]{2,1,0:T(8,128)(2,1)S(1)}, u32[]{:S(2)}, u32[]{:S(2)}) collective-permute-start(bf16[10,256,128]{2,1,0:T(8,128)(2,1)} %get-tuple-element.73), channel_id=1, source_target_pairs={{0,7},{1,0},{2,1},{3,2},{4,3},{5,4},{6,5},{7,6},{8,15},{9,8},{10,9... | collective-permute-start | bytes 1966088 | tf_op jit(solution)/shard_map/ppermute | solution.py:40
  76.9 14.1 %collective-permute-start.17 = (bf16[10,256,128]{2,1,0:T(8,128)(2,1)}, bf16[10,256,128]{2,1,0:T(8,128)(2,1)S(1)}, u32[]{:S(2)}, u32[]{:S(2)}) collective-permute-start(bf16[10,256,128]{2,1,0:T(8,128)(2,1)} %get-tuple-element.72.refs_0_), channel_id=1, source_target_pairs={{0,1},{1,2},{2,3},{3,4},{4,5},{5,6},{6,7},{7,0},{8,9},{9,10},{10,1... | collective-permute-start | bytes 1966088 | tf_op jit(solution)/shard_map/ppermute | solution.py:40
  78.4 12.7 %collective-permute-start.20 = (bf16[10,256,128]{2,1,0:T(8,128)(2,1)}, bf16[10,256,128]{2,1,0:T(8,128)(2,1)S(1)}, u32[]{:S(2)}, u32[]{:S(2)}) collective-permute-start(bf16[10,256,128]{2,1,0:T(8,128)(2,1)} %get-tuple-element.74.refs_1_), channel_id=1, source_target_pairs={{0,24},{1,25},{2,26},{3,27},{4,28},{5,29},{6,30},{7,31},{8,0},{9,1... | collective-permute-start | bytes 1966088 | tf_op jit(solution)/shard_map/ppermute | solution.py:40
  78.7 13.9 %collective-permute-start.19 = (bf16[10,256,128]{2,1,0:T(8,128)(2,1)}, bf16[10,256,128]{2,1,0:T(8,128)(2,1)}, u32[]{:S(2)}, u32[]{:S(2)}) collective-permute-start(bf16[10,256,128]{2,1,0:T(8,128)(2,1)} %get-tuple-element.74.refs_1_), channel_id=1, source_target_pairs={{0,8},{1,9},{2,10},{3,11},{4,12},{5,13},{6,14},{7,15},{8,16},{9,17... | collective-permute-start | bytes 1966088 | tf_op jit(solution)/shard_map/ppermute | solution.py:40
  93.8 11.3 %collective-permute-start.21 = (bf16[9,256,128]{2,1,0:T(8,128)(2,1)S(1)}, bf16[9,256,128]{2,1,0:T(8,128)(2,1)S(1)}, u32[]{:S(2)}, u32[]{:S(2)}) collective-permute-start(bf16[9,256,128]{2,1,0:T(8,128)(2,1)S(1)} %get-tuple-element.83), channel_id=1, source_target_pairs={{0,1},{1,2},{2,3},{3,4},{4,5},{5,6},{6,7},{7,0},{8,9},{9,10},{10,1... | collective-permute-start | bytes 1769480 | tf_op jit(solution)/shard_map/ppermute | solution.py:40
  94.2 11.0 %collective-permute-start.22 = (bf16[9,256,128]{2,1,0:T(8,128)(2,1)S(1)}, bf16[9,256,128]{2,1,0:T(8,128)(2,1)S(1)}, u32[]{:S(2)}, u32[]{:S(2)}) collective-permute-start(bf16[9,256,128]{2,1,0:T(8,128)(2,1)S(1)} %get-tuple-element.84), channel_id=1, source_target_pairs={{0,7},{1,0},{2,1},{3,2},{4,3},{5,4},{6,5},{7,6},{8,15},{9,8},{10,9... | collective-permute-start | bytes 1769480 | tf_op jit(solution)/shard_map/ppermute | solution.py:40
  96.6 10.7 %collective-permute-start.23 = (bf16[9,256,128]{2,1,0:T(8,128)(2,1)S(1)}, bf16[9,256,128]{2,1,0:T(8,128)(2,1)S(1)}, u32[]{:S(2)}, u32[]{:S(2)}) collective-permute-start(bf16[9,256,128]{2,1,0:T(8,128)(2,1)S(1)} %get-tuple-element.85), channel_id=1, source_target_pairs={{0,8},{1,9},{2,10},{3,11},{4,12},{5,13},{6,14},{7,15},{8,16},{9,17... | collective-permute-start | bytes 1769480 | tf_op jit(solution)/shard_map/ppermute | solution.py:40
  96.6 10.7 %collective-permute-start.24 = (bf16[9,256,128]{2,1,0:T(8,128)(2,1)S(1)}, bf16[9,256,128]{2,1,0:T(8,128)(2,1)S(1)}, u32[]{:S(2)}, u32[]{:S(2)}) collective-permute-start(bf16[9,256,128]{2,1,0:T(8,128)(2,1)S(1)} %get-tuple-element.86), channel_id=1, source_target_pairs={{0,24},{1,25},{2,26},{3,27},{4,28},{5,29},{6,30},{7,31},{8,0},{9,1... | collective-permute-start | bytes 1769480 | tf_op jit(solution)/shard_map/ppermute | solution.py:40
  107.5 11.3 %collective-permute-start.25 = (bf16[8,256,128]{2,1,0:T(8,128)(2,1)S(1)}, bf16[8,256,128]{2,1,0:T(8,128)(2,1)S(1)}, u32[]{:S(2)}, u32[]{:S(2)}) collective-permute-start(bf16[8,256,128]{2,1,0:T(8,128)(2,1)S(1)} %slice.64), channel_id=1, source_target_pairs={{0,1},{1,2},{2,3},{3,4},{4,5},{5,6},{6,7},{7,0},{8,9},{9,10},{10,1... | collective-permute-start | bytes 1572872 | tf_op jit(solution)/shard_map/ppermute | solution.py:40
  107.5 11.3 %collective-permute-start.26 = (bf16[8,256,128]{2,1,0:T(8,128)(2,1)S(1)}, bf16[8,256,128]{2,1,0:T(8,128)(2,1)S(1)}, u32[]{:S(2)}, u32[]{:S(2)}) collective-permute-start(bf16[8,256,128]{2,1,0:T(8,128)(2,1)S(1)} %slice.65), channel_id=1, source_target_pairs={{0,7},{1,0},{2,1},{3,2},{4,3},{5,4},{6,5},{7,6},{8,15},{9,8},{10,9... | collective-permute-start | bytes 1572872 | tf_op jit(solution)/shard_map/ppermute | solution.py:40
  110.2 5.5 %collective-permute-start.29 = (bf16[2,256,128]{2,1,0:T(8,128)(2,1)S(1)}, bf16[2,256,128]{2,1,0:T(8,128)(2,1)S(1)}, u32[]{:S(2)}, u32[]{:S(2)}) collective-permute-start(bf16[2,256,128]{2,1,0:T(8,128)(2,1)S(1)} %pad_maximum_fusion.3), channel_id=1, source_target_pairs={{0,16},{1,17},{2,18},{3,19},{4,20},{5,21},{6,22},{7,23},{8,24},{9,... | collective-permute-start | bytes 393224 | tf_op jit(solution)/shard_map/ppermute | solution.py:40
  111.5 7.3 %collective-permute-start.27 = (bf16[4,256,128]{2,1,0:T(8,128)(2,1)S(1)}, bf16[4,256,128]{2,1,0:T(8,128)(2,1)S(1)}, u32[]{:S(2)}, u32[]{:S(2)}) collective-permute-start(bf16[4,256,128]{2,1,0:T(8,128)(2,1)S(1)} %get-tuple-element.94), channel_id=1, source_target_pairs={{0,8},{1,9},{2,10},{3,11},{4,12},{5,13},{6,14},{7,15},{8,16},{9,17... | collective-permute-start | bytes 786440 | tf_op jit(solution)/shard_map/ppermute | solution.py:40
  113.3 5.5 %collective-permute-start.28 = (bf16[4,256,128]{2,1,0:T(8,128)(2,1)S(1)}, bf16[4,256,128]{2,1,0:T(8,128)(2,1)S(1)}, u32[]{:S(2)}, u32[]{:S(2)}) collective-permute-start(bf16[4,256,128]{2,1,0:T(8,128)(2,1)S(1)} %get-tuple-element.95), channel_id=1, source_target_pairs={{0,24},{1,25},{2,26},{3,27},{4,28},{5,29},{6,30},{7,31},{8,0},{9,1... | collective-permute-start | bytes 786440 | tf_op jit(solution)/shard_map/ppermute | solution.py:40
  118.9 7.5 %collective-permute-start.30 = (bf16[4,256,128]{2,1,0:T(8,128)(2,1)S(1)}, bf16[4,256,128]{2,1,0:T(8,128)(2,1)S(1)}, u32[]{:S(2)}, u32[]{:S(2)}) collective-permute-start(bf16[4,256,128]{2,1,0:T(8,128)(2,1)S(1)} %slice.70), channel_id=1, source_target_pairs={{0,1},{1,2},{2,3},{3,4},{4,5},{5,6},{6,7},{7,0},{8,9},{9,10},{10,1... | collective-permute-start | bytes 786440 | tf_op jit(solution)/shard_map/ppermute | solution.py:40
  119.0 7.4 %collective-permute-start.31 = (bf16[4,256,128]{2,1,0:T(8,128)(2,1)S(1)}, bf16[4,256,128]{2,1,0:T(8,128)(2,1)S(1)}, u32[]{:S(2)}, u32[]{:S(2)}) collective-permute-start(bf16[4,256,128]{2,1,0:T(8,128)(2,1)S(1)} %slice.71), channel_id=1, source_target_pairs={{0,7},{1,0},{2,1},{3,2},{4,3},{5,4},{6,5},{7,6},{8,15},{9,8},{10,9... | collective-permute-start | bytes 786440 | tf_op jit(solution)/shard_map/ppermute | solution.py:40
  127.3 10.0 %collective-permute-start.32 = (f32[4,2,32,256]{3,2,1,0:T(8,128)S(1)}, f32[4,2,32,256]{3,2,1,0:T(8,128)S(1)}, u32[]{:S(2)}, u32[]{:S(2)}) collective-permute-start(f32[4,2,32,256]{3,2,1,0:T(8,128)S(1)} %get-tuple-element.109), channel_id=1, source_target_pairs={{0,32},{32,0},{64,96},{96,64},{128,160},{160,128},{192,224},{224,1... | collective-permute-start | bytes 786440 | tf_op jit(solution)/shard_map/ppermute | solution.py:44
  (27 other events, 438.1 us)
